TPU v7x, 32 devices: a whole 2x2x4 slice. The times are simulated.
32 devices in a mesh: shard: 4 (over z), rep: 8 (over y, x, core).
Axes of the slice: x: 2, y: 2, z: 4, core: 2. Of those that a mesh axis runs over, the one named last changes fastest.
Arguments:
- pooled_grad: bfloat16 [8192, 256], P(('shard', 'rep')), may hold values from -6 to 6
- send_sample: int32 [128, 128], P(('shard', 'rep')), may hold values from 0 to 255
- send_row: int32 [128, 128], P(('shard', 'rep')), may hold values from 0 to 2047
- send_count: int32 [128], P(('shard', 'rep')), may hold values from 1 to 128, as said below
- union_blocks: int32 [4, 16], P('shard'), may hold values from 0 to 31, as said below
- table: float32 [16384, 256], P('shard'), may hold values from -6 to 6
- accum: float32 [16384], P('shard'), may hold values from 0.05 to 2
Outputs:
- new_table: float32 [16384, 256], P('shard')
- new_accum: float32 [16384], P('shard')
Inputs may be any that keep to these rules, and one draw needn't show every extreme that they name: `send_count`: in every replica group one owner gets 128 live entries from every device of the group. `union_blocks`: each shard's row blocks are distinct and increasing, and include its first and its last block.
All inputs are finite; a program needn't handle non-finite values.
Results may differ from a plain program's by a relative error of at most 0.00065.
Values may be sent and summed in bfloat16 or wider, within the bound.
No kernel may reach another device: no remote copies, remote signals or barrier semaphores. Data moves between devices by JAX's collectives and lax.ppermute only.
A program may use at most 64 MiB of HBM per device.

v0:
```python
import jax
import jax.numpy as jnp
from jax import lax
from jax.sharding import PartitionSpec as P

TILE = 128


LEARNING_RATE = 0.5
EPSILON = 1e-06


def row_adagrad(picked, acc_picked, gradient):
    acc_new = acc_picked + jnp.mean(gradient * gradient, axis=-1)
    rows_new = picked - LEARNING_RATE * gradient / (jnp.sqrt(acc_new)[:, None] + EPSILON)
    return (rows_new, acc_new)


def on_device(pooled_grad, send_sample, send_row, send_count, union_blocks, table, accum):
    columns = pooled_grad.shape[1]
    samples = pooled_grad.shape[0]
    active = (lax.broadcasted_iota(jnp.int32, send_sample.shape, 1) < send_count[:, None]).astype(
        jnp.float32
    )
    lengths = jax.ops.segment_sum(active.reshape(-1), send_sample.reshape(-1), num_segments=samples)
    scaled = active / jnp.maximum(lengths, 1.0)[send_sample]
    values = (pooled_grad[send_sample].astype(jnp.float32) * scaled[:, :, None]).astype(
        jnp.bfloat16
    )
    arrived, positions = (
        lax.all_to_all(values, "shard", split_axis=0, concat_axis=0, tiled=True),
        lax.all_to_all(send_row, "shard", split_axis=0, concat_axis=0, tiled=True),
    )
    blocks = union_blocks[0]
    union_span = blocks.shape[0] * TILE
    local_grad = (
        jnp.zeros((union_span, columns), jnp.float32)
        .at[positions.reshape(-1)]
        .add(arrived.reshape(-1, columns).astype(jnp.float32))
    )
    table_tiles = table.reshape(-1, TILE, columns)
    accum_tiles = accum.reshape(-1, TILE)
    picked = table_tiles[blocks].reshape(union_span, columns)
    acc_picked = accum_tiles[blocks].reshape(union_span)
    summed = lax.psum(local_grad.astype(jnp.bfloat16), "rep")
    rounded = lax.optimization_barrier(summed)
    rows_new, acc_new = row_adagrad(picked, acc_picked, rounded.astype(jnp.float32))
    table_out = table_tiles.at[blocks].set(rows_new.reshape(-1, TILE, columns)).reshape(table.shape)
    accum_out = accum_tiles.at[blocks].set(acc_new.reshape(-1, TILE)).reshape(accum.shape)
    return (table_out, accum_out)


def solution(mesh):
    in_specs = (
        P(("shard", "rep"), None),
        P(("shard", "rep"), None),
        P(("shard", "rep"), None),
        P(("shard", "rep")),
        P("shard", None),
        P("shard", None),
        P("shard"),
    )
    out_specs = (P("shard", None), P("shard"))
    return jax.shard_map(
        on_device, mesh=mesh, in_specs=in_specs, out_specs=out_specs, check_vma=False
    )
```

profile of v0, /device:TPU:0, one launch (start us, length us, event | category | flops | bytes accessed | tf_op | source)
XLA Modules:
  0.0 118.6 jit_solution(11932237321276147209)
XLA Ops:
  7.2 0.0 copy-start
  7.2 0.8 copy.15
  7.9 4.5 %copy.14 = f32[4096,256]{1,0:T(8,128)} copy(f32[4096,256]{1,0:T(8,128)} %param.12) | data formatting | bytes 8388608
  12.4 6.3 %all-to-all-start = ((s32[4,1,128]{2,1,0:T(1,128)}), s32[4,1,128]{2,1,0:T(1,128)S(1)}, u32[]{:S(2)}, u32[]{:S(2)}) async-start(s32[4,1,128]{2,1,0:T(1,128)} %bitcast.4), calls=%async_computation | async-start | bytes 4096 | tf_op jit(solution)/shard_map/all_to_all | solution.py:32
  18.8 0.1 convert_bitcast_fusion
  18.9 4.1 %scatter_custom_fusion = f32[256]{0:T(256)S(1)} fusion(s32[512]{0:T(512)S(1)} %bitcast.46, f32[512]{0:T(512)S(1)} %convert_bitcast_fusion, f32[]{:T(128)} %constant.11.clone.1), kind=kCustom, calls=%fused_computation.36 | custom fusion | flops 512 | bytes 1028 | tf_op jit(solution)/shard_map/scatter-add | solution.py:25
  23.0 3.5 %gather_fusion.2 = f32[512]{0:T(512)S(1)} fusion(f32[256]{0:T(256)S(1)} %broadcast_maximum_fusion, s32[1024]{0:T(1024)S(1)} %pad_clamp_fusion), kind=kCustom, calls=%fused_computation.2 | custom fusion | bytes 6144 | tf_op jit(solution)/shard_map/gather | solution.py:26
  26.5 0.1 convert_divide_fusion
  26.5 2.0 %gather_fusion.1 = bf16[512,256]{1,0:T(8,128)(2,1)S(1)} fusion(bf16[256,256]{1,0:T(8,128)(2,1)S(1)} %copy-done, s32[1024]{0:T(1024)S(1)} %pad_clamp_fusion), kind=kCustom, calls=%fused_computation.1 | custom fusion | bytes 526336 | tf_op jit(solution)/shard_map/gather | solution.py:27
  28.5 0.8 fusion.6
  29.3 5.1 %all-to-all-start.1 = ((bf16[4,128,256]{2,1,0:T(8,128)(2,1)}), bf16[4,128,256]{2,1,0:T(8,128)(2,1)S(1)}, u32[]{:S(2)}, u32[]{:S(2)}) async-start(bf16[4,128,256]{2,1,0:T(8,128)(2,1)} %fusion.6), calls=%async_computation.1 | async-start | bytes 524288 | tf_op jit(solution)/shard_map/all_to_all | solution.py:31
  34.4 8.3 %all-to-all-done.1 = bf16[4,128,256]{2,1,0:T(8,128)(2,1)S(1)} async-done(((bf16[4,128,256]{2,1,0:T(8,128)(2,1)}), bf16[4,128,256]{2,1,0:T(8,128)(2,1)S(1)}, u32[]{:S(2)}, u32[]{:S(2)}) %all-to-all-start.1) | async-done | bytes 262176 | tf_op jit(solution)/shard_map/all_to_all | solution.py:31
  42.7 3.8 %scatter_custom_fusion.1 = f32[2048,256]{1,0:T(8,128)S(1)} fusion(s32[512]{0:T(512)S(1)} %bitcast.47, f32[]{:T(128)} %constant.11.clone.1, bf16[512,256]{1,0:T(8,128)(2,1)S(1)} %bitcast.41), kind=kCustom, calls=%fused_computation.13 | custom fusion | flops 262144 | bytes 2359300 | tf_op jit(solution)/shard_map/scatter-add | solution.py:39
  46.6 0.0 copy-start.4
  46.6 1.1 convert_element_type.38
  47.7 0.0 all-reduce.2.cloned.1.call-update
  47.7 0.6 gather_fusion.3
  48.3 4.2 %gather_fusion = f32[16,128,256]{2,1,0:T(8,128)} fusion(f32[32,128,256]{2,1,0:T(8,128)} %bitcast.37, s32[1024]{0:T(1024)S(1)} %pad_clamp_fusion.1), kind=kCustom, calls=%fused_computation | custom fusion | bytes 4194368 | tf_op jit(solution)/shard_map/gather | solution.py:43
  52.5 51.0 %all-reduce.2.cloned.1.call-done = bf16[2048,256]{1,0:T(8,128)(2,1)} async-done(((bf16[2048,256]{1,0:T(8,128)(2,1)}), bf16[2048,256]{1,0:T(8,128)(2,1)}) %all-reduce.2.cloned.1.call-update) | async-done | bytes 1048592 | tf_op jit(solution)/shard_map/psum | solution.py:45
  103.6 1.6 %fusion.2 = f32[2048]{0:T(1024)S(1)} fusion(bf16[2048,256]{1,0:T(8,128)(2,1)} %all-reduce.2.cloned.1.call-done), kind=kLoop, calls=%fused_computation.12 | loop fusion | flops 1570816 | bytes 1056768 | tf_op jit(solution)/shard_map/reduce_sum | solution.py:14
  105.2 0.7 scatter_custom_fusion.3
  105.8 0.0 copy-start.1
  105.8 2.3 %fusion.1 = f32[2048,256]{1,0:T(8,128)S(1)} fusion(bf16[2048,256]{1,0:T(8,128)(2,1)} %all-reduce.2.cloned.1.call-done, f32[16,128,256]{2,1,0:T(8,128)} %gather_fusion, f32[2048]{0:T(1024)S(1)} %fusion.9), kind=kLoop, calls=%fused_computation.11 | loop fusion | flops 2097152 | bytes 5251072 | tf_op jit(solution)/shard_map/sub | solution.py:15
  108.1 3.7 %scatter_fusion = f32[32,128,256]{2,1,0:T(8,128)} fusion(f32[32,128,256]{2,1,0:T(8,128)} %bitcast.38, s32[16]{0:T(128)S(1)} %fusion.13, f32[16,128,256]{2,1,0:T(8,128)S(1)} %bitcast.40), kind=kCustom, calls=%fused_computation.6 | custom fusion | bytes 6291520 | tf_op jit(solution)/shard_map/scatter | solution.py:48
  (16 shorter events, 0.1 us)
Async XLA Ops:
  7.2 19.4 %copy-start = (bf16[256,256]{1,0:T(8,128)(2,1)S(1)}, bf16[256,256]{1,0:T(8,128)(2,1)}, u32[]{:S(2)}) copy-start(bf16[256,256]{1,0:T(8,128)(2,1)} %param.7) | copy-start | bytes 393220
  7.9 10.8 %copy-start.3 = (s32[4,128]{1,0:T(4,128)S(1)}, s32[4,128]{1,0:T(4,128)}, u32[]{:S(2)}) copy-start(s32[4,128]{1,0:T(4,128)} %param.8) | copy-start | bytes 6148
  7.9 10.8 %copy-start.2 = (s32[4]{0:T(128)S(1)}, s32[4]{0:T(128)}, u32[]{:S(2)}) copy-start(s32[4]{0:T(128)} %param.10) | copy-start | bytes 52
  12.4 16.9 %all-to-all-start = ((s32[4,1,128]{2,1,0:T(1,128)}), s32[4,1,128]{2,1,0:T(1,128)S(1)}, u32[]{:S(2)}, u32[]{:S(2)}) async-start(s32[4,1,128]{2,1,0:T(1,128)} %bitcast.4), calls=%async_computation | async-start | bytes 4096 | tf_op jit(solution)/shard_map/all_to_all | solution.py:32
  29.3 13.4 %all-to-all-start.1 = ((bf16[4,128,256]{2,1,0:T(8,128)(2,1)}), bf16[4,128,256]{2,1,0:T(8,128)(2,1)S(1)}, u32[]{:S(2)}, u32[]{:S(2)}) async-start(bf16[4,128,256]{2,1,0:T(8,128)(2,1)} %fusion.6), calls=%async_computation.1 | async-start | bytes 524288 | tf_op jit(solution)/shard_map/all_to_all | solution.py:31
  34.4 69.2 %all-reduce.2.cloned.1.call-start = ((), (), s32[]{:S(2)}) async-start(), calls=%async_computation.2 | async-start | bytes 2097152 | tf_op jit(solution)/shard_map/psum | solution.py:45
  46.6 1.1 copy-start.4
  105.8 2.3 %copy-start.1 = (f32[32,128]{1,0:T(8,128)}, f32[32,128]{1,0:T(8,128)S(1)}, u32[]{:S(2)}) copy-start(f32[32,128]{1,0:T(8,128)S(1)} %scatter_custom_fusion.3) | copy-start | bytes 49156
Sparse Core Ops, SparseCore 0:
  47.8 55.6 all-reduce.1
where the time goes:
time: 119 us
  waiting for transfers between devices  59.4 us (50%)
  local copies, waits for them, and re-layouts  19.2 us (16%)
  other arithmetic  14.5 us (12%)
  between operations  14.2 us (12%)
  starting transfers between devices  11.4 us (10%)
    psum x1, waiting for transfers between devices, on_device(): summed = lax.psum(local_grad.astype(jnp.bfloat16), 'rep')  51 us
    all_to_all x1, waiting for transfers between devices, on_device(): lax.all_to_all(values, 'shard', split_axis=0, concat_axis=0, tiled=True)  8.3 us
    all_to_all x1, starting transfers between devices, on_device(): lax.all_to_all(send_row, 'shard', split_axis=0, concat_axis=0, tiled=True)  6.32 us
    unnamed x12, local copies, waits for them, and re-layouts  5.28 us
    all_to_all x1, starting transfers between devices, on_device(): lax.all_to_all(values, 'shard', split_axis=0, concat_axis=0, tiled=True)  5.08 us
    gather x1, local copies, waits for them, and re-layouts, on_device(): picked = table_tiles[blocks].reshape(union_span, columns)  4.22 us
    scatter-add x1, other arithmetic, on_device(): jax.ops.segment_sum(active.reshape(-1), send_sample.reshape(-1), num_segm...  4.08 us
    scatter-add x1, other arithmetic, on_device(): local_grad = jnp.zeros((union_span, columns), jnp.float32).at[positions.r...  3.85 us
  transfers between devices with their start and end apart: 3, of which 2 were waited for; matrix products, arithmetic and copies ran while one was open for 13% of the time, Pallas kernels for 0%

commit v1 on v0

v1 whole, which is shorter than its diff:
```python
import functools

import jax
import jax.numpy as jnp
from jax import lax
from jax.experimental import pallas as pl
from jax.experimental.pallas import tpu as pltpu
from jax.sharding import PartitionSpec as P

TILE = 128
TAIL = 16
LEARNING_RATE = 0.5
EPSILON = 1e-06
VMEM = pltpu.VMEM
SMEM = pltpu.SMEM
F32 = jnp.float32
BF16 = jnp.bfloat16


def params(mib=40):
    return pltpu.CompilerParams(vmem_limit_bytes=mib * 2**20)


def whole(space=VMEM):
    return pl.BlockSpec(memory_space=space)


def pack_kernel(me_ref, count_ref, grad_ref, sample_ref, row_ref, *out_refs):
    owners, cap = sample_ref.shape
    samples, cols = grad_ref.shape
    lane = lax.broadcasted_iota(jnp.int32, (1, cap), 1)
    sub = lax.broadcasted_iota(jnp.int32, (samples, cap), 0)

    def picks(o):
        live = jnp.where(lane < count_ref[o], sample_ref[pl.ds(o, 1), :], -1)
        return (sub == live).astype(F32)

    total = picks(0)
    for o in range(1, owners):
        total = total + picks(o)
    lengths = jnp.sum(total, axis=1, keepdims=True)
    scaled = (grad_ref[...].astype(F32) * (1.0 / jnp.maximum(lengths, 1.0))).astype(BF16)
    tail_row = lax.broadcasted_iota(jnp.int32, (TAIL, cap), 0)
    for j in range(owners):
        o = me_ref[0] ^ j
        values = lax.dot_general(
            picks(o).astype(BF16), scaled, (((0,), (0,)), ((), ())), preferred_element_type=F32
        )
        out_refs[j][0:cap, :] = values.astype(BF16)
        row = row_ref[pl.ds(o, 1), :]
        slot = row // TILE
        within = row - slot * TILE
        tail = jnp.where(tail_row == 0, slot, jnp.where(tail_row == 1, within, 0))
        out_refs[j][cap : cap + TAIL, :] = jnp.zeros((TAIL, cols), BF16)
        out_refs[j][cap : cap + TAIL, 0:cap] = tail.astype(F32).astype(BF16)


def pack(me, count, grad, sample, row):
    owners, cap = sample.shape
    shape = jax.ShapeDtypeStruct((cap + TAIL, grad.shape[1]), BF16)
    return pl.pallas_call(
        pack_kernel,
        out_shape=[shape] * owners,
        in_specs=[whole(SMEM), whole(SMEM), whole(), whole(), whole()],
        out_specs=[whole()] * owners,
        compiler_params=params(),
    )(me, count, grad, sample, row)


def join_kernel(*refs):
    ins, out = refs[:-1], refs[-1]
    cap = ins[0].shape[0] - TAIL
    n = len(ins)
    for c, ref in enumerate(ins):
        out[c * cap : (c + 1) * cap, :] = ref[0:cap, :]
    sub = lax.broadcasted_iota(jnp.int32, (TAIL, ins[0].shape[1]), 0)
    tail = jnp.zeros((TAIL, ins[0].shape[1]), F32)
    for c, ref in enumerate(ins):
        own = ref[cap : cap + TAIL, :].astype(F32)
        tail = jnp.where(sub == 2 * c, own[0:1, :], jnp.where(sub == 2 * c + 1, own[1:2, :], tail))
    out[n * cap : n * cap + TAIL, :] = tail.astype(BF16)


def join(chunks):
    cap = chunks[0].shape[0] - TAIL
    cols = chunks[0].shape[1]
    return pl.pallas_call(
        join_kernel,
        out_shape=jax.ShapeDtypeStruct((len(chunks) * cap + TAIL, cols), BF16),
        in_specs=[whole()] * len(chunks),
        out_specs=whole(),
        compiler_params=params(),
    )(*chunks)


def positions(ref, cap):
    entries = ref.shape[0] - TAIL
    tail = ref[entries : entries + TAIL, 0:cap].astype(F32)
    n = entries // cap
    slot = jnp.concatenate([tail[2 * c : 2 * c + 1] for c in range(n)], axis=1)
    within = jnp.concatenate([tail[2 * c + 1 : 2 * c + 2] for c in range(n)], axis=1)
    return slot, within


def block_sum(ref, slot, within, k, cap):
    entries = ref.shape[0] - TAIL
    here = jnp.where(slot == k, within, -1.0).astype(BF16)
    sub = lax.broadcasted_iota(jnp.int32, (TILE, entries), 0).astype(F32).astype(BF16)
    pick = jnp.where(sub == here, jnp.ones((), BF16), jnp.zeros((), BF16))
    return jnp.dot(pick, ref[0:entries, :], preferred_element_type=F32)


def sum_kernel(cap, pairs, *refs):
    payloads, out = refs[: 2 * pairs], refs[2 * pairs]
    places = [positions(ref, cap) for ref in payloads]
    for k in range(out.shape[0] // TILE):
        parts = [block_sum(ref, *place, k, cap) for ref, place in zip(payloads, places)]
        halves = [parts[2 * i] + parts[2 * i + 1] for i in range(pairs)]
        total = halves[0] if pairs == 1 else halves[0] + halves[1]
        out[k * TILE : (k + 1) * TILE, :] = total


def sum_payloads(payloads, span, cap):
    cols = payloads[0].shape[1]
    entries = payloads[0].shape[0] - TAIL
    pairs = len(payloads) // 2
    return pl.pallas_call(
        functools.partial(sum_kernel, cap, pairs),
        out_shape=jax.ShapeDtypeStruct((span, cols), F32),
        in_specs=[whole()] * len(payloads),
        out_specs=whole(),
        compiler_params=params(),
        cost_estimate=pl.CostEstimate(
            flops=2 * span * entries * cols * len(payloads),
            bytes_accessed=span * cols * 4,
            transcendentals=0,
        ),
    )(*payloads)


def stage_kernel(blocks_ref, table_ref, copy_ref, picked_ref, sems):
    n = picked_ref.shape[0] // TILE
    full = pltpu.make_async_copy(table_ref, copy_ref, sems.at[n])
    full.start()
    copies = []
    for k in range(n):
        start = pl.multiple_of(blocks_ref[0, k] * TILE, TILE)
        c = pltpu.make_async_copy(
            table_ref.at[pl.ds(start, TILE), :],
            picked_ref.at[pl.ds(k * TILE, TILE), :],
            sems.at[k],
        )
        c.start()
        copies.append(c)
    for c in copies:
        c.wait()
    full.wait()


def stage(blocks, table):
    n = blocks.shape[1]
    return pl.pallas_call(
        stage_kernel,
        out_shape=[
            jax.ShapeDtypeStruct(table.shape, F32),
            jax.ShapeDtypeStruct((n * TILE, table.shape[1]), F32),
        ],
        in_specs=[whole(SMEM), whole(pl.ANY)],
        out_specs=[whole(pl.ANY), whole()],
        scratch_shapes=[pltpu.SemaphoreType.DMA((n + 1,))],
        compiler_params=params(),
        cost_estimate=pl.CostEstimate(
            flops=0, bytes_accessed=4 * table.size * 3, transcendentals=0
        ),
    )(blocks, table)


def update_kernel(
    cap, blocks_ref, last0, last1, side_ref, near_ref, picked_ref, accum_ref, table_in,
    table_ref, accum_out, rows_out, sems,
):
    del table_in
    n = picked_ref.shape[0] // TILE
    cols = picked_ref.shape[1]
    places = [positions(ref, cap) for ref in (last0, last1)]
    accum_out[...] = accum_ref[...]
    copies = []
    for k in range(n):
        span = slice(k * TILE, (k + 1) * TILE)
        far = block_sum(last0, *places[0], k, cap) + block_sum(last1, *places[1], k, cap)
        grad = (near_ref[span, :] + (side_ref[span, :] + far)).astype(BF16).astype(F32)
        block = blocks_ref[0, k]
        mean = jnp.sum(grad * grad, axis=1, keepdims=True) * (1.0 / cols)
        wide = jnp.broadcast_to(accum_ref[pl.ds(block, 1), :], (TILE, TILE)).T
        new = wide[:, 0:1] + mean
        rows_out[span, :] = picked_ref[span, :] - LEARNING_RATE * grad / (jnp.sqrt(new) + EPSILON)
        accum_out[pl.ds(block, 1), :] = jnp.broadcast_to(new, (TILE, TILE)).T[0:1, :]
        c = pltpu.make_async_copy(
            rows_out.at[span, :],
            table_ref.at[pl.ds(pl.multiple_of(block * TILE, TILE), TILE), :],
            sems.at[k],
        )
        c.start()
        copies.append(c)
    for c in copies:
        c.wait()


def update(blocks, last, side, near, picked, accum, table, cap):
    n = blocks.shape[1]
    return pl.pallas_call(
        functools.partial(update_kernel, cap),
        out_shape=[
            jax.ShapeDtypeStruct(table.shape, F32),
            jax.ShapeDtypeStruct(accum.shape, F32),
        ],
        in_specs=[whole(SMEM)] + [whole()] * 6 + [whole(pl.ANY)],
        out_specs=[whole(pl.ANY), whole()],
        scratch_shapes=[
            pltpu.VMEM(picked.shape, F32),
            pltpu.SemaphoreType.DMA((n,)),
        ],
        input_output_aliases={7: 0},
        compiler_params=params(),
    )(blocks, *last, side, near, picked, accum, table)


def gathered(pooled_grad, send_sample, send_row, send_count, union_blocks, table, accum):
    shards = lax.axis_size("shard")
    reps = lax.axis_size("rep")
    cap = send_sample.shape[1]
    span = union_blocks.shape[1] * TILE
    me = lax.axis_index("shard").astype(jnp.int32).reshape(1)
    axes = ("shard", "rep")

    def swap(x, flip):
        pairs = []
        for z in range(shards):
            for r in range(reps):
                dz, dr = flip(r)
                pairs.append((z * reps + r, (z ^ dz) * reps + (r ^ dr)))
        return lax.ppermute(x, axes, pairs)

    mine = pack(me, send_count, pooled_grad, send_sample, send_row)
    far = swap(mine[2], lambda r: (2, 0))
    up = swap(mine[3], lambda r: (3, 0))
    down = swap(mine[1], lambda r: (1, 0))
    own = join([mine[0], down, far, up])
    one = swap(own, lambda r: (0, 2 if r % 2 == 0 else 4))
    two = swap(own, lambda r: (0, 4 if r % 2 == 0 else 2))
    diag = swap(one, lambda r: (0, 4 if r % 2 == 0 else 2))
    core = lambda x: swap(x, lambda r: (0, 1))
    table_copy, picked = stage(union_blocks, table)
    own_c, one_c, two_c, diag_c = core(own), core(one), core(two), core(diag)
    even = lax.axis_index("rep") % 2 == 0
    x0 = lax.select(even, one, two)
    x1 = lax.select(even, two_c, one_c)
    y0 = lax.select(even, two, one)
    y1 = lax.select(even, one_c, two_c)
    near = sum_payloads([own, own_c, x0, x1], span, cap)
    side = sum_payloads([y0, y1], span, cap)
    table_out, accum_out = update(
        union_blocks, (diag, diag_c), side, near, picked, accum.reshape(-1, TILE), table_copy, cap
    )
    return table_out, accum_out.reshape(accum.shape)


def reduced(pooled_grad, send_sample, send_row, send_count, union_blocks, table, accum):
    columns = pooled_grad.shape[1]
    samples = pooled_grad.shape[0]
    active = (lax.broadcasted_iota(jnp.int32, send_sample.shape, 1) < send_count[:, None]).astype(F32)
    lengths = jax.ops.segment_sum(active.reshape(-1), send_sample.reshape(-1), num_segments=samples)
    scaled = active / jnp.maximum(lengths, 1.0)[send_sample]
    values = (pooled_grad[send_sample].astype(F32) * scaled[:, :, None]).astype(BF16)
    arrived = lax.all_to_all(values, "shard", split_axis=0, concat_axis=0, tiled=True)
    places = lax.all_to_all(send_row, "shard", split_axis=0, concat_axis=0, tiled=True)
    blocks = union_blocks[0]
    span = blocks.shape[0] * TILE
    local = (
        jnp.zeros((span, columns), F32)
        .at[places.reshape(-1)]
        .add(arrived.reshape(-1, columns).astype(F32))
    )
    table_tiles = table.reshape(-1, TILE, columns)
    accum_tiles = accum.reshape(-1, TILE)
    grad = lax.optimization_barrier(lax.psum(local.astype(BF16), "rep")).astype(F32)
    acc_new = accum_tiles[blocks].reshape(span) + jnp.mean(grad * grad, axis=-1)
    rows_new = table_tiles[blocks].reshape(span, columns) - LEARNING_RATE * grad / (
        jnp.sqrt(acc_new)[:, None] + EPSILON
    )
    table_out = table_tiles.at[blocks].set(rows_new.reshape(-1, TILE, columns)).reshape(table.shape)
    accum_out = accum_tiles.at[blocks].set(acc_new.reshape(-1, TILE)).reshape(accum.shape)
    return table_out, accum_out


def solution(mesh):
    both = ("shard", "rep")
    in_specs = (
        P(both, None),
        P(both, None),
        P(both, None),
        P(both),
        P("shard", None),
        P("shard", None),
        P("shard"),
    )
    out_specs = (P("shard", None), P("shard"))
    small = mesh.shape["shard"] == 4 and mesh.shape["rep"] == 8
    return jax.shard_map(
        gathered if small else reduced,
        mesh=mesh,
        in_specs=in_specs,
        out_specs=out_specs,
        check_vma=False,
    )
```

time: 119 us -> 42.3 us (0.36)
  waiting for transfers between devices: 59.4 us -> 12.6 us
  other arithmetic: 14.5 us -> 0.08 us
  between operations: 14.2 us -> 0.76 us
  local copies, waits for them, and re-layouts: 19.2 us -> 5.77 us
  Pallas kernels: 0 us -> 13 us
  starting transfers between devices: 11.4 us -> 9.9 us
    psum x1 -> x0, waiting for transfers between devices: 51 us -> none  [on_device(): summed = lax.psum(local_grad.astype(jnp.bfloat16), 'rep')]
    pallas_call x0 -> x6, Pallas kernels: none -> 13 us  [the longest x1 4.98 us: update(): pl.pallas_call(functools.partial(update_kernel, cap), out_shape=[jax.Shap...]
    ppermute x0 -> x10, waiting for transfers between devices: none -> 12.6 us  [swap(): return lax.ppermute(x, axes, pairs)]
    all_to_all x2 -> x0, starting transfers between devices: 11.4 us -> none  [the longest x1 6.32 us: on_device(): lax.all_to_all(send_row, 'shard', split_axis=0, concat_axis=0, tiled=True)]
    gather x4 -> x0, local copies, waits for them, and re-layouts: 10.2 us -> none  [the longest x1 4.22 us: on_device(): picked = table_tiles[blocks].reshape(union_span, columns)]
    ppermute x0 -> x10, starting transfers between devices: none -> 9.9 us  [swap(): return lax.ppermute(x, axes, pairs)]
    all_to_all x2 -> x0, waiting for transfers between devices: 8.31 us -> none  [the longest x1 8.3 us: on_device(): lax.all_to_all(values, 'shard', split_axis=0, concat_axis=0, tiled=True)]
    scatter-add x2 -> x0, other arithmetic: 7.93 us -> none  [the longest x1 4.08 us: on_device(): jax.ops.segment_sum(active.reshape(-1), send_sample.reshape(-1), num_segm...]
  transfers between devices with their start and end apart: 3 -> 10, of which waited for: 2 -> 3; matrix products, arithmetic and copies ran while one was open for 13% -> 0% of each run, Pallas kernels for 0% -> 17%
where the time goes in v1:
time: 42.3 us; the launch traced here: 42 us
  Pallas kernels  13 us (31%)
  waiting for transfers between devices  12.6 us (30%)
  starting transfers between devices  9.9 us (23%)
  local copies, waits for them, and re-layouts  5.77 us (14%)
  between operations  0.76 us (2%)
    ppermute x10, waiting for transfers between devices, swap(): return lax.ppermute(x, axes, pairs)  12.6 us
    ppermute x10, starting transfers between devices, swap(): return lax.ppermute(x, axes, pairs)  9.9 us
    unnamed x16, local copies, waits for them, and re-layouts  5.77 us
    pallas_call x1, Pallas kernels, update(): pl.pallas_call(functools.partial(update_kernel, cap), out_shape=[jax.Shap...  4.98 us
    pallas_call x2, Pallas kernels, sum_payloads(): pl.pallas_call(functools.partial(sum_kernel, cap, pairs), out_shape=jax.S...  3.59 us
    pallas_call x1, Pallas kernels, stage(): pl.pallas_call(stage_kernel, out_shape=[jax.ShapeDtypeStruct(table.shape,...  3.49 us
    pallas_call x1, Pallas kernels, pack(): pl.pallas_call(pack_kernel, out_shape=[shape] * owners, in_specs=[whole(S...  0.9 us
  transfers between devices with their start and end apart: 10, of which 3 were waited for; matrix products, arithmetic and copies ran while one was open for 0% of the time, Pallas kernels for 17%

profile of v1, /device:TPU:0, one launch (start us, length us, event | category | flops | bytes accessed | tf_op | source)
XLA Modules:
  0.0 42.0 jit_solution(14120798021139259318)
XLA Ops:
  0.6 0.9 %copy-done.1 = bf16[256,256]{1,0:T(8,128)(2,1)S(1)} copy-done((bf16[256,256]{1,0:T(8,128)(2,1)S(1)}, bf16[256,256]{1,0:T(8,128)(2,1)}, u32[]{:S(2)}) %copy-start.1) | copy-done | bytes 131096
  1.5 0.7 %copy-done.3 = s32[4,128]{1,0:T(4,128)S(1)} copy-done((s32[4,128]{1,0:T(4,128)S(1)}, s32[4,128]{1,0:T(4,128)}, u32[]{:S(2)}) %copy-start.3) | copy-done | bytes 2072
  2.2 0.7 %copy-done.4 = s32[4,128]{1,0:T(4,128)S(1)} copy-done((s32[4,128]{1,0:T(4,128)S(1)}, s32[4,128]{1,0:T(4,128)}, u32[]{:S(2)}) %copy-start.4) | copy-done | bytes 2072
  2.9 0.7 %copy-done.7 = s32[4]{0:T(128)S(1)} copy-done((s32[4]{0:T(128)S(1)}, s32[4]{0:T(128)}, u32[]{:S(2)}) %copy-start.7) | copy-done | bytes 40
  3.6 0.9 %shard_map.86 = (bf16[144,256]{1,0:T(8,128)(2,1)S(1)}, bf16[144,256]{1,0:T(8,128)(2,1)S(1)}, bf16[144,256]{1,0:T(8,128)(2,1)S(1)}, bf16[144,256]{1,0:T(8,128)(2,1)S(1)}) custom-call(s32[1]{0:T(128)} %bitcast.me_ref, s32[4]{0:T(128)S(1)} %copy-done.7, bf16[256,256]{1,0:T(8,128)(2,1)S(1)} %copy-done.1, s32[4,128]{1,0:T(4,128)S(1)} %copy-done.3, ...), custom_call_target="tpu_custom_call" | custom-call | tf_op jit(solution)/shard_map/pallas_call | solution.py:61
  4.5 3.1 %collective-permute-start = (bf16[144,256]{1,0:T(8,128)(2,1)S(1)}, bf16[144,256]{1,0:T(8,128)(2,1)S(1)}, u32[]{:S(2)}, u32[]{:S(2)}) collective-permute-start(bf16[144,256]{1,0:T(8,128)(2,1)S(1)} %get-tuple-element.11), channel_id=1, source_target_pairs={{0,8},{1,9},{2,10},{3,11},{4,12},{5,13},{6,14},{7,15},{8,0},{9,1},... | collective-permute-start | bytes 221192 | tf_op jit(solution)/shard_map/ppermute | solution.py:242
  7.6 2.6 %collective-permute-start.1 = (bf16[144,256]{1,0:T(8,128)(2,1)S(1)}, bf16[144,256]{1,0:T(8,128)(2,1)S(1)}, u32[]{:S(2)}, u32[]{:S(2)}) collective-permute-start(bf16[144,256]{1,0:T(8,128)(2,1)S(1)} %get-tuple-element.12), channel_id=1, source_target_pairs={{0,16},{1,17},{2,18},{3,19},{4,20},{5,21},{6,22},{7,23},{8,24},{9,... | collective-permute-start | bytes 221192 | tf_op jit(solution)/shard_map/ppermute | solution.py:242
  10.1 5.2 %collective-permute-done.1.refs_2_ = bf16[144,256]{1,0:T(8,128)(2,1)S(1)} collective-permute-done((bf16[144,256]{1,0:T(8,128)(2,1)S(1)}, bf16[144,256]{1,0:T(8,128)(2,1)S(1)}, u32[]{:S(2)}, u32[]{:S(2)}) %collective-permute-start.1) | collective-permute-done | bytes 73760 | tf_op jit(solution)/shard_map/ppermute | solution.py:242
  15.3 1.1 %collective-permute-done.2.refs_3_ = bf16[144,256]{1,0:T(8,128)(2,1)S(1)} collective-permute-done((bf16[144,256]{1,0:T(8,128)(2,1)S(1)}, bf16[144,256]{1,0:T(8,128)(2,1)S(1)}, u32[]{:S(2)}, u32[]{:S(2)}) %collective-permute-start.2) | collective-permute-done | bytes 73760 | tf_op jit(solution)/shard_map/ppermute | solution.py:242
  16.4 1.6 %collective-permute-start.3 = (bf16[528,256]{1,0:T(8,128)(2,1)S(1)}, bf16[528,256]{1,0:T(8,128)(2,1)S(1)}, u32[]{:S(2)}, u32[]{:S(2)}) collective-permute-start(bf16[528,256]{1,0:T(8,128)(2,1)S(1)} %shard_map.87.refs_0_), channel_id=1, source_target_pairs={{0,2},{1,5},{2,0},{3,7},{4,6},{5,1},{6,4},{7,3},{8,10},{9,13},{10,... | collective-permute-start | bytes 811016 | tf_op jit(solution)/shard_map/ppermute | solution.py:242
  18.0 1.5 %collective-permute-start.6 = (bf16[528,256]{1,0:T(8,128)(2,1)S(1)}, bf16[528,256]{1,0:T(8,128)(2,1)S(1)}, u32[]{:S(2)}, u32[]{:S(2)}) collective-permute-start(bf16[528,256]{1,0:T(8,128)(2,1)S(1)} %shard_map.87.refs_0_), channel_id=1, source_target_pairs={{0,4},{1,3},{2,6},{3,1},{4,0},{5,7},{6,2},{7,5},{8,12},{9,11},{10,... | collective-permute-start | bytes 811016 | tf_op jit(solution)/shard_map/ppermute | solution.py:242
  19.5 6.3 %collective-permute-done.3 = bf16[528,256]{1,0:T(8,128)(2,1)S(1)} collective-permute-done((bf16[528,256]{1,0:T(8,128)(2,1)S(1)}, bf16[528,256]{1,0:T(8,128)(2,1)S(1)}, u32[]{:S(2)}, u32[]{:S(2)}) %collective-permute-start.3) | collective-permute-done | bytes 270368 | tf_op jit(solution)/shard_map/ppermute | solution.py:242
  25.8 0.0 collective-permute-start.8
  25.8 0.5 %collective-permute-start.7 = (bf16[528,256]{1,0:T(8,128)(2,1)S(1)}, bf16[528,256]{1,0:T(8,128)(2,1)S(1)}, u32[]{:S(2)}, u32[]{:S(2)}) collective-permute-start(bf16[528,256]{1,0:T(8,128)(2,1)S(1)} %collective-permute-done.3), channel_id=1, source_target_pairs={{0,1},{1,0},{2,3},{3,2},{4,5},{5,4},{6,7},{7,6},{8,9},{9,8},{10,11... | collective-permute-start | bytes 811016 | tf_op jit(solution)/shard_map/ppermute | solution.py:242
  26.3 2.2 %copy-done = f32[4096,256]{1,0:T(8,128)S(1)} copy-done((f32[4096,256]{1,0:T(8,128)S(1)}, f32[4096,256]{1,0:T(8,128)}, u32[]{:S(2)}) %copy-start) | copy-done | bytes 4194328
  28.5 0.7 %copy-done.5 = s32[1,16]{1,0:T(1,128)S(1)} copy-done((s32[1,16]{1,0:T(1,128)S(1)}, s32[1,16]{1,0:T(1,128)}, u32[]{:S(2)}) %copy-start.5) | copy-done | bytes 88
  29.2 3.5 %shard_map.90 = (f32[4096,256]{1,0:T(8,128)}, f32[2048,256]{1,0:T(8,128)S(1)}) custom-call(s32[1,16]{1,0:T(1,128)S(1)} %copy-done.5, f32[4096,256]{1,0:T(8,128)S(1)} %copy-done), custom_call_target="tpu_custom_call" | custom-call | bytes 12582912 | tf_op jit(solution)/shard_map/pallas_call | solution.py:162
  32.7 0.1 collective-permute-start.9
  32.8 0.5 %collective-permute-start.5 = (bf16[528,256]{1,0:T(8,128)(2,1)S(1)}, bf16[528,256]{1,0:T(8,128)(2,1)S(1)}, u32[]{:S(2)}, u32[]{:S(2)}) collective-permute-start(bf16[528,256]{1,0:T(8,128)(2,1)S(1)} %collective-permute-done.4.last0), channel_id=1, source_target_pairs={{0,1},{1,0},{2,3},{3,2},{4,5},{5,4},{6,7},{7,6},{8,9},{9,8},{10,11... | collective-permute-start | bytes 811016 | tf_op jit(solution)/shard_map/ppermute | solution.py:242
  33.4 1.3 %shard_map.88.side_ref = f32[2048,256]{1,0:T(8,128)S(1)} custom-call(bf16[528,256]{1,0:T(8,128)(2,1)S(1)} %get-tuple-element.21.refs_0_, bf16[528,256]{1,0:T(8,128)(2,1)S(1)} %get-tuple-element.19.refs_1_), custom_call_target="tpu_custom_call" | custom-call | flops 1073741824 | bytes 2097152 | tf_op jit(solution)/shard_map/pallas_call | solution.py:127
  34.7 0.0 copy-start.2
  34.7 0.0 copy-start.6
  34.7 2.3 %shard_map.89.near_ref = f32[2048,256]{1,0:T(8,128)S(1)} custom-call(bf16[528,256]{1,0:T(8,128)(2,1)S(1)} %shard_map.87.refs_0_, bf16[528,256]{1,0:T(8,128)(2,1)S(1)} %collective-permute-done.9.refs_1_, bf16[528,256]{1,0:T(8,128)(2,1)S(1)} %get-tuple-element.20.refs_2_, bf16[528,256]{1,0:T(8,128)(2,1)S(1)} %get-tuple-element.18.refs_3_), custom_call_target="tpu_custom_call" | custom-call | flops 2147483648 | bytes 2097152 | tf_op jit(solution)/shard_map/pallas_call | solution.py:127
  37.1 5.0 %shard_map.91 = (f32[4096,256]{1,0:T(8,128)}, f32[32,128]{1,0:T(8,128)}) custom-call(s32[1,16]{1,0:T(1,128)S(1)} %copy-done.6, bf16[528,256]{1,0:T(8,128)(2,1)S(1)} %collective-permute-done.4.last0, bf16[528,256]{1,0:T(8,128)(2,1)S(1)} %collective-permute-done.5.last1, f32[2048,256]{1,0:T(8,128)S(1)} %shard_map.88.side_ref, ...), custom_call_target="tpu_custom_call", output_to_operand_aliasing={{0}: (7, {})} | custom-call | tf_op jit(solution)/shard_map/pallas_call | solution.py:211
  (20 shorter events, 0.1 us)
Async XLA Ops:
  0.6 0.9 %copy-start.1 = (bf16[256,256]{1,0:T(8,128)(2,1)S(1)}, bf16[256,256]{1,0:T(8,128)(2,1)}, u32[]{:S(2)}) copy-start(bf16[256,256]{1,0:T(8,128)(2,1)} %grad_ref.1) | copy-start | bytes 393220
  1.5 0.7 %copy-start.3 = (s32[4,128]{1,0:T(4,128)S(1)}, s32[4,128]{1,0:T(4,128)}, u32[]{:S(2)}) copy-start(s32[4,128]{1,0:T(4,128)} %sample_ref.1) | copy-start | bytes 6148
  2.2 0.7 %copy-start.4 = (s32[4,128]{1,0:T(4,128)S(1)}, s32[4,128]{1,0:T(4,128)}, u32[]{:S(2)}) copy-start(s32[4,128]{1,0:T(4,128)} %row_ref.1) | copy-start | bytes 6148
  2.9 0.7 %copy-start.7 = (s32[4]{0:T(128)S(1)}, s32[4]{0:T(128)}, u32[]{:S(2)}) copy-start(s32[4]{0:T(128)} %count_ref.1) | copy-start | bytes 52
  4.5 5.7 %collective-permute-start = (bf16[144,256]{1,0:T(8,128)(2,1)S(1)}, bf16[144,256]{1,0:T(8,128)(2,1)S(1)}, u32[]{:S(2)}, u32[]{:S(2)}) collective-permute-start(bf16[144,256]{1,0:T(8,128)(2,1)S(1)} %get-tuple-element.11), channel_id=1, source_target_pairs={{0,8},{1,9},{2,10},{3,11},{4,12},{5,13},{6,14},{7,15},{8,0},{9,1},... | collective-permute-start | bytes 221192 | tf_op jit(solution)/shard_map/ppermute | solution.py:242
  7.6 7.8 %collective-permute-start.1 = (bf16[144,256]{1,0:T(8,128)(2,1)S(1)}, bf16[144,256]{1,0:T(8,128)(2,1)S(1)}, u32[]{:S(2)}, u32[]{:S(2)}) collective-permute-start(bf16[144,256]{1,0:T(8,128)(2,1)S(1)} %get-tuple-element.12), channel_id=1, source_target_pairs={{0,16},{1,17},{2,18},{3,19},{4,20},{5,21},{6,22},{7,23},{8,24},{9,... | collective-permute-start | bytes 221192 | tf_op jit(solution)/shard_map/ppermute | solution.py:242
  10.1 6.3 %collective-permute-start.2 = (bf16[144,256]{1,0:T(8,128)(2,1)S(1)}, bf16[144,256]{1,0:T(8,128)(2,1)S(1)}, u32[]{:S(2)}, u32[]{:S(2)}) collective-permute-start(bf16[144,256]{1,0:T(8,128)(2,1)S(1)} %get-tuple-element.13), channel_id=1, source_target_pairs={{0,24},{1,25},{2,26},{3,27},{4,28},{5,29},{6,30},{7,31},{8,16},{9,... | collective-permute-start | bytes 221192 | tf_op jit(solution)/shard_map/ppermute | solution.py:242
  16.4 9.4 %collective-permute-start.3 = (bf16[528,256]{1,0:T(8,128)(2,1)S(1)}, bf16[528,256]{1,0:T(8,128)(2,1)S(1)}, u32[]{:S(2)}, u32[]{:S(2)}) collective-permute-start(bf16[528,256]{1,0:T(8,128)(2,1)S(1)} %shard_map.87.refs_0_), channel_id=1, source_target_pairs={{0,2},{1,5},{2,0},{3,7},{4,6},{5,1},{6,4},{7,3},{8,10},{9,13},{10,... | collective-permute-start | bytes 811016 | tf_op jit(solution)/shard_map/ppermute | solution.py:242
  18.0 7.8 %collective-permute-start.6 = (bf16[528,256]{1,0:T(8,128)(2,1)S(1)}, bf16[528,256]{1,0:T(8,128)(2,1)S(1)}, u32[]{:S(2)}, u32[]{:S(2)}) collective-permute-start(bf16[528,256]{1,0:T(8,128)(2,1)S(1)} %shard_map.87.refs_0_), channel_id=1, source_target_pairs={{0,4},{1,3},{2,6},{3,1},{4,0},{5,7},{6,2},{7,5},{8,12},{9,11},{10,... | collective-permute-start | bytes 811016 | tf_op jit(solution)/shard_map/ppermute | solution.py:242
  25.8 7.0 %collective-permute-start.4 = (bf16[528,256]{1,0:T(8,128)(2,1)S(1)}, bf16[528,256]{1,0:T(8,128)(2,1)S(1)}, u32[]{:S(2)}, u32[]{:S(2)}) collective-permute-start(bf16[528,256]{1,0:T(8,128)(2,1)S(1)} %collective-permute-done.3), channel_id=1, source_target_pairs={{0,4},{1,3},{2,6},{3,1},{4,0},{5,7},{6,2},{7,5},{8,12},{9,11},{10,... | collective-permute-start | bytes 811016 | tf_op jit(solution)/shard_map/ppermute | solution.py:242
  25.8 7.6 %collective-permute-start.8 = (bf16[528,256]{1,0:T(8,128)(2,1)S(1)}, bf16[528,256]{1,0:T(8,128)(2,1)S(1)}, u32[]{:S(2)}, u32[]{:S(2)}) collective-permute-start(bf16[528,256]{1,0:T(8,128)(2,1)S(1)} %collective-permute-done.6), channel_id=1, source_target_pairs={{0,1},{1,0},{2,3},{3,2},{4,5},{5,4},{6,7},{7,6},{8,9},{9,8},{10,11... | collective-permute-start | bytes 811016 | tf_op jit(solution)/shard_map/ppermute | solution.py:242
  25.8 7.5 %collective-permute-start.7 = (bf16[528,256]{1,0:T(8,128)(2,1)S(1)}, bf16[528,256]{1,0:T(8,128)(2,1)S(1)}, u32[]{:S(2)}, u32[]{:S(2)}) collective-permute-start(bf16[528,256]{1,0:T(8,128)(2,1)S(1)} %collective-permute-done.3), channel_id=1, source_target_pairs={{0,1},{1,0},{2,3},{3,2},{4,5},{5,4},{6,7},{7,6},{8,9},{9,8},{10,11... | collective-permute-start | bytes 811016 | tf_op jit(solution)/shard_map/ppermute | solution.py:242
  26.3 2.2 %copy-start = (f32[4096,256]{1,0:T(8,128)S(1)}, f32[4096,256]{1,0:T(8,128)}, u32[]{:S(2)}) copy-start(f32[4096,256]{1,0:T(8,128)} %table_ref.1) | copy-start | bytes 12582916
  28.5 0.7 %copy-start.5 = (s32[1,16]{1,0:T(1,128)S(1)}, s32[1,16]{1,0:T(1,128)}, u32[]{:S(2)}) copy-start(s32[1,16]{1,0:T(1,128)} %blocks_ref.3) | copy-start | bytes 196
  32.7 2.0 %collective-permute-start.9 = (bf16[528,256]{1,0:T(8,128)(2,1)S(1)}, bf16[528,256]{1,0:T(8,128)(2,1)S(1)}, u32[]{:S(2)}, u32[]{:S(2)}) collective-permute-start(bf16[528,256]{1,0:T(8,128)(2,1)S(1)} %shard_map.87.refs_0_), channel_id=1, source_target_pairs={{0,1},{1,0},{2,3},{3,2},{4,5},{5,4},{6,7},{7,6},{8,9},{9,8},{10,11... | collective-permute-start | bytes 811016 | tf_op jit(solution)/shard_map/ppermute | solution.py:242
  32.8 4.2 %collective-permute-start.5 = (bf16[528,256]{1,0:T(8,128)(2,1)S(1)}, bf16[528,256]{1,0:T(8,128)(2,1)S(1)}, u32[]{:S(2)}, u32[]{:S(2)}) collective-permute-start(bf16[528,256]{1,0:T(8,128)(2,1)S(1)} %collective-permute-done.4.last0), channel_id=1, source_target_pairs={{0,1},{1,0},{2,3},{3,2},{4,5},{5,4},{6,7},{7,6},{8,9},{9,8},{10,11... | collective-permute-start | bytes 811016 | tf_op jit(solution)/shard_map/ppermute | solution.py:242
  34.7 2.4 %copy-start.2 = (f32[4096]{0:T(1024)S(1)}, f32[4096]{0:T(1024)}, u32[]{:S(2)}) copy-start(f32[4096]{0:T(1024)} %param.13) | copy-start | bytes 49156
  34.7 2.4 %copy-start.6 = (s32[1,16]{1,0:T(1,128)S(1)}, s32[1,16]{1,0:T(1,128)}, u32[]{:S(2)}) copy-start(s32[1,16]{1,0:T(1,128)} %blocks_ref.3) | copy-start | bytes 196

commit v2 on v1

v2 whole, which is shorter than its diff:
```python
import functools

import jax
import jax.numpy as jnp
from jax import lax
from jax.experimental import pallas as pl
from jax.experimental.pallas import tpu as pltpu
from jax.sharding import PartitionSpec as P

TILE = 128
TAIL = 16
LEARNING_RATE = 0.5
EPSILON = 1e-06
ORDER = 3, 2, 1
VMEM = pltpu.VMEM
SMEM = pltpu.SMEM
F32 = jnp.float32
BF16 = jnp.bfloat16


def params(mib=24):
    return pltpu.CompilerParams(vmem_limit_bytes=mib * 2**20)


def whole(space=VMEM):
    return pl.BlockSpec(memory_space=space)


def pack_kernel(me_ref, grad_ref, places_ref, *out_refs):
    owners = len(out_refs)
    cap = places_ref.shape[1]
    samples, cols = grad_ref.shape
    sub = lax.broadcasted_iota(jnp.int32, (samples, cap), 0)

    def picks(o):
        return (sub == places_ref[pl.ds(o, 1), :]).astype(F32)

    total = picks(0)
    for o in range(1, owners):
        total = total + picks(o)
    lengths = jnp.sum(total, axis=1, keepdims=True)
    scaled = (grad_ref[...].astype(F32) * (1.0 / jnp.maximum(lengths, 1.0))).astype(BF16)
    tail_row = lax.broadcasted_iota(jnp.int32, (TAIL, cap), 0)
    for j in range(owners):
        o = me_ref[0] ^ j
        values = lax.dot_general(
            picks(o).astype(BF16), scaled, (((0,), (0,)), ((), ())), preferred_element_type=F32
        )
        out_refs[j][0:cap, :] = values.astype(BF16)
        row = places_ref[pl.ds(owners + o, 1), :]
        slot = row // TILE
        within = row - slot * TILE
        tail = jnp.where(tail_row == 0, slot, jnp.where(tail_row == 1, within, 0))
        out_refs[j][cap : cap + TAIL, :] = jnp.zeros((TAIL, cols), BF16)
        out_refs[j][cap : cap + TAIL, 0:cap] = tail.astype(F32).astype(BF16)


def pack(me, count, grad, sample, row):
    owners, cap = sample.shape
    live = lax.broadcasted_iota(jnp.int32, sample.shape, 1) < count[:, None]
    places = jnp.concatenate([jnp.where(live, sample, -1), row], axis=0)
    shape = jax.ShapeDtypeStruct((cap + TAIL, grad.shape[1]), BF16)
    return pl.pallas_call(
        pack_kernel,
        out_shape=[shape] * owners,
        in_specs=[whole(SMEM), whole(), whole()],
        out_specs=[whole()] * owners,
        compiler_params=params(),
    )(me, grad, places)


def join_kernel(*refs):
    ins, out = refs[:-1], refs[-1]
    cap = ins[0].shape[0] - TAIL
    n = len(ins)
    for c, ref in enumerate(ins):
        out[c * cap : (c + 1) * cap, :] = ref[0:cap, :]
    sub = lax.broadcasted_iota(jnp.int32, (TAIL, ins[0].shape[1]), 0)
    tail = jnp.zeros((TAIL, ins[0].shape[1]), F32)
    for c, ref in enumerate(ins):
        own = ref[cap : cap + TAIL, :].astype(F32)
        tail = jnp.where(sub == 2 * c, own[0:1, :], jnp.where(sub == 2 * c + 1, own[1:2, :], tail))
    out[n * cap : n * cap + TAIL, :] = tail.astype(BF16)


def join(chunks):
    cap = chunks[0].shape[0] - TAIL
    cols = chunks[0].shape[1]
    return pl.pallas_call(
        join_kernel,
        out_shape=jax.ShapeDtypeStruct((len(chunks) * cap + TAIL, cols), BF16),
        in_specs=[whole()] * len(chunks),
        out_specs=whole(),
        compiler_params=params(),
    )(*chunks)


def positions(ref, cap):
    entries = ref.shape[0] - TAIL
    tail = ref[entries : entries + TAIL, 0:cap].astype(F32)
    n = entries // cap
    slot = jnp.concatenate([tail[2 * c : 2 * c + 1] for c in range(n)], axis=1)
    within = jnp.concatenate([tail[2 * c + 1 : 2 * c + 2] for c in range(n)], axis=1)
    return slot, within


def block_sum(ref, place, k):
    slot, within = place
    here = jnp.where(slot == k, within, -1.0).astype(BF16)
    entries = here.shape[1]
    sub = lax.broadcasted_iota(jnp.int32, (TILE, entries), 0).astype(F32).astype(BF16)
    pick = jnp.where(sub == here, jnp.ones((), BF16), jnp.zeros((), BF16))
    return jnp.dot(pick, ref[0:entries, :], preferred_element_type=F32)


def own_kernel(cap, own, part):
    place = positions(own, cap)
    for k in range(part.shape[0] // TILE):
        part[k * TILE : (k + 1) * TILE, :] = block_sum(own, place, k)


def side_kernel(cap, odd_ref, own_c, one, two_c, two, one_c, part, near, side):
    even = odd_ref[0] == 0
    payloads = (own_c, one, two_c, two, one_c)
    places = [positions(ref, cap) for ref in payloads]
    for k in range(near.shape[0] // TILE):
        span = slice(k * TILE, (k + 1) * TILE)
        other, a, b, c, d = [block_sum(ref, place, k) for ref, place in zip(payloads, places)]
        left, right = a + b, c + d
        near[span, :] = (part[span, :] + other) + jnp.where(even, left, right)
        side[span, :] = jnp.where(even, right, left)


def sum_cost(payloads, span):
    entries, cols = payloads[0].shape[0] - TAIL, payloads[0].shape[1]
    return pl.CostEstimate(
        flops=2 * span * entries * cols * len(payloads),
        bytes_accessed=span * cols * 4,
        transcendentals=0,
    )


def own_sum(own, span, cap):
    return pl.pallas_call(
        functools.partial(own_kernel, cap),
        out_shape=jax.ShapeDtypeStruct((span, own.shape[1]), F32),
        in_specs=[whole()],
        out_specs=whole(),
        compiler_params=params(),
        cost_estimate=sum_cost([own], span),
    )(own)


def side_sum(odd, payloads, part, span, cap):
    return pl.pallas_call(
        functools.partial(side_kernel, cap),
        out_shape=[jax.ShapeDtypeStruct((span, part.shape[1]), F32)] * 2,
        in_specs=[whole(SMEM)] + [whole()] * 6,
        out_specs=[whole()] * 2,
        compiler_params=params(),
        cost_estimate=sum_cost(payloads, span),
    )(odd, *payloads, part)


def update_kernel(
    cap, blocks_ref, last_m, last_c, near, side, table_in, accum_ref,
    table_ref, accum_out, rows_out, kept, sems,
):
    n = rows_out.shape[0] // TILE
    cols = rows_out.shape[1]
    tiles = accum_ref.shape[0]

    def tile(ref, block):
        return ref.at[pl.ds(pl.multiple_of(block * TILE, TILE), TILE), :]

    seen = jnp.int32(0)
    for t in range(tiles):
        touched = blocks_ref[0, jnp.minimum(seen, n - 1)] == t

        @pl.when(jnp.logical_not(touched))
        def _():
            pltpu.make_async_copy(tile(table_in, t), tile(table_ref, t), kept).start()

        seen = seen + touched.astype(jnp.int32)
    place_m, place_c = positions(last_m, cap), positions(last_c, cap)
    accum_out[...] = accum_ref[...]
    old = jnp.concatenate(
        [accum_ref[pl.ds(blocks_ref[0, k], 1), :] for k in range(n)], axis=0
    ).T
    news = []
    copies = []
    for k in range(n):
        span = slice(k * TILE, (k + 1) * TILE)
        block = pl.multiple_of(blocks_ref[0, k] * TILE, TILE)
        far = block_sum(last_m, place_m, k) + block_sum(last_c, place_c, k)
        total = near[span, :] + (side[span, :] + far)
        grad = total.astype(BF16).astype(F32)
        mean = jnp.sum(grad * grad, axis=1, keepdims=True) * (1.0 / cols)
        new = old[:, k : k + 1] + mean
        rate = LEARNING_RATE / (jnp.sqrt(new) + EPSILON)
        rows_out[span, :] = table_in[pl.ds(block, TILE), :] - grad * rate
        news.append(new)
        c = pltpu.make_async_copy(rows_out.at[span, :], tile(table_ref, blocks_ref[0, k]), sems.at[k])
        c.start()
        copies.append(c)
    flat = jnp.concatenate(news, axis=1).T
    for k in range(n):
        accum_out[pl.ds(blocks_ref[0, k], 1), :] = flat[k : k + 1, :]
    for _ in range(tiles - n):
        pltpu.make_async_copy(tile(table_in, 0), tile(table_ref, 0), kept).wait()
    for c in copies:
        c.wait()


def update(blocks, last, sums, table, accum, cap):
    n = blocks.shape[1]
    cols = table.shape[1]
    return pl.pallas_call(
        functools.partial(update_kernel, cap),
        out_shape=[
            jax.ShapeDtypeStruct(table.shape, F32),
            jax.ShapeDtypeStruct(accum.shape, F32),
        ],
        in_specs=[whole(SMEM)] + [whole()] * 6,
        out_specs=[whole(pltpu.HBM), whole()],
        scratch_shapes=[
            VMEM((n * TILE, cols), F32),
            pltpu.SemaphoreType.DMA,
            pltpu.SemaphoreType.DMA((n,)),
        ],
        compiler_params=params(),
    )(blocks, *last, *sums, table, accum)


def after(x, *earlier):
    return lax.optimization_barrier((x,) + earlier)[0]


def gathered(pooled_grad, send_sample, send_row, send_count, union_blocks, table, accum):
    shards = lax.axis_size("shard")
    reps = lax.axis_size("rep")
    cap = send_sample.shape[1]
    span = union_blocks.shape[1] * TILE
    me = lax.axis_index("shard").astype(jnp.int32).reshape(1)

    def swap(x, flip):
        pairs = []
        for z in range(shards):
            for r in range(reps):
                dz, dr = flip(r)
                pairs.append((z * reps + r, (z ^ dz) * reps + (r ^ dr)))
        return lax.ppermute(x, ("shard", "rep"), pairs)

    def first(x):
        return swap(x, lambda r: (0, 2 if r % 2 == 0 else 4))

    def second(x):
        return swap(x, lambda r: (0, 4 if r % 2 == 0 else 2))

    def core(x):
        return swap(x, lambda r: (0, 1))

    odd = (lax.axis_index("rep").astype(jnp.int32) % 2).reshape(1)
    mine = pack(me, send_count, pooled_grad, send_sample, send_row)
    arrived = [swap(mine[j], lambda r: (j, 0)) for j in ORDER]
    own = join([mine[0]] + arrived)
    one = first(own)
    part = own_sum(own, span, cap)
    two = second(after(own, part))
    own_c = core(own)
    diag = second(one)
    one_c, two_c = core(one), core(two)
    near, side = side_sum(odd, [own_c, one, two_c, two, one_c], part, span, cap)
    diag_c = core(after(diag, near))
    table_out, accum_out = update(
        union_blocks, (diag, diag_c), (near, side), table, accum.reshape(-1, TILE), cap
    )
    return table_out, accum_out.reshape(accum.shape)


def reduced(pooled_grad, send_sample, send_row, send_count, union_blocks, table, accum):
    columns = pooled_grad.shape[1]
    samples = pooled_grad.shape[0]
    active = (lax.broadcasted_iota(jnp.int32, send_sample.shape, 1) < send_count[:, None]).astype(F32)
    lengths = jax.ops.segment_sum(active.reshape(-1), send_sample.reshape(-1), num_segments=samples)
    scaled = active / jnp.maximum(lengths, 1.0)[send_sample]
    values = (pooled_grad[send_sample].astype(F32) * scaled[:, :, None]).astype(BF16)
    arrived = lax.all_to_all(values, "shard", split_axis=0, concat_axis=0, tiled=True)
    places = lax.all_to_all(send_row, "shard", split_axis=0, concat_axis=0, tiled=True)
    blocks = union_blocks[0]
    span = blocks.shape[0] * TILE
    local = (
        jnp.zeros((span, columns), F32)
        .at[places.reshape(-1)]
        .add(arrived.reshape(-1, columns).astype(F32))
    )
    table_tiles = table.reshape(-1, TILE, columns)
    accum_tiles = accum.reshape(-1, TILE)
    grad = lax.optimization_barrier(lax.psum(local.astype(BF16), "rep")).astype(F32)
    acc_new = accum_tiles[blocks].reshape(span) + jnp.mean(grad * grad, axis=-1)
    rows_new = table_tiles[blocks].reshape(span, columns) - LEARNING_RATE * grad / (
        jnp.sqrt(acc_new)[:, None] + EPSILON
    )
    table_out = table_tiles.at[blocks].set(rows_new.reshape(-1, TILE, columns)).reshape(table.shape)
    accum_out = accum_tiles.at[blocks].set(acc_new.reshape(-1, TILE)).reshape(accum.shape)
    return table_out, accum_out


def solution(mesh):
    both = ("shard", "rep")
    in_specs = (
        P(both, None),
        P(both, None),
        P(both, None),
        P(both),
        P("shard", None),
        P("shard", None),
        P("shard"),
    )
    out_specs = (P("shard", None), P("shard"))
    small = mesh.shape["shard"] == 4 and mesh.shape["rep"] == 8
    return jax.shard_map(
        gathered if small else reduced,
        mesh=mesh,
        in_specs=in_specs,
        out_specs=out_specs,
        check_vma=False,
    )
```

time: 42.3 us -> 36.4 us (0.86)
  local copies, waits for them, and re-layouts: 5.77 us -> 0.92 us
  Pallas kernels: 13 us -> 9.44 us
  other arithmetic: 0.08 us -> 1.44 us
  starting transfers between devices: 9.9 us -> 11 us
    unnamed x16 -> x8, local copies, waits for them, and re-layouts: 5.77 us -> 0.92 us
    pallas_call x3 -> x2, Pallas kernels: 7.08 us -> 4.87 us  [the longest x1 4.16 us: side_sum(): pl.pallas_call(functools.partial(side_kernel, cap), out_shape=[jax.ShapeD...]
    ppermute x10, starting transfers between devices: 9.9 us -> 11 us  [swap(): return lax.ppermute(x, ('shard', 'rep'), pairs)]
    pallas_call x1, Pallas kernels: 4.98 us -> 4.19 us  [update(): pl.pallas_call(functools.partial(update_kernel, cap), out_shape=[jax.Shap...]
    concatenate x0 -> x1, other arithmetic: none -> 0.69 us  [pack(): places = jnp.concatenate([jnp.where(live, sample, -1), row], axis=0)]
    select_n x2 -> x1, other arithmetic: 0.08 us -> 0.75 us  [pack(): places = jnp.concatenate([jnp.where(live, sample, -1), row], axis=0)]
    pallas_call x1, Pallas kernels: 0.9 us -> 0.36 us  [pack(): pl.pallas_call(pack_kernel, out_shape=[shape] * owners, in_specs=[whole(S...]
  transfers between devices with their start and end apart: 10 -> 10, of which waited for: 3 -> 5; matrix products, arithmetic and copies ran while one was open for 0% -> 0% of each run, Pallas kernels for 17% -> 13%
where the time goes in v2:
time: 36.4 us; the launch traced here: 36.2 us
  waiting for transfers between devices  12.6 us (35%)
  starting transfers between devices  11 us (30%)
  Pallas kernels  9.44 us (26%)
  other arithmetic  1.44 us (4%)
  local copies, waits for them, and re-layouts  0.92 us (3%)
  between operations  0.71 us (2%)
    ppermute x10, waiting for transfers between devices, swap(): return lax.ppermute(x, ('shard', 'rep'), pairs)  12.6 us
    ppermute x10, starting transfers between devices, swap(): return lax.ppermute(x, ('shard', 'rep'), pairs)  11 us
    pallas_call x1, Pallas kernels, update(): pl.pallas_call(functools.partial(update_kernel, cap), out_shape=[jax.Shap...  4.19 us
    pallas_call x1, Pallas kernels, side_sum(): pl.pallas_call(functools.partial(side_kernel, cap), out_shape=[jax.ShapeD...  4.16 us
    unnamed x8, local copies, waits for them, and re-layouts  0.92 us
    select_n x1, other arithmetic, pack(): places = jnp.concatenate([jnp.where(live, sample, -1), row], axis=0)  0.75 us
  transfers between devices with their start and end apart: 10, of which 5 were waited for; matrix products, arithmetic and copies ran while one was open for 0% of the time, Pallas kernels for 13%

profile of v2, /device:TPU:0, one launch (start us, length us, event | category | flops | bytes accessed | tf_op | source)
XLA Modules:
  0.0 36.2 jit_solution(6412020732065597350)
XLA Ops:
  0.6 0.8 %fusion = s32[4,128]{1,0:T(4,128)S(1)} fusion(s32[4,128]{1,0:T(4,128)} %param.8, s32[4]{0:T(128)} %param.10), kind=kLoop, calls=%fused_computation.2 | loop fusion | flops 1024 | bytes 4112 | tf_op jit(solution)/shard_map/jit(_where)/select_n | solution.py:61
  1.4 0.7 %pad_add_fusion.places_ref = s32[8,128]{1,0:T(8,128)S(1)} fusion(s32[4,128]{1,0:T(4,128)} %param.9, s32[4,128]{1,0:T(4,128)S(1)} %fusion), kind=kLoop, calls=%fused_computation | loop fusion | flops 1024 | bytes 8192 | tf_op jit(solution)/shard_map/concatenate | solution.py:61
  2.1 0.9 %copy-done.1 = bf16[256,256]{1,0:T(8,128)(2,1)S(1)} copy-done((bf16[256,256]{1,0:T(8,128)(2,1)S(1)}, bf16[256,256]{1,0:T(8,128)(2,1)}, u32[]{:S(2)}) %copy-start.1) | copy-done | bytes 131096
  3.0 0.4 shard_map.86
  3.3 5.1 %collective-permute-start = (bf16[144,256]{1,0:T(8,128)(2,1)S(1)}, bf16[144,256]{1,0:T(8,128)(2,1)S(1)}, u32[]{:S(2)}, u32[]{:S(2)}) collective-permute-start(bf16[144,256]{1,0:T(8,128)(2,1)S(1)} %get-tuple-element.13), channel_id=1, source_target_pairs={{0,24},{1,25},{2,26},{3,27},{4,28},{5,29},{6,30},{7,31},{8,16},{9,... | collective-permute-start | bytes 221192 | tf_op jit(solution)/shard_map/ppermute | solution.py:252
  8.5 0.0 collective-permute-start.1
  8.5 0.6 %collective-permute-start.2 = (bf16[144,256]{1,0:T(8,128)(2,1)S(1)}, bf16[144,256]{1,0:T(8,128)(2,1)S(1)}, u32[]{:S(2)}, u32[]{:S(2)}) collective-permute-start(bf16[144,256]{1,0:T(8,128)(2,1)S(1)} %get-tuple-element.15), channel_id=1, source_target_pairs={{0,8},{1,9},{2,10},{3,11},{4,12},{5,13},{6,14},{7,15},{8,0},{9,1},... | collective-permute-start | bytes 221192 | tf_op jit(solution)/shard_map/ppermute | solution.py:252
  9.1 2.1 %collective-permute-done.refs_1_ = bf16[144,256]{1,0:T(8,128)(2,1)S(1)} collective-permute-done((bf16[144,256]{1,0:T(8,128)(2,1)S(1)}, bf16[144,256]{1,0:T(8,128)(2,1)S(1)}, u32[]{:S(2)}, u32[]{:S(2)}) %collective-permute-start) | collective-permute-done | bytes 73760 | tf_op jit(solution)/shard_map/ppermute | solution.py:252
  11.2 3.5 %collective-permute-done.1.refs_2_ = bf16[144,256]{1,0:T(8,128)(2,1)S(1)} collective-permute-done((bf16[144,256]{1,0:T(8,128)(2,1)S(1)}, bf16[144,256]{1,0:T(8,128)(2,1)S(1)}, u32[]{:S(2)}, u32[]{:S(2)}) %collective-permute-start.1) | collective-permute-done | bytes 73760 | tf_op jit(solution)/shard_map/ppermute | solution.py:252
  14.7 0.0 collective-permute-done.2.refs_3_
  14.7 1.6 %collective-permute-start.3 = (bf16[528,256]{1,0:T(8,128)(2,1)S(1)}, bf16[528,256]{1,0:T(8,128)(2,1)S(1)}, u32[]{:S(2)}, u32[]{:S(2)}) collective-permute-start(bf16[528,256]{1,0:T(8,128)(2,1)S(1)} %shard_map.87.own), channel_id=1, source_target_pairs={{0,2},{1,5},{2,0},{3,7},{4,6},{5,1},{6,4},{7,3},{8,10},{9,13},{10,... | collective-permute-start | bytes 811016 | tf_op jit(solution)/shard_map/ppermute | solution.py:252
  16.3 0.7 %shard_map.88.part = f32[2048,256]{1,0:T(8,128)S(1)} custom-call(bf16[528,256]{1,0:T(8,128)(2,1)S(1)} %shard_map.87.own), custom_call_target="tpu_custom_call" | custom-call | flops 536870912 | bytes 2097152 | tf_op jit(solution)/shard_map/pallas_call | solution.py:144
  17.0 1.6 %collective-permute-start.6 = (bf16[528,256]{1,0:T(8,128)(2,1)S(1)}, bf16[528,256]{1,0:T(8,128)(2,1)S(1)}, u32[]{:S(2)}, u32[]{:S(2)}) collective-permute-start(bf16[528,256]{1,0:T(8,128)(2,1)S(1)} %shard_map.87.own), channel_id=1, source_target_pairs={{0,4},{1,3},{2,6},{3,1},{4,0},{5,7},{6,2},{7,5},{8,12},{9,11},{10,... | collective-permute-start | bytes 811016 | tf_op jit(solution)/shard_map/ppermute | solution.py:252
  18.6 4.9 %collective-permute-done.3.one = bf16[528,256]{1,0:T(8,128)(2,1)S(1)} collective-permute-done((bf16[528,256]{1,0:T(8,128)(2,1)S(1)}, bf16[528,256]{1,0:T(8,128)(2,1)S(1)}, u32[]{:S(2)}, u32[]{:S(2)}) %collective-permute-start.3) | collective-permute-done | bytes 270368 | tf_op jit(solution)/shard_map/ppermute | solution.py:252
  23.5 0.0 collective-permute-done.6.two
  23.5 0.5 %collective-permute-start.7 = (bf16[528,256]{1,0:T(8,128)(2,1)S(1)}, bf16[528,256]{1,0:T(8,128)(2,1)}, u32[]{:S(2)}, u32[]{:S(2)}) collective-permute-start(bf16[528,256]{1,0:T(8,128)(2,1)S(1)} %collective-permute-done.6.two), channel_id=1, source_target_pairs={{0,1},{1,0},{2,3},{3,2},{4,5},{5,4},{6,7},{7,6},{8,9},{9,8},{10,11... | collective-permute-start | bytes 811016 | tf_op jit(solution)/shard_map/ppermute | solution.py:252
  24.0 1.7 %collective-permute-start.4 = (bf16[528,256]{1,0:T(8,128)(2,1)S(1)}, bf16[528,256]{1,0:T(8,128)(2,1)S(1)}, u32[]{:S(2)}, u32[]{:S(2)}) collective-permute-start(bf16[528,256]{1,0:T(8,128)(2,1)S(1)} %collective-permute-done.3.one), channel_id=1, source_target_pairs={{0,4},{1,3},{2,6},{3,1},{4,0},{5,7},{6,2},{7,5},{8,12},{9,11},{10,... | collective-permute-start | bytes 811016 | tf_op jit(solution)/shard_map/ppermute | solution.py:252
  25.7 0.0 copy-start
  25.7 0.0 copy-start.2
  25.7 0.0 copy-start.3
  25.7 4.2 %shard_map.89 = (f32[2048,256]{1,0:T(8,128)S(1)}, f32[2048,256]{1,0:T(8,128)S(1)}) custom-call(s32[1]{0:T(128)} %bitcast.1.odd_ref, bf16[528,256]{1,0:T(8,128)(2,1)S(1)} %collective-permute-done.5.own_c, bf16[528,256]{1,0:T(8,128)(2,1)S(1)} %collective-permute-done.3.one, bf16[528,256]{1,0:T(8,128)(2,1)} %collective-permute-done.7.two_c, ...), custom_call_target="tpu_custom_call" | custom-call | flops 2684354560 | bytes 2097152 | tf_op jit(solution)/shard_map/pallas_call | solution.py:155
  29.9 0.6 %collective-permute-done.4.last_m = bf16[528,256]{1,0:T(8,128)(2,1)S(1)} collective-permute-done((bf16[528,256]{1,0:T(8,128)(2,1)S(1)}, bf16[528,256]{1,0:T(8,128)(2,1)S(1)}, u32[]{:S(2)}, u32[]{:S(2)}) %collective-permute-start.4) | collective-permute-done | bytes 270368 | tf_op jit(solution)/shard_map/ppermute | solution.py:252
  30.4 1.5 %collective-permute-done.9.last_c = bf16[528,256]{1,0:T(8,128)(2,1)S(1)} collective-permute-done((bf16[528,256]{1,0:T(8,128)(2,1)S(1)}, bf16[528,256]{1,0:T(8,128)(2,1)S(1)}, u32[]{:S(2)}, u32[]{:S(2)}) %collective-permute-start.9) | collective-permute-done | bytes 270368 | tf_op jit(solution)/shard_map/ppermute | solution.py:252
  32.0 4.2 %shard_map.90 = (f32[4096,256]{1,0:T(8,128)}, f32[32,128]{1,0:T(8,128)}) custom-call(s32[1,16]{1,0:T(1,128)S(1)} %copy-done.3, bf16[528,256]{1,0:T(8,128)(2,1)S(1)} %collective-permute-done.4.last_m, bf16[528,256]{1,0:T(8,128)(2,1)S(1)} %collective-permute-done.9.last_c, f32[2048,256]{1,0:T(8,128)S(1)} %get-tuple-element.17.near, ...), custom_call_target="tpu_custom_call" | custom-call | tf_op jit(solution)/shard_map/pallas_call | solution.py:218
  (11 shorter events, 0.0 us)
Async XLA Ops:
  2.1 0.9 %copy-start.1 = (bf16[256,256]{1,0:T(8,128)(2,1)S(1)}, bf16[256,256]{1,0:T(8,128)(2,1)}, u32[]{:S(2)}) copy-start(bf16[256,256]{1,0:T(8,128)(2,1)} %grad_ref.1) | copy-start | bytes 393220
  3.3 7.9 %collective-permute-start = (bf16[144,256]{1,0:T(8,128)(2,1)S(1)}, bf16[144,256]{1,0:T(8,128)(2,1)S(1)}, u32[]{:S(2)}, u32[]{:S(2)}) collective-permute-start(bf16[144,256]{1,0:T(8,128)(2,1)S(1)} %get-tuple-element.13), channel_id=1, source_target_pairs={{0,24},{1,25},{2,26},{3,27},{4,28},{5,29},{6,30},{7,31},{8,16},{9,... | collective-permute-start | bytes 221192 | tf_op jit(solution)/shard_map/ppermute | solution.py:252
  8.5 6.2 %collective-permute-start.1 = (bf16[144,256]{1,0:T(8,128)(2,1)S(1)}, bf16[144,256]{1,0:T(8,128)(2,1)S(1)}, u32[]{:S(2)}, u32[]{:S(2)}) collective-permute-start(bf16[144,256]{1,0:T(8,128)(2,1)S(1)} %get-tuple-element.14), channel_id=1, source_target_pairs={{0,16},{1,17},{2,18},{3,19},{4,20},{5,21},{6,22},{7,23},{8,24},{9,... | collective-permute-start | bytes 221192 | tf_op jit(solution)/shard_map/ppermute | solution.py:252
  8.5 6.2 %collective-permute-start.2 = (bf16[144,256]{1,0:T(8,128)(2,1)S(1)}, bf16[144,256]{1,0:T(8,128)(2,1)S(1)}, u32[]{:S(2)}, u32[]{:S(2)}) collective-permute-start(bf16[144,256]{1,0:T(8,128)(2,1)S(1)} %get-tuple-element.15), channel_id=1, source_target_pairs={{0,8},{1,9},{2,10},{3,11},{4,12},{5,13},{6,14},{7,15},{8,0},{9,1},... | collective-permute-start | bytes 221192 | tf_op jit(solution)/shard_map/ppermute | solution.py:252
  14.7 8.8 %collective-permute-start.3 = (bf16[528,256]{1,0:T(8,128)(2,1)S(1)}, bf16[528,256]{1,0:T(8,128)(2,1)S(1)}, u32[]{:S(2)}, u32[]{:S(2)}) collective-permute-start(bf16[528,256]{1,0:T(8,128)(2,1)S(1)} %shard_map.87.own), channel_id=1, source_target_pairs={{0,2},{1,5},{2,0},{3,7},{4,6},{5,1},{6,4},{7,3},{8,10},{9,13},{10,... | collective-permute-start | bytes 811016 | tf_op jit(solution)/shard_map/ppermute | solution.py:252
  17.0 6.5 %collective-permute-start.6 = (bf16[528,256]{1,0:T(8,128)(2,1)S(1)}, bf16[528,256]{1,0:T(8,128)(2,1)S(1)}, u32[]{:S(2)}, u32[]{:S(2)}) collective-permute-start(bf16[528,256]{1,0:T(8,128)(2,1)S(1)} %shard_map.87.own), channel_id=1, source_target_pairs={{0,4},{1,3},{2,6},{3,1},{4,0},{5,7},{6,2},{7,5},{8,12},{9,11},{10,... | collective-permute-start | bytes 811016 | tf_op jit(solution)/shard_map/ppermute | solution.py:252
  18.6 7.1 %collective-permute-start.5 = (bf16[528,256]{1,0:T(8,128)(2,1)S(1)}, bf16[528,256]{1,0:T(8,128)(2,1)S(1)}, u32[]{:S(2)}, u32[]{:S(2)}) collective-permute-start(bf16[528,256]{1,0:T(8,128)(2,1)S(1)} %shard_map.87.own), channel_id=1, source_target_pairs={{0,1},{1,0},{2,3},{3,2},{4,5},{5,4},{6,7},{7,6},{8,9},{9,8},{10,11... | collective-permute-start | bytes 811016 | tf_op jit(solution)/shard_map/ppermute | solution.py:252
  23.5 2.2 %collective-permute-start.8 = (bf16[528,256]{1,0:T(8,128)(2,1)S(1)}, bf16[528,256]{1,0:T(8,128)(2,1)}, u32[]{:S(2)}, u32[]{:S(2)}) collective-permute-start(bf16[528,256]{1,0:T(8,128)(2,1)S(1)} %collective-permute-done.3.one), channel_id=1, source_target_pairs={{0,1},{1,0},{2,3},{3,2},{4,5},{5,4},{6,7},{7,6},{8,9},{9,8},{10,11... | collective-permute-start | bytes 811016 | tf_op jit(solution)/shard_map/ppermute | solution.py:252
  23.5 2.2 %collective-permute-start.7 = (bf16[528,256]{1,0:T(8,128)(2,1)S(1)}, bf16[528,256]{1,0:T(8,128)(2,1)}, u32[]{:S(2)}, u32[]{:S(2)}) collective-permute-start(bf16[528,256]{1,0:T(8,128)(2,1)S(1)} %collective-permute-done.6.two), channel_id=1, source_target_pairs={{0,1},{1,0},{2,3},{3,2},{4,5},{5,4},{6,7},{7,6},{8,9},{9,8},{10,11... | collective-permute-start | bytes 811016 | tf_op jit(solution)/shard_map/ppermute | solution.py:252
  24.0 6.5 %collective-permute-start.4 = (bf16[528,256]{1,0:T(8,128)(2,1)S(1)}, bf16[528,256]{1,0:T(8,128)(2,1)S(1)}, u32[]{:S(2)}, u32[]{:S(2)}) collective-permute-start(bf16[528,256]{1,0:T(8,128)(2,1)S(1)} %collective-permute-done.3.one), channel_id=1, source_target_pairs={{0,4},{1,3},{2,6},{3,1},{4,0},{5,7},{6,2},{7,5},{8,12},{9,11},{10,... | collective-permute-start | bytes 811016 | tf_op jit(solution)/shard_map/ppermute | solution.py:252
  25.7 6.3 %copy-start = (f32[4096,256]{1,0:T(8,128)S(1)}, f32[4096,256]{1,0:T(8,128)}, u32[]{:S(2)}) copy-start(f32[4096,256]{1,0:T(8,128)} %table_in.1) | copy-start | bytes 12582916
  25.7 6.3 %copy-start.2 = (f32[4096]{0:T(1024)S(1)}, f32[4096]{0:T(1024)}, u32[]{:S(2)}) copy-start(f32[4096]{0:T(1024)} %param.13) | copy-start | bytes 49156
  25.7 6.3 %copy-start.3 = (s32[1,16]{1,0:T(1,128)S(1)}, s32[1,16]{1,0:T(1,128)}, u32[]{:S(2)}) copy-start(s32[1,16]{1,0:T(1,128)} %blocks_ref.1) | copy-start | bytes 196
  30.4 1.5 %collective-permute-start.9 = (bf16[528,256]{1,0:T(8,128)(2,1)S(1)}, bf16[528,256]{1,0:T(8,128)(2,1)S(1)}, u32[]{:S(2)}, u32[]{:S(2)}) collective-permute-start(bf16[528,256]{1,0:T(8,128)(2,1)S(1)} %collective-permute-done.4.last_m), channel_id=1, source_target_pairs={{0,1},{1,0},{2,3},{3,2},{4,5},{5,4},{6,7},{7,6},{8,9},{9,8},{10,11... | collective-permute-start | bytes 811016 | tf_op jit(solution)/shard_map/ppermute | solution.py:252

commit v3 on v2

v3 whole, which is shorter than its diff:
```python
import functools

import jax
import jax.numpy as jnp
from jax import lax
from jax.experimental import pallas as pl
from jax.experimental.pallas import tpu as pltpu
from jax.sharding import PartitionSpec as P

TILE = 128
STAGE_MIB = 61
TAIL = 16
LEARNING_RATE = 0.5
EPSILON = 1e-06
VMEM = pltpu.VMEM
SMEM = pltpu.SMEM
F32 = jnp.float32
BF16 = jnp.bfloat16


def params(mib=24):
    return pltpu.CompilerParams(vmem_limit_bytes=mib * 2**20)


def whole(space=VMEM):
    return pl.BlockSpec(memory_space=space)


def pack_kernel(grad_ref, places_ref, *out_refs):
    owners = len(out_refs)
    cap = places_ref.shape[1]
    samples, cols = grad_ref.shape
    me = lax.axis_index("shard")
    lane = lax.broadcasted_iota(jnp.int32, (1, cap), 1)
    sub = lax.broadcasted_iota(jnp.int32, (samples, cap), 0)
    counts = places_ref[2 * owners : 2 * owners + 1, :]

    def picks(o):
        count = jnp.sum(jnp.where(lane == o, counts, 0), axis=1, keepdims=True)
        live = jnp.where(lane < count, places_ref[pl.ds(o, 1), :], -1)
        return (sub == live).astype(F32)

    total = picks(0)
    for o in range(1, owners):
        total = total + picks(o)
    lengths = jnp.sum(total, axis=1, keepdims=True)
    scaled = (grad_ref[...].astype(F32) * (1.0 / jnp.maximum(lengths, 1.0))).astype(BF16)
    tail_row = lax.broadcasted_iota(jnp.int32, (TAIL, cap), 0)
    for j in range(owners):
        o = me ^ j
        values = lax.dot_general(
            picks(o).astype(BF16), scaled, (((0,), (0,)), ((), ())), preferred_element_type=F32
        )
        out_refs[j][0:cap, :] = values.astype(BF16)
        row = places_ref[pl.ds(owners + o, 1), :]
        slot = row // TILE
        within = row - slot * TILE
        tail = jnp.where(tail_row == 0, slot, jnp.where(tail_row == 1, within, 0))
        out_refs[j][cap : cap + TAIL, :] = jnp.zeros((TAIL, cols), BF16)
        out_refs[j][cap : cap + TAIL, 0:cap] = tail.astype(F32).astype(BF16)


def pack(count, grad, sample, row):
    owners, cap = sample.shape
    counts = jnp.pad(count[None, :], ((0, 0), (0, cap - owners)))
    places = jnp.concatenate([sample, row, counts], axis=0)
    shape = jax.ShapeDtypeStruct((cap + TAIL, grad.shape[1]), BF16)
    return pl.pallas_call(
        pack_kernel,
        out_shape=[shape] * owners,
        in_specs=[whole(), whole()],
        out_specs=[whole()] * owners,
        compiler_params=params(),
    )(grad, places)


def tiny(cols):
    return pl.CostEstimate(flops=cols, bytes_accessed=cols, transcendentals=0)


def join_kernel(*refs):
    *payloads, out = refs
    cols = out.shape[1]
    sub = lax.broadcasted_iota(jnp.int32, (TAIL, cols), 0)
    tail = jnp.zeros((TAIL, cols), F32)
    at = 0
    for ref in payloads:
        rows = ref.shape[0] - TAIL
        out[at : at + rows, :] = ref[0:rows, :]
        own = ref[rows : rows + TAIL, :].astype(F32)
        for i in range(2 * (rows // TILE)):
            tail = jnp.where(sub == 2 * (at // TILE) + i, own[i : i + 1, :], tail)
        at += rows
    out[at : at + TAIL, :] = tail.astype(BF16)


def join(*payloads):
    cols = payloads[0].shape[1]
    rows = sum(p.shape[0] - TAIL for p in payloads) + TAIL
    return pl.pallas_call(
        join_kernel,
        out_shape=jax.ShapeDtypeStruct((rows, cols), BF16),
        in_specs=[whole()] * len(payloads),
        out_specs=whole(),
        compiler_params=params(),
        cost_estimate=tiny(cols),
    )(*payloads)


def positions(ref, cap):
    entries = ref.shape[0] - TAIL
    tail = ref[entries : entries + TAIL, 0:cap].astype(F32)
    n = entries // cap
    slot = jnp.concatenate([tail[2 * c : 2 * c + 1] for c in range(n)], axis=1)
    within = jnp.concatenate([tail[2 * c + 1 : 2 * c + 2] for c in range(n)], axis=1)
    return slot, within


def block_sum(ref, place, k):
    slot, within = place
    here = jnp.where(slot == k, within, -1.0).astype(BF16)
    entries = here.shape[1]
    sub = lax.broadcasted_iota(jnp.int32, (TILE, entries), 0).astype(F32).astype(BF16)
    pick = jnp.where(sub == here, jnp.ones((), BF16), jnp.zeros((), BF16))
    return jnp.dot(pick, ref[0:entries, :], preferred_element_type=F32)


def tile(ref, block):
    return ref.at[pl.ds(pl.multiple_of(block * TILE, TILE), TILE), :]


def stage_kernel(blocks_ref, table_in, table_ref, free_ref, bounce, into, out):
    n = blocks_ref.shape[1]
    tiles = table_in.shape[0] // TILE
    seen = jnp.int32(0)
    for t in range(tiles):
        free_ref[t - seen] = t
        seen = seen + (blocks_ref[0, jnp.minimum(seen, n - 1)] == t).astype(jnp.int32)
    loads, stores = [], []
    for i in range(tiles - n):
        here = bounce.at[i * TILE : (i + 1) * TILE, :]
        loads.append(pltpu.make_async_copy(tile(table_in, free_ref[i]), here, into.at[i]))
        stores.append(pltpu.make_async_copy(here, tile(table_ref, free_ref[i]), out.at[i]))
    for c in loads:
        c.start()
    for load, store in zip(loads, stores):
        load.wait()
        store.start()
    for c in stores:
        c.wait()


def stage(blocks, table):
    n = blocks.shape[1]
    tiles = table.shape[0] // TILE
    free = tiles - n
    return pl.pallas_call(
        stage_kernel,
        out_shape=jax.ShapeDtypeStruct(table.shape, F32),
        in_specs=[whole(SMEM), whole(pltpu.HBM)],
        out_specs=whole(pltpu.HBM),
        scratch_shapes=[
            SMEM((tiles + 1,), jnp.int32),
            VMEM((free * TILE, table.shape[1]), F32),
            pltpu.SemaphoreType.DMA((free,)),
            pltpu.SemaphoreType.DMA((free,)),
        ],
        compiler_params=params(STAGE_MIB),
        cost_estimate=pl.CostEstimate(
            flops=0, bytes_accessed=4 * table.size * 3, transcendentals=0
        ),
    )(blocks, table)


def own_kernel(cap, blocks_ref, own, accum_ref, part, old):
    place = positions(own, cap)
    for k in range(part.shape[0] // TILE):
        span = slice(k * TILE, (k + 1) * TILE)
        part[span, :] = block_sum(own, place, k)
        row = accum_ref[pl.ds(blocks_ref[0, k], 1), :]
        old[span, :] = jnp.broadcast_to(row, (TILE, TILE)).T


def own_sum(blocks, own, accum, span, cap):
    entries, cols = own.shape[0] - TAIL, own.shape[1]
    return pl.pallas_call(
        functools.partial(own_kernel, cap),
        out_shape=[
            jax.ShapeDtypeStruct((span, cols), F32),
            jax.ShapeDtypeStruct((span, TILE), F32),
        ],
        in_specs=[whole(SMEM), whole(), whole()],
        out_specs=[whole()] * 2,
        compiler_params=params(),
        cost_estimate=pl.CostEstimate(
            flops=2 * span * entries * cols, bytes_accessed=span * cols * 4, transcendentals=0
        ),
    )(blocks, own, accum)


def one_kernel(cap, payload, part):
    place = positions(payload, cap)
    for k in range(part.shape[0] // TILE):
        part[k * TILE : (k + 1) * TILE, :] = block_sum(payload, place, k)


def near_kernel(cap, one, two, part, near, side):
    places = [positions(ref, cap) for ref in (one, two)]
    for k in range(near.shape[0] // TILE):
        span = slice(k * TILE, (k + 1) * TILE)
        near[span, :] = part[span, :] + block_sum(one, places[0], k)
        side[span, :] = block_sum(two, places[1], k)


def rest_kernel(cap, diag, one_c, two_c, near, side, part_c, mine, near_c, side_c):
    places = [positions(ref, cap) for ref in (diag, one_c, two_c)]
    for k in range(near.shape[0] // TILE):
        span = slice(k * TILE, (k + 1) * TILE)
        mine[span, :] = near[span, :] + (side[span, :] + block_sum(diag, places[0], k))
        near_c[span, :] = part_c[span, :] + block_sum(one_c, places[1], k)
        side_c[span, :] = block_sum(two_c, places[2], k)


def sum_call(kernel, payloads, parts, results, span, cap):
    entries, cols = payloads[0].shape[0] - TAIL, payloads[0].shape[1]
    wide = jax.ShapeDtypeStruct((span, cols), F32)
    return pl.pallas_call(
        functools.partial(kernel, cap),
        out_shape=[wide] * results,
        in_specs=[whole()] * (len(payloads) + len(parts)),
        out_specs=[whole()] * results,
        compiler_params=params(),
        cost_estimate=pl.CostEstimate(
            flops=2 * span * entries * cols * len(payloads),
            bytes_accessed=span * cols * 4 * (results + len(parts)),
            transcendentals=0,
        ),
    )(*payloads, *parts)


def update_kernel(
    cap, blocks_ref, last, mine, near, side, old, table_in, accum_ref, alias,
    table_ref, accum_out, rows_out, accum_new, sem, sems,
):
    del alias
    n = rows_out.shape[0] // TILE
    cols = rows_out.shape[1]
    place = positions(last, cap)
    accum_new[...] = accum_ref[...]
    diagonal = lax.broadcasted_iota(jnp.int32, (TILE, TILE), 0) == lax.broadcasted_iota(
        jnp.int32, (TILE, TILE), 1
    )
    ones = jnp.ones((2 * cols, TILE), BF16)
    news = []
    copies = []
    for k in range(n):
        span = slice(k * TILE, (k + 1) * TILE)
        block = pl.multiple_of(blocks_ref[0, k] * TILE, TILE)
        other = near[span, :] + (side[span, :] + block_sum(last, place, k))
        grad = (mine[span, :] + other).astype(BF16).astype(F32)
        square = grad * grad
        high = square.astype(BF16)
        low = (square - high.astype(F32)).astype(BF16)
        total = jnp.dot(jnp.concatenate([high, low], axis=1), ones, preferred_element_type=F32)
        new = old[span, :] + total * (1.0 / cols)
        rate = LEARNING_RATE / (jnp.sqrt(new) + EPSILON)
        for c in range(0, cols, TILE):
            rows_out[span, c : c + TILE] = (
                table_in[pl.ds(block, TILE), c : c + TILE] - grad[:, c : c + TILE] * rate
            )
        news.append(jnp.sum(jnp.where(diagonal, new, 0.0), axis=0, keepdims=True))
        c = pltpu.make_async_copy(rows_out.at[span, :], tile(table_ref, blocks_ref[0, k]), sems.at[k])
        c.start()
        copies.append(c)
    for k in range(n):
        accum_new[pl.ds(blocks_ref[0, k], 1), :] = news[k]
    c = pltpu.make_async_copy(accum_new, accum_out, sem)
    c.start()
    for c in copies + [c]:
        c.wait()


def update(blocks, last, sums, old, table, accum, target, cap):
    n = blocks.shape[1]
    return pl.pallas_call(
        functools.partial(update_kernel, cap),
        out_shape=[
            jax.ShapeDtypeStruct(table.shape, F32),
            jax.ShapeDtypeStruct(accum.shape, F32),
        ],
        in_specs=[whole(SMEM)] + [whole()] * 7 + [whole(pltpu.HBM)],
        out_specs=[whole(pltpu.HBM), whole(pltpu.HBM)],
        scratch_shapes=[
            VMEM((n * TILE, table.shape[1]), F32),
            VMEM(accum.shape, F32),
            pltpu.SemaphoreType.DMA,
            pltpu.SemaphoreType.DMA((n,)),
        ],
        input_output_aliases={8: 0},
        compiler_params=params(),
    )(blocks, last, *sums, old, table, accum, target)


def after(x, *earlier):
    return lax.optimization_barrier((x,) + earlier)[0]


def gathered(pooled_grad, send_sample, send_row, send_count, union_blocks, table, accum):
    shards = lax.axis_size("shard")
    reps = lax.axis_size("rep")
    cap = send_sample.shape[1]
    span = union_blocks.shape[1] * TILE
    old_accum = accum.reshape(-1, TILE)

    def swap(x, flip):
        pairs = []
        for z in range(shards):
            for r in range(reps):
                dz, dr = flip(r)
                pairs.append((z * reps + r, (z ^ dz) * reps + (r ^ dr)))
        return lax.ppermute(x, ("shard", "rep"), pairs)

    def first(x):
        return swap(x, lambda r: (0, 2 if r % 2 == 0 else 4))

    def second(x):
        return swap(x, lambda r: (0, 4 if r % 2 == 0 else 2))

    def core(x):
        return swap(x, lambda r: (0, 1))

    mine = pack(send_count, pooled_grad, send_sample, send_row)
    target = stage(after(union_blocks, mine[0]), table)
    arrived = [swap(mine[j], lambda r: (j, 0)) for j in (3, 2, 1)]
    own = join(after(mine[0], target), *arrived)
    one = first(own)
    own_c = core(own)
    part, old = own_sum(union_blocks, own, old_accum, span, cap)
    two = second(after(own, part))
    (part_c,) = sum_call(one_kernel, [own_c], [], 1, span, cap)
    diag = second(after(one, part_c))
    near, side = sum_call(near_kernel, [one, two], [part], 2, span, cap)
    one_c, two_c = core(one), core(two)
    last = core(after(diag, near))
    mine, near_c, side_c = sum_call(
        rest_kernel, [diag, one_c, two_c], [near, side, part_c], 3, span, cap
    )
    table_out, accum_out = update(
        union_blocks, last, (mine, near_c, side_c), old, table, old_accum, target, cap
    )
    return table_out, accum_out.reshape(accum.shape)


def reduced(pooled_grad, send_sample, send_row, send_count, union_blocks, table, accum):
    columns = pooled_grad.shape[1]
    samples = pooled_grad.shape[0]
    active = (lax.broadcasted_iota(jnp.int32, send_sample.shape, 1) < send_count[:, None]).astype(F32)
    lengths = jax.ops.segment_sum(active.reshape(-1), send_sample.reshape(-1), num_segments=samples)
    scaled = active / jnp.maximum(lengths, 1.0)[send_sample]
    values = (pooled_grad[send_sample].astype(F32) * scaled[:, :, None]).astype(BF16)
    arrived = lax.all_to_all(values, "shard", split_axis=0, concat_axis=0, tiled=True)
    places = lax.all_to_all(send_row, "shard", split_axis=0, concat_axis=0, tiled=True)
    blocks = union_blocks[0]
    span = blocks.shape[0] * TILE
    local = (
        jnp.zeros((span, columns), F32)
        .at[places.reshape(-1)]
        .add(arrived.reshape(-1, columns).astype(F32))
    )
    table_tiles = table.reshape(-1, TILE, columns)
    accum_tiles = accum.reshape(-1, TILE)
    grad = lax.optimization_barrier(lax.psum(local.astype(BF16), "rep")).astype(F32)
    acc_new = accum_tiles[blocks].reshape(span) + jnp.mean(grad * grad, axis=-1)
    rows_new = table_tiles[blocks].reshape(span, columns) - LEARNING_RATE * grad / (
        jnp.sqrt(acc_new)[:, None] + EPSILON
    )
    table_out = table_tiles.at[blocks].set(rows_new.reshape(-1, TILE, columns)).reshape(table.shape)
    accum_out = accum_tiles.at[blocks].set(acc_new.reshape(-1, TILE)).reshape(accum.shape)
    return table_out, accum_out


def solution(mesh):
    both = ("shard", "rep")
    in_specs = (
        P(both, None),
        P(both, None),
        P(both, None),
        P(both),
        P("shard", None),
        P("shard", None),
        P("shard"),
    )
    out_specs = (P("shard", None), P("shard"))
    small = mesh.shape["shard"] == 4 and mesh.shape["rep"] == 8
    return jax.shard_map(
        gathered if small else reduced,
        mesh=mesh,
        in_specs=in_specs,
        out_specs=out_specs,
        check_vma=False,
    )
```

time: 36.4 us -> 34.6 us (0.951)
  waiting for transfers between devices: 12.6 us -> 6.77 us
  Pallas kernels: 9.44 us -> 13 us
  starting transfers between devices: 11 us -> 12.1 us
  other arithmetic: 1.44 us -> 0.72 us
    ppermute x10, waiting for transfers between devices: 12.6 us -> 6.77 us  [swap(): return lax.ppermute(x, ('shard', 'rep'), pairs)]
    pallas_call x4 -> x7, Pallas kernels: 5.25 us -> 9.43 us  [the longest x3 4.15 us: sum_call(): pl.pallas_call(functools.partial(kernel, cap), out_shape=[wide] * results...]
    ppermute x10, starting transfers between devices: 11 us -> 12.1 us  [swap(): return lax.ppermute(x, ('shard', 'rep'), pairs)]
    select_n x1 -> x0, other arithmetic: 0.75 us -> none  [pack(): places = jnp.concatenate([jnp.where(live, sample, -1), row], axis=0)]
    pallas_call x1, Pallas kernels: 4.19 us -> 3.57 us  [update(): pl.pallas_call(functools.partial(update_kernel, cap), out_shape=[jax.Shap...]
  transfers between devices with their start and end apart: 10 -> 10, of which waited for: 5 -> 3; matrix products, arithmetic and copies ran while one was open for 0% -> 0% of each run, Pallas kernels for 13% -> 26%
where the time goes in v3:
time: 34.6 us; the launch traced here: 34.3 us
  Pallas kernels  13 us (38%)
  starting transfers between devices  12.1 us (35%)
  waiting for transfers between devices  6.77 us (20%)
  local copies, waits for them, and re-layouts  0.97 us (3%)
  between operations  0.73 us (2%)
  other arithmetic  0.72 us (2%)
    ppermute x10, starting transfers between devices, swap(): return lax.ppermute(x, ('shard', 'rep'), pairs)  12.1 us
    ppermute x10, waiting for transfers between devices, swap(): return lax.ppermute(x, ('shard', 'rep'), pairs)  6.77 us
    pallas_call x3, Pallas kernels, sum_call(): pl.pallas_call(functools.partial(kernel, cap), out_shape=[wide] * results...  4.15 us
    pallas_call x1, Pallas kernels, stage(): pl.pallas_call(stage_kernel, out_shape=jax.ShapeDtypeStruct(table.shape,...  3.57 us
    pallas_call x1, Pallas kernels, update(): pl.pallas_call(functools.partial(update_kernel, cap), out_shape=[jax.Shap...  3.57 us
    pallas_call x1, Pallas kernels, own_sum(): pl.pallas_call(functools.partial(own_kernel, cap), out_shape=[jax.ShapeDt...  1.25 us
    unnamed x8, local copies, waits for them, and re-layouts  0.97 us
    concatenate x1, other arithmetic, pack(): places = jnp.concatenate([sample, row, counts], axis=0)  0.72 us
  transfers between devices with their start and end apart: 10, of which 3 were waited for; matrix products, arithmetic and copies ran while one was open for 0% of the time, Pallas kernels for 26%

profile of v3, /device:TPU:0, one launch (start us, length us, event | category | flops | bytes accessed | tf_op | source)
XLA Modules:
  0.0 34.3 jit_solution(10019912191465680329)
XLA Ops:
  0.6 0.7 %pad_add_fusion.places_ref = s32[9,128]{1,0:T(8,128)S(1)} fusion(s32[1,4]{1,0:T(1,128)} %bitcast.5, s32[4,128]{1,0:T(4,128)} %param.9, s32[4,128]{1,0:T(4,128)} %param.8), kind=kLoop, calls=%fused_computation | loop fusion | flops 2304 | bytes 8720 | tf_op jit(solution)/shard_map/concatenate | solution.py:66
  1.4 0.9 %copy-done.1 = bf16[256,256]{1,0:T(8,128)(2,1)S(1)} copy-done((bf16[256,256]{1,0:T(8,128)(2,1)S(1)}, bf16[256,256]{1,0:T(8,128)(2,1)}, u32[]{:S(2)}) %copy-start.1) | copy-done | bytes 131096
  2.3 0.4 %shard_map.86 = (bf16[144,256]{1,0:T(8,128)(2,1)S(1)}, bf16[144,256]{1,0:T(8,128)(2,1)S(1)}, bf16[144,256]{1,0:T(8,128)(2,1)S(1)}, bf16[144,256]{1,0:T(8,128)(2,1)S(1)}) custom-call(bf16[256,256]{1,0:T(8,128)(2,1)S(1)} %copy-done.1, s32[9,128]{1,0:T(8,128)S(1)} %pad_add_fusion.places_ref), custom_call_target="tpu_custom_call" | custom-call | tf_op jit(solution)/shard_map/pallas_call | solution.py:68
  2.7 5.1 %collective-permute-start = (bf16[144,256]{1,0:T(8,128)(2,1)S(1)}, bf16[144,256]{1,0:T(8,128)(2,1)S(1)}, u32[]{:S(2)}, u32[]{:S(2)}) collective-permute-start(bf16[144,256]{1,0:T(8,128)(2,1)S(1)} %get-tuple-element.23), channel_id=1, source_target_pairs={{0,24},{1,25},{2,26},{3,27},{4,28},{5,29},{6,30},{7,31},{8,16},{9,... | collective-permute-start | bytes 221192 | tf_op jit(solution)/shard_map/ppermute | solution.py:321
  7.8 0.0 collective-permute-start.1
  7.8 0.6 %collective-permute-start.2 = (bf16[144,256]{1,0:T(8,128)(2,1)S(1)}, bf16[144,256]{1,0:T(8,128)(2,1)S(1)}, u32[]{:S(2)}, u32[]{:S(2)}) collective-permute-start(bf16[144,256]{1,0:T(8,128)(2,1)S(1)} %get-tuple-element.25), channel_id=1, source_target_pairs={{0,8},{1,9},{2,10},{3,11},{4,12},{5,13},{6,14},{7,15},{8,0},{9,1},... | collective-permute-start | bytes 221192 | tf_op jit(solution)/shard_map/ppermute | solution.py:321
  8.5 3.6 %shard_map.87.alias = f32[4096,256]{1,0:T(8,128)} custom-call(s32[1,16]{1,0:T(1,128)} %blocks_ref.4, f32[4096,256]{1,0:T(8,128)} %table_in.3), custom_call_target="tpu_custom_call" | custom-call | bytes 12582912 | tf_op jit(solution)/shard_map/pallas_call | solution.py:157
  12.0 2.0 %collective-permute-done.1.refs_2_ = bf16[144,256]{1,0:T(8,128)(2,1)S(1)} collective-permute-done((bf16[144,256]{1,0:T(8,128)(2,1)S(1)}, bf16[144,256]{1,0:T(8,128)(2,1)S(1)}, u32[]{:S(2)}, u32[]{:S(2)}) %collective-permute-start.1) | collective-permute-done | bytes 73760 | tf_op jit(solution)/shard_map/ppermute | solution.py:321
  14.0 0.0 collective-permute-done.2.refs_3_
  14.1 0.1 collective-permute-start.4
  14.1 1.6 %collective-permute-start.3 = (bf16[528,256]{1,0:T(8,128)(2,1)S(1)}, bf16[528,256]{1,0:T(8,128)(2,1)S(1)}, u32[]{:S(2)}, u32[]{:S(2)}) collective-permute-start(bf16[528,256]{1,0:T(8,128)(2,1)S(1)} %shard_map.88.own), channel_id=1, source_target_pairs={{0,2},{1,5},{2,0},{3,7},{4,6},{5,1},{6,4},{7,3},{8,10},{9,13},{10,... | collective-permute-start | bytes 811016 | tf_op jit(solution)/shard_map/ppermute | solution.py:321
  15.7 1.3 %shard_map.90 = (f32[2048,256]{1,0:T(8,128)S(1)}, f32[2048,128]{1,0:T(8,128)S(1)}) custom-call(s32[1,16]{1,0:T(1,128)S(1)} %copy-done.3, bf16[528,256]{1,0:T(8,128)(2,1)S(1)} %shard_map.88.own, f32[32,128]{1,0:T(8,128)S(1)} %bitcast.3), custom_call_target="tpu_custom_call" | custom-call | flops 536870912 | bytes 2097152 | tf_op jit(solution)/shard_map/pallas_call | solution.py:186
  17.0 1.6 %collective-permute-start.6 = (bf16[528,256]{1,0:T(8,128)(2,1)S(1)}, bf16[528,256]{1,0:T(8,128)(2,1)S(1)}, u32[]{:S(2)}, u32[]{:S(2)}) collective-permute-start(bf16[528,256]{1,0:T(8,128)(2,1)S(1)} %shard_map.88.own), channel_id=1, source_target_pairs={{0,4},{1,3},{2,6},{3,1},{4,0},{5,7},{6,2},{7,5},{8,12},{9,11},{10,... | collective-permute-start | bytes 811016 | tf_op jit(solution)/shard_map/ppermute | solution.py:321
  18.5 0.0 collective-permute-done.4.payload
  18.6 0.7 %shard_map.89.part_c = f32[2048,256]{1,0:T(8,128)S(1)} custom-call(bf16[528,256]{1,0:T(8,128)(2,1)S(1)} %collective-permute-done.4.payload), custom_call_target="tpu_custom_call" | custom-call | flops 536870912 | bytes 2097152 | tf_op jit(solution)/shard_map/pallas_call | solution.py:227
  19.3 2.2 %collective-permute-done.3.one = bf16[528,256]{1,0:T(8,128)(2,1)S(1)} collective-permute-done((bf16[528,256]{1,0:T(8,128)(2,1)S(1)}, bf16[528,256]{1,0:T(8,128)(2,1)S(1)}, u32[]{:S(2)}, u32[]{:S(2)}) %collective-permute-start.3) | collective-permute-done | bytes 270368 | tf_op jit(solution)/shard_map/ppermute | solution.py:321
  21.5 2.6 %collective-permute-start.5 = (bf16[528,256]{1,0:T(8,128)(2,1)S(1)}, bf16[528,256]{1,0:T(8,128)(2,1)S(1)}, u32[]{:S(2)}, u32[]{:S(2)}) collective-permute-start(bf16[528,256]{1,0:T(8,128)(2,1)S(1)} %collective-permute-done.3.one), channel_id=1, source_target_pairs={{0,4},{1,3},{2,6},{3,1},{4,0},{5,7},{6,2},{7,5},{8,12},{9,11},{10,... | collective-permute-start | bytes 811016 | tf_op jit(solution)/shard_map/ppermute | solution.py:321
  24.1 0.5 %collective-permute-start.8 = (bf16[528,256]{1,0:T(8,128)(2,1)S(1)}, bf16[528,256]{1,0:T(8,128)(2,1)S(1)}, u32[]{:S(2)}, u32[]{:S(2)}) collective-permute-start(bf16[528,256]{1,0:T(8,128)(2,1)S(1)} %collective-permute-done.3.one), channel_id=1, source_target_pairs={{0,1},{1,0},{2,3},{3,2},{4,5},{5,4},{6,7},{7,6},{8,9},{9,8},{10,11... | collective-permute-start | bytes 811016 | tf_op jit(solution)/shard_map/ppermute | solution.py:321
  24.6 1.3 %shard_map.91 = (f32[2048,256]{1,0:T(8,128)S(1)}, f32[2048,256]{1,0:T(8,128)S(1)}) custom-call(bf16[528,256]{1,0:T(8,128)(2,1)S(1)} %collective-permute-done.3.one, bf16[528,256]{1,0:T(8,128)(2,1)S(1)} %collective-permute-done.6.two, f32[2048,256]{1,0:T(8,128)S(1)} %get-tuple-element.27.part), custom_call_target="tpu_custom_call" | custom-call | flops 1073741824 | bytes 6291456 | tf_op jit(solution)/shard_map/pallas_call | solution.py:227
  25.9 2.6 %collective-permute-done.5.diag = bf16[528,256]{1,0:T(8,128)(2,1)S(1)} collective-permute-done((bf16[528,256]{1,0:T(8,128)(2,1)S(1)}, bf16[528,256]{1,0:T(8,128)(2,1)S(1)}, u32[]{:S(2)}, u32[]{:S(2)}) %collective-permute-start.5) | collective-permute-done | bytes 270368 | tf_op jit(solution)/shard_map/ppermute | solution.py:321
  28.5 0.0 copy-start
  28.5 2.1 %shard_map.92 = (f32[2048,256]{1,0:T(8,128)S(1)}, f32[2048,256]{1,0:T(8,128)S(1)}, f32[2048,256]{1,0:T(8,128)S(1)}) custom-call(bf16[528,256]{1,0:T(8,128)(2,1)S(1)} %collective-permute-done.5.diag, bf16[528,256]{1,0:T(8,128)(2,1)S(1)} %collective-permute-done.8.one_c, bf16[528,256]{1,0:T(8,128)(2,1)S(1)} %collective-permute-done.9.two_c, ...), custom_call_target="tpu_custom_call" | custom-call | flops 1610612736 | bytes 12582912 | tf_op jit(solution)/shard_map/pallas_call | solution.py:227
  30.6 0.1 copy-done
  30.7 3.6 %shard_map.93 = (f32[4096,256]{1,0:T(8,128)}, f32[32,128]{1,0:T(8,128)}) custom-call(s32[1,16]{1,0:T(1,128)S(1)} %copy-done.3, bf16[528,256]{1,0:T(8,128)(2,1)S(1)} %collective-permute-done.7.last, f32[2048,256]{1,0:T(8,128)S(1)} %get-tuple-element.32.mine, f32[2048,256]{1,0:T(8,128)S(1)} %get-tuple-element.33.near, ...), custom_call_target="tpu_custom_call", output_to_operand_aliasing={{0}: (8, {})} | custom-call | tf_op jit(solution)/shard_map/pallas_call | solution.py:285
  (13 shorter events, 0.1 us)
Async XLA Ops:
  1.4 0.9 %copy-start.1 = (bf16[256,256]{1,0:T(8,128)(2,1)S(1)}, bf16[256,256]{1,0:T(8,128)(2,1)}, u32[]{:S(2)}) copy-start(bf16[256,256]{1,0:T(8,128)(2,1)} %grad_ref.1) | copy-start | bytes 393220
  2.7 9.3 %collective-permute-start = (bf16[144,256]{1,0:T(8,128)(2,1)S(1)}, bf16[144,256]{1,0:T(8,128)(2,1)S(1)}, u32[]{:S(2)}, u32[]{:S(2)}) collective-permute-start(bf16[144,256]{1,0:T(8,128)(2,1)S(1)} %get-tuple-element.23), channel_id=1, source_target_pairs={{0,24},{1,25},{2,26},{3,27},{4,28},{5,29},{6,30},{7,31},{8,16},{9,... | collective-permute-start | bytes 221192 | tf_op jit(solution)/shard_map/ppermute | solution.py:321
  7.8 6.2 %collective-permute-start.1 = (bf16[144,256]{1,0:T(8,128)(2,1)S(1)}, bf16[144,256]{1,0:T(8,128)(2,1)S(1)}, u32[]{:S(2)}, u32[]{:S(2)}) collective-permute-start(bf16[144,256]{1,0:T(8,128)(2,1)S(1)} %get-tuple-element.24), channel_id=1, source_target_pairs={{0,16},{1,17},{2,18},{3,19},{4,20},{5,21},{6,22},{7,23},{8,24},{9,... | collective-permute-start | bytes 221192 | tf_op jit(solution)/shard_map/ppermute | solution.py:321
  7.8 6.2 %collective-permute-start.2 = (bf16[144,256]{1,0:T(8,128)(2,1)S(1)}, bf16[144,256]{1,0:T(8,128)(2,1)S(1)}, u32[]{:S(2)}, u32[]{:S(2)}) collective-permute-start(bf16[144,256]{1,0:T(8,128)(2,1)S(1)} %get-tuple-element.25), channel_id=1, source_target_pairs={{0,8},{1,9},{2,10},{3,11},{4,12},{5,13},{6,14},{7,15},{8,0},{9,1},... | collective-permute-start | bytes 221192 | tf_op jit(solution)/shard_map/ppermute | solution.py:321
  8.5 7.2 %copy-start.2 = (f32[4096]{0:T(1024)S(1)}, f32[4096]{0:T(1024)}, u32[]{:S(2)}) copy-start(f32[4096]{0:T(1024)} %param.13) | copy-start | bytes 49156
  8.5 7.2 %copy-start.3 = (s32[1,16]{1,0:T(1,128)S(1)}, s32[1,16]{1,0:T(1,128)}, u32[]{:S(2)}) copy-start(s32[1,16]{1,0:T(1,128)} %blocks_ref.4) | copy-start | bytes 196
  14.1 4.5 %collective-permute-start.4 = (bf16[528,256]{1,0:T(8,128)(2,1)S(1)}, bf16[528,256]{1,0:T(8,128)(2,1)S(1)}, u32[]{:S(2)}, u32[]{:S(2)}) collective-permute-start(bf16[528,256]{1,0:T(8,128)(2,1)S(1)} %shard_map.88.own), channel_id=1, source_target_pairs={{0,1},{1,0},{2,3},{3,2},{4,5},{5,4},{6,7},{7,6},{8,9},{9,8},{10,11... | collective-permute-start | bytes 811016 | tf_op jit(solution)/shard_map/ppermute | solution.py:321
  14.1 7.3 %collective-permute-start.3 = (bf16[528,256]{1,0:T(8,128)(2,1)S(1)}, bf16[528,256]{1,0:T(8,128)(2,1)S(1)}, u32[]{:S(2)}, u32[]{:S(2)}) collective-permute-start(bf16[528,256]{1,0:T(8,128)(2,1)S(1)} %shard_map.88.own), channel_id=1, source_target_pairs={{0,2},{1,5},{2,0},{3,7},{4,6},{5,1},{6,4},{7,3},{8,10},{9,13},{10,... | collective-permute-start | bytes 811016 | tf_op jit(solution)/shard_map/ppermute | solution.py:321
  17.0 7.1 %collective-permute-start.6 = (bf16[528,256]{1,0:T(8,128)(2,1)S(1)}, bf16[528,256]{1,0:T(8,128)(2,1)S(1)}, u32[]{:S(2)}, u32[]{:S(2)}) collective-permute-start(bf16[528,256]{1,0:T(8,128)(2,1)S(1)} %shard_map.88.own), channel_id=1, source_target_pairs={{0,4},{1,3},{2,6},{3,1},{4,0},{5,7},{6,2},{7,5},{8,12},{9,11},{10,... | collective-permute-start | bytes 811016 | tf_op jit(solution)/shard_map/ppermute | solution.py:321
  21.5 7.0 %collective-permute-start.5 = (bf16[528,256]{1,0:T(8,128)(2,1)S(1)}, bf16[528,256]{1,0:T(8,128)(2,1)S(1)}, u32[]{:S(2)}, u32[]{:S(2)}) collective-permute-start(bf16[528,256]{1,0:T(8,128)(2,1)S(1)} %collective-permute-done.3.one), channel_id=1, source_target_pairs={{0,4},{1,3},{2,6},{3,1},{4,0},{5,7},{6,2},{7,5},{8,12},{9,11},{10,... | collective-permute-start | bytes 811016 | tf_op jit(solution)/shard_map/ppermute | solution.py:321
  24.1 4.4 %collective-permute-start.9 = (bf16[528,256]{1,0:T(8,128)(2,1)S(1)}, bf16[528,256]{1,0:T(8,128)(2,1)S(1)}, u32[]{:S(2)}, u32[]{:S(2)}) collective-permute-start(bf16[528,256]{1,0:T(8,128)(2,1)S(1)} %collective-permute-done.6.two), channel_id=1, source_target_pairs={{0,1},{1,0},{2,3},{3,2},{4,5},{5,4},{6,7},{7,6},{8,9},{9,8},{10,11... | collective-permute-start | bytes 811016 | tf_op jit(solution)/shard_map/ppermute | solution.py:321
  24.1 4.4 %collective-permute-start.8 = (bf16[528,256]{1,0:T(8,128)(2,1)S(1)}, bf16[528,256]{1,0:T(8,128)(2,1)S(1)}, u32[]{:S(2)}, u32[]{:S(2)}) collective-permute-start(bf16[528,256]{1,0:T(8,128)(2,1)S(1)} %collective-permute-done.3.one), channel_id=1, source_target_pairs={{0,1},{1,0},{2,3},{3,2},{4,5},{5,4},{6,7},{7,6},{8,9},{9,8},{10,11... | collective-permute-start | bytes 811016 | tf_op jit(solution)/shard_map/ppermute | solution.py:321
  28.5 2.1 %collective-permute-start.7 = (bf16[528,256]{1,0:T(8,128)(2,1)S(1)}, bf16[528,256]{1,0:T(8,128)(2,1)S(1)}, u32[]{:S(2)}, u32[]{:S(2)}) collective-permute-start(bf16[528,256]{1,0:T(8,128)(2,1)S(1)} %collective-permute-done.5.diag), channel_id=1, source_target_pairs={{0,1},{1,0},{2,3},{3,2},{4,5},{5,4},{6,7},{7,6},{8,9},{9,8},{10,11... | collective-permute-start | bytes 811016 | tf_op jit(solution)/shard_map/ppermute | solution.py:321
  28.5 2.2 %copy-start = (f32[4096,256]{1,0:T(8,128)S(1)}, f32[4096,256]{1,0:T(8,128)}, u32[]{:S(2)}) copy-start(f32[4096,256]{1,0:T(8,128)} %table_in.3) | copy-start | bytes 12582916

commit v4 on v3

--- a/solution.py
+++ b/solution.py
@@ -9,6 +9,7 @@
 
 TILE = 128
 STAGE_MIB = 61
+PACK_BYTES = 60 * 1024 * 1024
 TAIL = 16
 LEARNING_RATE = 0.5
 EPSILON = 1e-06
@@ -26,25 +27,41 @@
     return pl.BlockSpec(memory_space=space)
 
 
-def pack_kernel(grad_ref, places_ref, *out_refs):
+def pack_kernel(count_in, grad_in, sample_in, row_in, *refs):
+    *out_refs, count_ref, grad_ref, sample_ref, row_ref, sems = refs
+    copies = [
+        pltpu.make_async_copy(src, dst, sems.at[i])
+        for i, (src, dst) in enumerate(
+            (
+                (sample_in, sample_ref),
+                (count_in, count_ref),
+                (grad_in, grad_ref),
+                (row_in, row_ref),
+            )
+        )
+    ]
+    for c in copies:
+        c.start()
     owners = len(out_refs)
-    cap = places_ref.shape[1]
+    cap = sample_ref.shape[1]
     samples, cols = grad_ref.shape
     me = lax.axis_index("shard")
     lane = lax.broadcasted_iota(jnp.int32, (1, cap), 1)
     sub = lax.broadcasted_iota(jnp.int32, (samples, cap), 0)
-    counts = places_ref[2 * owners : 2 * owners + 1, :]
 
     def picks(o):
-        count = jnp.sum(jnp.where(lane == o, counts, 0), axis=1, keepdims=True)
-        live = jnp.where(lane < count, places_ref[pl.ds(o, 1), :], -1)
+        live = jnp.where(lane < count_ref[o], sample_ref[pl.ds(o, 1), :], -1)
         return (sub == live).astype(F32)
 
+    copies[0].wait()
+    copies[1].wait()
     total = picks(0)
     for o in range(1, owners):
         total = total + picks(o)
     lengths = jnp.sum(total, axis=1, keepdims=True)
+    copies[2].wait()
     scaled = (grad_ref[...].astype(F32) * (1.0 / jnp.maximum(lengths, 1.0))).astype(BF16)
+    copies[3].wait()
     tail_row = lax.broadcasted_iota(jnp.int32, (TAIL, cap), 0)
     for j in range(owners):
         o = me ^ j
@@ -52,7 +69,7 @@
             picks(o).astype(BF16), scaled, (((0,), (0,)), ((), ())), preferred_element_type=F32
         )
         out_refs[j][0:cap, :] = values.astype(BF16)
-        row = places_ref[pl.ds(owners + o, 1), :]
+        row = row_ref[pl.ds(o, 1), :]
         slot = row // TILE
         within = row - slot * TILE
         tail = jnp.where(tail_row == 0, slot, jnp.where(tail_row == 1, within, 0))
@@ -62,16 +79,21 @@
 
 def pack(count, grad, sample, row):
     owners, cap = sample.shape
-    counts = jnp.pad(count[None, :], ((0, 0), (0, cap - owners)))
-    places = jnp.concatenate([sample, row, counts], axis=0)
-    shape = jax.ShapeDtypeStruct((cap + TAIL, grad.shape[1]), BF16)
+    shape = VMEM((cap + TAIL, grad.shape[1]), BF16)
     return pl.pallas_call(
         pack_kernel,
         out_shape=[shape] * owners,
-        in_specs=[whole(), whole()],
+        in_specs=[whole(pltpu.HBM)] * 4,
         out_specs=[whole()] * owners,
-        compiler_params=params(),
-    )(grad, places)
+        scratch_shapes=[
+            SMEM(count.shape, jnp.int32),
+            VMEM(grad.shape, BF16),
+            VMEM(sample.shape, jnp.int32),
+            VMEM(row.shape, jnp.int32),
+            pltpu.SemaphoreType.DMA((4,)),
+        ],
+        compiler_params=pltpu.CompilerParams(vmem_limit_bytes=PACK_BYTES),
+    )(count, grad, sample, row)
 
 
 def tiny(cols):
@@ -336,9 +358,9 @@
     one = first(own)
     own_c = core(own)
     part, old = own_sum(union_blocks, own, old_accum, span, cap)
-    two = second(after(own, part))
     (part_c,) = sum_call(one_kernel, [own_c], [], 1, span, cap)
-    diag = second(after(one, part_c))
+    two = second(after(own, part, part_c))
+    diag = second(one)
     near, side = sum_call(near_kernel, [one, two], [part], 2, span, cap)
     one_c, two_c = core(one), core(two)
     last = core(after(diag, near))

time: 34.6 us -> 33 us (0.954)
  local copies, waits for them, and re-layouts: 0.97 us -> 0.17 us
  other arithmetic: 0.72 us -> 0 us
  Pallas kernels: 13 us -> 13.7 us
  starting transfers between devices: 12.1 us -> 11.5 us
    pallas_call x1, Pallas kernels: 0.43 us -> 1.28 us  [pack(): pl.pallas_call(pack_kernel, out_shape=[shape] * owners, in_specs=[whole(p...]
    unnamed x8 -> x6, local copies, waits for them, and re-layouts: 0.97 us -> 0.17 us
    concatenate x1 -> x0, other arithmetic: 0.72 us -> none  [pack(): places = jnp.concatenate([sample, row, counts], axis=0)]
    ppermute x10, starting transfers between devices: 12.1 us -> 11.5 us  [swap(): return lax.ppermute(x, ('shard', 'rep'), pairs)]
  transfers between devices with their start and end apart: 10 -> 10, of which waited for: 3 -> 4; matrix products, arithmetic and copies ran while one was open for 0% -> 0% of each run, Pallas kernels for 26% -> 27%
where the time goes in v4:
time: 33 us; the launch traced here: 32.7 us
  Pallas kernels  13.7 us (42%)
  starting transfers between devices  11.5 us (35%)
  waiting for transfers between devices  6.63 us (20%)
  between operations  0.73 us (2%)
    ppermute x10, starting transfers between devices, swap(): return lax.ppermute(x, ('shard', 'rep'), pairs)  11.5 us
    ppermute x10, waiting for transfers between devices, swap(): return lax.ppermute(x, ('shard', 'rep'), pairs)  6.63 us
    pallas_call x3, Pallas kernels, sum_call(): pl.pallas_call(functools.partial(kernel, cap), out_shape=[wide] * results...  3.97 us
    pallas_call x1, Pallas kernels, stage(): pl.pallas_call(stage_kernel, out_shape=jax.ShapeDtypeStruct(table.shape,...  3.57 us
    pallas_call x1, Pallas kernels, update(): pl.pallas_call(functools.partial(update_kernel, cap), out_shape=[jax.Shap...  3.57 us
    pallas_call x1, Pallas kernels, pack(): pl.pallas_call(pack_kernel, out_shape=[shape] * owners, in_specs=[whole(p...  1.28 us
    pallas_call x1, Pallas kernels, own_sum(): pl.pallas_call(functools.partial(own_kernel, cap), out_shape=[jax.ShapeDt...  1.25 us
  transfers between devices with their start and end apart: 10, of which 4 were waited for; matrix products, arithmetic and copies ran while one was open for 0% of the time, Pallas kernels for 27%

profile of v4, /device:TPU:0, one launch (start us, length us, event | category | flops | bytes accessed | tf_op | source)
XLA Modules:
  0.0 32.7 jit_solution(49833907853958361)
XLA Ops:
  0.6 1.3 %shard_map.86 = (bf16[144,256]{1,0:T(8,128)(2,1)S(1)}, bf16[144,256]{1,0:T(8,128)(2,1)S(1)}, bf16[144,256]{1,0:T(8,128)(2,1)S(1)}, bf16[144,256]{1,0:T(8,128)(2,1)S(1)}) custom-call(s32[4]{0:T(128)} %count_in.1, bf16[256,256]{1,0:T(8,128)(2,1)} %grad_in.1, s32[4,128]{1,0:T(4,128)} %sample_in.1, s32[4,128]{1,0:T(4,128)} %row_in.1), custom_call_target="tpu_custom_call" | custom-call | tf_op jit(solution)/shard_map/pallas_call | solution.py:83
  1.9 5.1 %collective-permute-start = (bf16[144,256]{1,0:T(8,128)(2,1)S(1)}, bf16[144,256]{1,0:T(8,128)(2,1)S(1)}, u32[]{:S(2)}, u32[]{:S(2)}) collective-permute-start(bf16[144,256]{1,0:T(8,128)(2,1)S(1)} %get-tuple-element.22), channel_id=1, source_target_pairs={{0,24},{1,25},{2,26},{3,27},{4,28},{5,29},{6,30},{7,31},{8,16},{9,... | collective-permute-start | bytes 221192 | tf_op jit(solution)/shard_map/ppermute | solution.py:343
  7.0 0.6 %collective-permute-start.2 = (bf16[144,256]{1,0:T(8,128)(2,1)S(1)}, bf16[144,256]{1,0:T(8,128)(2,1)S(1)}, u32[]{:S(2)}, u32[]{:S(2)}) collective-permute-start(bf16[144,256]{1,0:T(8,128)(2,1)S(1)} %get-tuple-element.24), channel_id=1, source_target_pairs={{0,8},{1,9},{2,10},{3,11},{4,12},{5,13},{6,14},{7,15},{8,0},{9,1},... | collective-permute-start | bytes 221192 | tf_op jit(solution)/shard_map/ppermute | solution.py:343
  7.7 3.6 %shard_map.87.alias = f32[4096,256]{1,0:T(8,128)} custom-call(s32[1,16]{1,0:T(1,128)} %blocks_ref.4, f32[4096,256]{1,0:T(8,128)} %table_in.3), custom_call_target="tpu_custom_call" | custom-call | bytes 12582912 | tf_op jit(solution)/shard_map/pallas_call | solution.py:179
  11.3 0.0 collective-permute-done.refs_1_
  11.3 2.0 %collective-permute-done.1.refs_2_ = bf16[144,256]{1,0:T(8,128)(2,1)S(1)} collective-permute-done((bf16[144,256]{1,0:T(8,128)(2,1)S(1)}, bf16[144,256]{1,0:T(8,128)(2,1)S(1)}, u32[]{:S(2)}, u32[]{:S(2)}) %collective-permute-start.1) | collective-permute-done | bytes 73760 | tf_op jit(solution)/shard_map/ppermute | solution.py:343
  13.3 0.1 collective-permute-start.5
  13.4 1.6 %collective-permute-start.3 = (bf16[528,256]{1,0:T(8,128)(2,1)S(1)}, bf16[528,256]{1,0:T(8,128)(2,1)S(1)}, u32[]{:S(2)}, u32[]{:S(2)}) collective-permute-start(bf16[528,256]{1,0:T(8,128)(2,1)S(1)} %shard_map.88.own), channel_id=1, source_target_pairs={{0,2},{1,5},{2,0},{3,7},{4,6},{5,1},{6,4},{7,3},{8,10},{9,13},{10,... | collective-permute-start | bytes 811016 | tf_op jit(solution)/shard_map/ppermute | solution.py:343
  14.9 1.3 %shard_map.89 = (f32[2048,256]{1,0:T(8,128)S(1)}, f32[2048,128]{1,0:T(8,128)S(1)}) custom-call(s32[1,16]{1,0:T(1,128)S(1)} %copy-done.2, bf16[528,256]{1,0:T(8,128)(2,1)S(1)} %shard_map.88.own, f32[32,128]{1,0:T(8,128)S(1)} %bitcast.2), custom_call_target="tpu_custom_call" | custom-call | flops 536870912 | bytes 2097152 | tf_op jit(solution)/shard_map/pallas_call | solution.py:208
  16.2 0.7 %shard_map.90.part_c = f32[2048,256]{1,0:T(8,128)S(1)} custom-call(bf16[528,256]{1,0:T(8,128)(2,1)S(1)} %collective-permute-done.5.payload), custom_call_target="tpu_custom_call" | custom-call | flops 536870912 | bytes 2097152 | tf_op jit(solution)/shard_map/pallas_call | solution.py:249
  16.9 1.6 %collective-permute-start.6 = (bf16[528,256]{1,0:T(8,128)(2,1)S(1)}, bf16[528,256]{1,0:T(8,128)(2,1)S(1)}, u32[]{:S(2)}, u32[]{:S(2)}) collective-permute-start(bf16[528,256]{1,0:T(8,128)(2,1)S(1)} %shard_map.88.own), channel_id=1, source_target_pairs={{0,4},{1,3},{2,6},{3,1},{4,0},{5,7},{6,2},{7,5},{8,12},{9,11},{10,... | collective-permute-start | bytes 811016 | tf_op jit(solution)/shard_map/ppermute | solution.py:343
  18.5 1.5 %collective-permute-done.3.one = bf16[528,256]{1,0:T(8,128)(2,1)S(1)} collective-permute-done((bf16[528,256]{1,0:T(8,128)(2,1)S(1)}, bf16[528,256]{1,0:T(8,128)(2,1)S(1)}, u32[]{:S(2)}, u32[]{:S(2)}) %collective-permute-start.3) | collective-permute-done | bytes 270368 | tf_op jit(solution)/shard_map/ppermute | solution.py:343
  20.0 2.5 %collective-permute-start.4 = (bf16[528,256]{1,0:T(8,128)(2,1)S(1)}, bf16[528,256]{1,0:T(8,128)(2,1)S(1)}, u32[]{:S(2)}, u32[]{:S(2)}) collective-permute-start(bf16[528,256]{1,0:T(8,128)(2,1)S(1)} %collective-permute-done.3.one), channel_id=1, source_target_pairs={{0,4},{1,3},{2,6},{3,1},{4,0},{5,7},{6,2},{7,5},{8,12},{9,11},{10,... | collective-permute-start | bytes 811016 | tf_op jit(solution)/shard_map/ppermute | solution.py:343
  22.5 1.0 %collective-permute-done.6.two = bf16[528,256]{1,0:T(8,128)(2,1)S(1)} collective-permute-done((bf16[528,256]{1,0:T(8,128)(2,1)S(1)}, bf16[528,256]{1,0:T(8,128)(2,1)S(1)}, u32[]{:S(2)}, u32[]{:S(2)}) %collective-permute-start.6) | collective-permute-done | bytes 270368 | tf_op jit(solution)/shard_map/ppermute | solution.py:343
  23.4 0.0 collective-permute-start.9
  23.4 1.3 %shard_map.91 = (f32[2048,256]{1,0:T(8,128)S(1)}, f32[2048,256]{1,0:T(8,128)S(1)}) custom-call(bf16[528,256]{1,0:T(8,128)(2,1)S(1)} %collective-permute-done.3.one, bf16[528,256]{1,0:T(8,128)(2,1)S(1)} %collective-permute-done.6.two, f32[2048,256]{1,0:T(8,128)S(1)} %get-tuple-element.25.part), custom_call_target="tpu_custom_call" | custom-call | flops 1073741824 | bytes 6291456 | tf_op jit(solution)/shard_map/pallas_call | solution.py:249
  24.7 2.2 %collective-permute-done.4.diag = bf16[528,256]{1,0:T(8,128)(2,1)S(1)} collective-permute-done((bf16[528,256]{1,0:T(8,128)(2,1)S(1)}, bf16[528,256]{1,0:T(8,128)(2,1)S(1)}, u32[]{:S(2)}, u32[]{:S(2)}) %collective-permute-start.4) | collective-permute-done | bytes 270368 | tf_op jit(solution)/shard_map/ppermute | solution.py:343
  26.9 0.0 collective-permute-start.7
  26.9 0.0 collective-permute-done.8.one_c
  26.9 0.0 collective-permute-done.9.two_c
  26.9 0.0 copy-start
  26.9 2.0 %shard_map.92 = (f32[2048,256]{1,0:T(8,128)S(1)}, f32[2048,256]{1,0:T(8,128)S(1)}, f32[2048,256]{1,0:T(8,128)S(1)}) custom-call(bf16[528,256]{1,0:T(8,128)(2,1)S(1)} %collective-permute-done.4.diag, bf16[528,256]{1,0:T(8,128)(2,1)S(1)} %collective-permute-done.8.one_c, bf16[528,256]{1,0:T(8,128)(2,1)S(1)} %collective-permute-done.9.two_c, ...), custom_call_target="tpu_custom_call" | custom-call | flops 1610612736 | bytes 12582912 | tf_op jit(solution)/shard_map/pallas_call | solution.py:249
  29.0 0.2 copy-done
  29.1 3.6 %shard_map.93 = (f32[4096,256]{1,0:T(8,128)}, f32[32,128]{1,0:T(8,128)}) custom-call(s32[1,16]{1,0:T(1,128)S(1)} %copy-done.2, bf16[528,256]{1,0:T(8,128)(2,1)S(1)} %collective-permute-done.7.last, f32[2048,256]{1,0:T(8,128)S(1)} %get-tuple-element.30.mine, f32[2048,256]{1,0:T(8,128)S(1)} %get-tuple-element.31.near, ...), custom_call_target="tpu_custom_call", output_to_operand_aliasing={{0}: (8, {})} | custom-call | tf_op jit(solution)/shard_map/pallas_call | solution.py:307
  (10 shorter events, 0.0 us)
Async XLA Ops:
  1.9 9.3 %collective-permute-start = (bf16[144,256]{1,0:T(8,128)(2,1)S(1)}, bf16[144,256]{1,0:T(8,128)(2,1)S(1)}, u32[]{:S(2)}, u32[]{:S(2)}) collective-permute-start(bf16[144,256]{1,0:T(8,128)(2,1)S(1)} %get-tuple-element.22), channel_id=1, source_target_pairs={{0,24},{1,25},{2,26},{3,27},{4,28},{5,29},{6,30},{7,31},{8,16},{9,... | collective-permute-start | bytes 221192 | tf_op jit(solution)/shard_map/ppermute | solution.py:343
  7.0 6.2 %collective-permute-start.1 = (bf16[144,256]{1,0:T(8,128)(2,1)S(1)}, bf16[144,256]{1,0:T(8,128)(2,1)S(1)}, u32[]{:S(2)}, u32[]{:S(2)}) collective-permute-start(bf16[144,256]{1,0:T(8,128)(2,1)S(1)} %get-tuple-element.23), channel_id=1, source_target_pairs={{0,16},{1,17},{2,18},{3,19},{4,20},{5,21},{6,22},{7,23},{8,24},{9,... | collective-permute-start | bytes 221192 | tf_op jit(solution)/shard_map/ppermute | solution.py:343
  7.0 6.2 %collective-permute-start.2 = (bf16[144,256]{1,0:T(8,128)(2,1)S(1)}, bf16[144,256]{1,0:T(8,128)(2,1)S(1)}, u32[]{:S(2)}, u32[]{:S(2)}) collective-permute-start(bf16[144,256]{1,0:T(8,128)(2,1)S(1)} %get-tuple-element.24), channel_id=1, source_target_pairs={{0,8},{1,9},{2,10},{3,11},{4,12},{5,13},{6,14},{7,15},{8,0},{9,1},... | collective-permute-start | bytes 221192 | tf_op jit(solution)/shard_map/ppermute | solution.py:343
  7.7 7.2 %copy-start.1 = (f32[4096]{0:T(1024)S(1)}, f32[4096]{0:T(1024)}, u32[]{:S(2)}) copy-start(f32[4096]{0:T(1024)} %param.13) | copy-start | bytes 49156
  7.7 7.2 %copy-start.2 = (s32[1,16]{1,0:T(1,128)S(1)}, s32[1,16]{1,0:T(1,128)}, u32[]{:S(2)}) copy-start(s32[1,16]{1,0:T(1,128)} %blocks_ref.4) | copy-start | bytes 196
  13.3 2.9 %collective-permute-start.5 = (bf16[528,256]{1,0:T(8,128)(2,1)S(1)}, bf16[528,256]{1,0:T(8,128)(2,1)S(1)}, u32[]{:S(2)}, u32[]{:S(2)}) collective-permute-start(bf16[528,256]{1,0:T(8,128)(2,1)S(1)} %shard_map.88.own), channel_id=1, source_target_pairs={{0,1},{1,0},{2,3},{3,2},{4,5},{5,4},{6,7},{7,6},{8,9},{9,8},{10,11... | collective-permute-start | bytes 811016 | tf_op jit(solution)/shard_map/ppermute | solution.py:343
  13.4 6.6 %collective-permute-start.3 = (bf16[528,256]{1,0:T(8,128)(2,1)S(1)}, bf16[528,256]{1,0:T(8,128)(2,1)S(1)}, u32[]{:S(2)}, u32[]{:S(2)}) collective-permute-start(bf16[528,256]{1,0:T(8,128)(2,1)S(1)} %shard_map.88.own), channel_id=1, source_target_pairs={{0,2},{1,5},{2,0},{3,7},{4,6},{5,1},{6,4},{7,3},{8,10},{9,13},{10,... | collective-permute-start | bytes 811016 | tf_op jit(solution)/shard_map/ppermute | solution.py:343
  16.9 6.5 %collective-permute-start.6 = (bf16[528,256]{1,0:T(8,128)(2,1)S(1)}, bf16[528,256]{1,0:T(8,128)(2,1)S(1)}, u32[]{:S(2)}, u32[]{:S(2)}) collective-permute-start(bf16[528,256]{1,0:T(8,128)(2,1)S(1)} %shard_map.88.own), channel_id=1, source_target_pairs={{0,4},{1,3},{2,6},{3,1},{4,0},{5,7},{6,2},{7,5},{8,12},{9,11},{10,... | collective-permute-start | bytes 811016 | tf_op jit(solution)/shard_map/ppermute | solution.py:343
  20.0 6.9 %collective-permute-start.4 = (bf16[528,256]{1,0:T(8,128)(2,1)S(1)}, bf16[528,256]{1,0:T(8,128)(2,1)S(1)}, u32[]{:S(2)}, u32[]{:S(2)}) collective-permute-start(bf16[528,256]{1,0:T(8,128)(2,1)S(1)} %collective-permute-done.3.one), channel_id=1, source_target_pairs={{0,4},{1,3},{2,6},{3,1},{4,0},{5,7},{6,2},{7,5},{8,12},{9,11},{10,... | collective-permute-start | bytes 811016 | tf_op jit(solution)/shard_map/ppermute | solution.py:343
  22.5 4.4 %collective-permute-start.8 = (bf16[528,256]{1,0:T(8,128)(2,1)S(1)}, bf16[528,256]{1,0:T(8,128)(2,1)S(1)}, u32[]{:S(2)}, u32[]{:S(2)}) collective-permute-start(bf16[528,256]{1,0:T(8,128)(2,1)S(1)} %collective-permute-done.3.one), channel_id=1, source_target_pairs={{0,1},{1,0},{2,3},{3,2},{4,5},{5,4},{6,7},{7,6},{8,9},{9,8},{10,11... | collective-permute-start | bytes 811016 | tf_op jit(solution)/shard_map/ppermute | solution.py:343
  23.4 3.5 %collective-permute-start.9 = (bf16[528,256]{1,0:T(8,128)(2,1)S(1)}, bf16[528,256]{1,0:T(8,128)(2,1)S(1)}, u32[]{:S(2)}, u32[]{:S(2)}) collective-permute-start(bf16[528,256]{1,0:T(8,128)(2,1)S(1)} %collective-permute-done.6.two), channel_id=1, source_target_pairs={{0,1},{1,0},{2,3},{3,2},{4,5},{5,4},{6,7},{7,6},{8,9},{9,8},{10,11... | collective-permute-start | bytes 811016 | tf_op jit(solution)/shard_map/ppermute | solution.py:343
  26.9 2.0 %collective-permute-start.7 = (bf16[528,256]{1,0:T(8,128)(2,1)S(1)}, bf16[528,256]{1,0:T(8,128)(2,1)S(1)}, u32[]{:S(2)}, u32[]{:S(2)}) collective-permute-start(bf16[528,256]{1,0:T(8,128)(2,1)S(1)} %collective-permute-done.4.diag), channel_id=1, source_target_pairs={{0,1},{1,0},{2,3},{3,2},{4,5},{5,4},{6,7},{7,6},{8,9},{9,8},{10,11... | collective-permute-start | bytes 811016 | tf_op jit(solution)/shard_map/ppermute | solution.py:343
  26.9 2.2 %copy-start = (f32[4096,256]{1,0:T(8,128)S(1)}, f32[4096,256]{1,0:T(8,128)}, u32[]{:S(2)}) copy-start(f32[4096,256]{1,0:T(8,128)} %table_in.3) | copy-start | bytes 12582916

commit v5 on v4

--- a/solution.py
+++ b/solution.py
@@ -8,7 +8,7 @@
 from jax.sharding import PartitionSpec as P
 
 TILE = 128
-STAGE_MIB = 61
+LOAD_MIB = 56
 PACK_BYTES = 60 * 1024 * 1024
 TAIL = 16
 LEARNING_RATE = 0.5
@@ -151,87 +151,77 @@
     return ref.at[pl.ds(pl.multiple_of(block * TILE, TILE), TILE), :]
 
 
-def stage_kernel(blocks_ref, table_in, table_ref, free_ref, bounce, into, out):
-    n = blocks_ref.shape[1]
-    tiles = table_in.shape[0] // TILE
+def load_kernel(table_in, table_out, sem):
+    c = pltpu.make_async_copy(table_in, table_out, sem)
+    c.start()
+    c.wait()
+
+
+def load(table):
+    return pl.pallas_call(
+        load_kernel,
+        out_shape=VMEM(table.shape, F32),
+        in_specs=[whole(pltpu.HBM)],
+        out_specs=whole(),
+        scratch_shapes=[pltpu.SemaphoreType.DMA],
+        compiler_params=params(LOAD_MIB),
+        cost_estimate=pl.CostEstimate(
+            flops=0, bytes_accessed=4 * table.size * 3, transcendentals=0
+        ),
+    )(table)
+
+
+def own_kernel(cap, blocks_ref, own, accum_ref, table_in, part, old, table_ref, free_ref, sems):
+    n = part.shape[0] // TILE
+    tiles = accum_ref.shape[0]
     seen = jnp.int32(0)
     for t in range(tiles):
         free_ref[t - seen] = t
         seen = seen + (blocks_ref[0, jnp.minimum(seen, n - 1)] == t).astype(jnp.int32)
-    loads, stores = [], []
-    for i in range(tiles - n):
-        here = bounce.at[i * TILE : (i + 1) * TILE, :]
-        loads.append(pltpu.make_async_copy(tile(table_in, free_ref[i]), here, into.at[i]))
-        stores.append(pltpu.make_async_copy(here, tile(table_ref, free_ref[i]), out.at[i]))
-    for c in loads:
+    copies = [
+        pltpu.make_async_copy(tile(table_in, free_ref[i]), tile(table_ref, free_ref[i]), sems.at[i])
+        for i in range(tiles - n)
+    ]
+    for c in copies:
         c.start()
-    for load, store in zip(loads, stores):
-        load.wait()
-        store.start()
-    for c in stores:
-        c.wait()
-
-
-def stage(blocks, table):
-    n = blocks.shape[1]
-    tiles = table.shape[0] // TILE
-    free = tiles - n
-    return pl.pallas_call(
-        stage_kernel,
-        out_shape=jax.ShapeDtypeStruct(table.shape, F32),
-        in_specs=[whole(SMEM), whole(pltpu.HBM)],
-        out_specs=whole(pltpu.HBM),
-        scratch_shapes=[
-            SMEM((tiles + 1,), jnp.int32),
-            VMEM((free * TILE, table.shape[1]), F32),
-            pltpu.SemaphoreType.DMA((free,)),
-            pltpu.SemaphoreType.DMA((free,)),
-        ],
-        compiler_params=params(STAGE_MIB),
-        cost_estimate=pl.CostEstimate(
-            flops=0, bytes_accessed=4 * table.size * 3, transcendentals=0
-        ),
-    )(blocks, table)
-
-
-def own_kernel(cap, blocks_ref, own, accum_ref, part, old):
     place = positions(own, cap)
-    for k in range(part.shape[0] // TILE):
+    for k in range(n):
         span = slice(k * TILE, (k + 1) * TILE)
         part[span, :] = block_sum(own, place, k)
         row = accum_ref[pl.ds(blocks_ref[0, k], 1), :]
         old[span, :] = jnp.broadcast_to(row, (TILE, TILE)).T
-
-
-def own_sum(blocks, own, accum, span, cap):
+    for c in copies:
+        c.wait()
+
+
+def own_sum(blocks, own, accum, table, span, cap):
     entries, cols = own.shape[0] - TAIL, own.shape[1]
+    tiles = accum.shape[0]
+    free = tiles - span // TILE
     return pl.pallas_call(
         functools.partial(own_kernel, cap),
         out_shape=[
             jax.ShapeDtypeStruct((span, cols), F32),
             jax.ShapeDtypeStruct((span, TILE), F32),
+            jax.ShapeDtypeStruct(table.shape, F32),
         ],
-        in_specs=[whole(SMEM), whole(), whole()],
-        out_specs=[whole()] * 2,
+        in_specs=[whole(SMEM), whole(), whole(), whole()],
+        out_specs=[whole(), whole(), whole(pltpu.HBM)],
+        scratch_shapes=[SMEM((tiles + 1,), jnp.int32), pltpu.SemaphoreType.DMA((free,))],
         compiler_params=params(),
         cost_estimate=pl.CostEstimate(
             flops=2 * span * entries * cols, bytes_accessed=span * cols * 4, transcendentals=0
         ),
-    )(blocks, own, accum)
-
-
-def one_kernel(cap, payload, part):
-    place = positions(payload, cap)
-    for k in range(part.shape[0] // TILE):
-        part[k * TILE : (k + 1) * TILE, :] = block_sum(payload, place, k)
-
-
-def near_kernel(cap, one, two, part, near, side):
-    places = [positions(ref, cap) for ref in (one, two)]
+    )(blocks, own, accum, table)
+
+
+def near_kernel(cap, one, two, own_c, part, near, side, part_c):
+    places = [positions(ref, cap) for ref in (one, two, own_c)]
     for k in range(near.shape[0] // TILE):
         span = slice(k * TILE, (k + 1) * TILE)
         near[span, :] = part[span, :] + block_sum(one, places[0], k)
         side[span, :] = block_sum(two, places[1], k)
+        part_c[span, :] = block_sum(own_c, places[2], k)
 
 
 def rest_kernel(cap, diag, one_c, two_c, near, side, part_c, mine, near_c, side_c):
@@ -352,16 +342,15 @@
         return swap(x, lambda r: (0, 1))
 
     mine = pack(send_count, pooled_grad, send_sample, send_row)
-    target = stage(after(union_blocks, mine[0]), table)
-    arrived = [swap(mine[j], lambda r: (j, 0)) for j in (3, 2, 1)]
-    own = join(after(mine[0], target), *arrived)
+    table = load(after(table, mine[0]))
+    arrived = [swap(mine[j], lambda r: (j, 0)) for j in (2, 3, 1)]
+    own = join(after(mine[0], table), *arrived)
     one = first(own)
     own_c = core(own)
-    part, old = own_sum(union_blocks, own, old_accum, span, cap)
-    (part_c,) = sum_call(one_kernel, [own_c], [], 1, span, cap)
-    two = second(after(own, part, part_c))
+    part, old, target = own_sum(union_blocks, own, old_accum, table, span, cap)
+    two = second(after(own, part, own_c))
     diag = second(one)
-    near, side = sum_call(near_kernel, [one, two], [part], 2, span, cap)
+    near, side, part_c = sum_call(near_kernel, [one, two, own_c], [part], 3, span, cap)
     one_c, two_c = core(one), core(two)
     last = core(after(diag, near))
     mine, near_c, side_c = sum_call(

time: 33 us -> 32.4 us (0.982)
    pallas_call x1, Pallas kernels: 1.25 us -> 2.64 us  [own_sum(): pl.pallas_call(functools.partial(own_kernel, cap), out_shape=[jax.ShapeDt...]
    pallas_call x1, Pallas kernels: 3.57 us -> 2.22 us  [load(): pl.pallas_call(load_kernel, out_shape=VMEM(table.shape, F32), in_specs=[w...]
    pallas_call x3 -> x2, Pallas kernels: 3.97 us -> 3.92 us  [sum_call(): pl.pallas_call(functools.partial(kernel, cap), out_shape=[wide] * results...]
  transfers between devices with their start and end apart: 10 -> 10, of which waited for: 4 -> 6; matrix products, arithmetic and copies ran while one was open for 0% -> 0% of each run, Pallas kernels for 27% -> 27%
where the time goes in v5:
time: 32.4 us; the launch traced here: 32.2 us
  Pallas kernels  13.6 us (42%)
  starting transfers between devices  11.4 us (35%)
  waiting for transfers between devices  6.42 us (20%)
  between operations  0.71 us (2%)
    ppermute x10, starting transfers between devices, swap(): return lax.ppermute(x, ('shard', 'rep'), pairs)  11.4 us
    ppermute x10, waiting for transfers between devices, swap(): return lax.ppermute(x, ('shard', 'rep'), pairs)  6.42 us
    pallas_call x2, Pallas kernels, sum_call(): pl.pallas_call(functools.partial(kernel, cap), out_shape=[wide] * results...  3.92 us
    pallas_call x1, Pallas kernels, update(): pl.pallas_call(functools.partial(update_kernel, cap), out_shape=[jax.Shap...  3.53 us
    pallas_call x1, Pallas kernels, own_sum(): pl.pallas_call(functools.partial(own_kernel, cap), out_shape=[jax.ShapeDt...  2.64 us
    pallas_call x1, Pallas kernels, load(): pl.pallas_call(load_kernel, out_shape=VMEM(table.shape, F32), in_specs=[w...  2.22 us
    pallas_call x1, Pallas kernels, pack(): pl.pallas_call(pack_kernel, out_shape=[shape] * owners, in_specs=[whole(p...  1.28 us
  transfers between devices with their start and end apart: 10, of which 6 were waited for; matrix products, arithmetic and copies ran while one was open for 0% of the time, Pallas kernels for 27%

profile of v5, /device:TPU:0, one launch (start us, length us, event | category | flops | bytes accessed | tf_op | source)
XLA Modules:
  0.0 32.2 jit_solution(15305561342240560959)
XLA Ops:
  0.6 1.3 %shard_map.86 = (bf16[144,256]{1,0:T(8,128)(2,1)S(1)}, bf16[144,256]{1,0:T(8,128)(2,1)S(1)}, bf16[144,256]{1,0:T(8,128)(2,1)S(1)}, bf16[144,256]{1,0:T(8,128)(2,1)S(1)}) custom-call(s32[4]{0:T(128)} %count_in.1, bf16[256,256]{1,0:T(8,128)(2,1)} %grad_in.1, s32[4,128]{1,0:T(4,128)} %sample_in.1, s32[4,128]{1,0:T(4,128)} %row_in.1), custom_call_target="tpu_custom_call" | custom-call | tf_op jit(solution)/shard_map/pallas_call | solution.py:83
  1.9 4.1 %collective-permute-start = (bf16[144,256]{1,0:T(8,128)(2,1)S(1)}, bf16[144,256]{1,0:T(8,128)(2,1)S(1)}, u32[]{:S(2)}, u32[]{:S(2)}) collective-permute-start(bf16[144,256]{1,0:T(8,128)(2,1)S(1)} %get-tuple-element.24), channel_id=1, source_target_pairs={{0,16},{1,17},{2,18},{3,19},{4,20},{5,21},{6,22},{7,23},{8,24},{9,... | collective-permute-start | bytes 221192 | tf_op jit(solution)/shard_map/ppermute | solution.py:333
  6.0 1.3 %collective-permute-start.1 = (bf16[144,256]{1,0:T(8,128)(2,1)S(1)}, bf16[144,256]{1,0:T(8,128)(2,1)S(1)}, u32[]{:S(2)}, u32[]{:S(2)}) collective-permute-start(bf16[144,256]{1,0:T(8,128)(2,1)S(1)} %get-tuple-element.25), channel_id=1, source_target_pairs={{0,24},{1,25},{2,26},{3,27},{4,28},{5,29},{6,30},{7,31},{8,16},{9,... | collective-permute-start | bytes 221192 | tf_op jit(solution)/shard_map/ppermute | solution.py:333
  7.4 0.2 collective-permute-start.2
  7.6 2.2 %shard_map.87.table_in = f32[4096,256]{1,0:T(8,128)S(1)} custom-call(f32[4096,256]{1,0:T(8,128)} %table_in), custom_call_target="tpu_custom_call" | custom-call | bytes 12582912 | tf_op jit(solution)/shard_map/pallas_call | solution.py:161
  9.8 1.1 %collective-permute-done.refs_1_ = bf16[144,256]{1,0:T(8,128)(2,1)S(1)} collective-permute-done((bf16[144,256]{1,0:T(8,128)(2,1)S(1)}, bf16[144,256]{1,0:T(8,128)(2,1)S(1)}, u32[]{:S(2)}, u32[]{:S(2)}) %collective-permute-start) | collective-permute-done | bytes 73760 | tf_op jit(solution)/shard_map/ppermute | solution.py:333
  10.9 1.6 %collective-permute-done.1.refs_2_ = bf16[144,256]{1,0:T(8,128)(2,1)S(1)} collective-permute-done((bf16[144,256]{1,0:T(8,128)(2,1)S(1)}, bf16[144,256]{1,0:T(8,128)(2,1)S(1)}, u32[]{:S(2)}, u32[]{:S(2)}) %collective-permute-start.1) | collective-permute-done | bytes 73760 | tf_op jit(solution)/shard_map/ppermute | solution.py:333
  12.5 0.2 collective-permute-done.2.refs_3_
  12.7 0.1 collective-permute-start.5
  12.8 1.8 %collective-permute-start.3 = (bf16[528,256]{1,0:T(8,128)(2,1)S(1)}, bf16[528,256]{1,0:T(8,128)(2,1)S(1)}, u32[]{:S(2)}, u32[]{:S(2)}) collective-permute-start(bf16[528,256]{1,0:T(8,128)(2,1)S(1)} %shard_map.88.own), channel_id=1, source_target_pairs={{0,2},{1,5},{2,0},{3,7},{4,6},{5,1},{6,4},{7,3},{8,10},{9,13},{10,... | collective-permute-start | bytes 811016 | tf_op jit(solution)/shard_map/ppermute | solution.py:333
  14.5 2.6 %shard_map.89 = (f32[2048,256]{1,0:T(8,128)S(1)}, f32[2048,128]{1,0:T(8,128)S(1)}, f32[4096,256]{1,0:T(8,128)}) custom-call(s32[1,16]{1,0:T(1,128)S(1)} %copy-done.1, bf16[528,256]{1,0:T(8,128)(2,1)S(1)} %shard_map.88.own, f32[32,128]{1,0:T(8,128)S(1)} %bitcast.2, f32[4096,256]{1,0:T(8,128)S(1)} %shard_map.87.table_in), custom_call_target="tpu_custom_call" | custom-call | flops 536870912 | bytes 2097152 | tf_op jit(solution)/shard_map/pallas_call | solution.py:201
  17.2 0.0 collective-permute-done.5.own_c
  17.2 1.6 %collective-permute-start.6 = (bf16[528,256]{1,0:T(8,128)(2,1)S(1)}, bf16[528,256]{1,0:T(8,128)(2,1)S(1)}, u32[]{:S(2)}, u32[]{:S(2)}) collective-permute-start(bf16[528,256]{1,0:T(8,128)(2,1)S(1)} %shard_map.88.own), channel_id=1, source_target_pairs={{0,4},{1,3},{2,6},{3,1},{4,0},{5,7},{6,2},{7,5},{8,12},{9,11},{10,... | collective-permute-start | bytes 811016 | tf_op jit(solution)/shard_map/ppermute | solution.py:333
  18.8 0.5 %collective-permute-done.3.one = bf16[528,256]{1,0:T(8,128)(2,1)S(1)} collective-permute-done((bf16[528,256]{1,0:T(8,128)(2,1)S(1)}, bf16[528,256]{1,0:T(8,128)(2,1)S(1)}, u32[]{:S(2)}, u32[]{:S(2)}) %collective-permute-start.3) | collective-permute-done | bytes 270368 | tf_op jit(solution)/shard_map/ppermute | solution.py:333
  19.3 2.3 %collective-permute-start.4 = (bf16[528,256]{1,0:T(8,128)(2,1)S(1)}, bf16[528,256]{1,0:T(8,128)(2,1)S(1)}, u32[]{:S(2)}, u32[]{:S(2)}) collective-permute-start(bf16[528,256]{1,0:T(8,128)(2,1)S(1)} %collective-permute-done.3.one), channel_id=1, source_target_pairs={{0,4},{1,3},{2,6},{3,1},{4,0},{5,7},{6,2},{7,5},{8,12},{9,11},{10,... | collective-permute-start | bytes 811016 | tf_op jit(solution)/shard_map/ppermute | solution.py:333
  21.6 0.0 collective-permute-start.8
  21.6 2.1 %collective-permute-done.6.two = bf16[528,256]{1,0:T(8,128)(2,1)S(1)} collective-permute-done((bf16[528,256]{1,0:T(8,128)(2,1)S(1)}, bf16[528,256]{1,0:T(8,128)(2,1)S(1)}, u32[]{:S(2)}, u32[]{:S(2)}) %collective-permute-start.6) | collective-permute-done | bytes 270368 | tf_op jit(solution)/shard_map/ppermute | solution.py:333
  23.7 0.0 collective-permute-start.9
  23.7 1.9 %shard_map.90 = (f32[2048,256]{1,0:T(8,128)S(1)}, f32[2048,256]{1,0:T(8,128)S(1)}, f32[2048,256]{1,0:T(8,128)S(1)}) custom-call(bf16[528,256]{1,0:T(8,128)(2,1)S(1)} %collective-permute-done.3.one, bf16[528,256]{1,0:T(8,128)(2,1)S(1)} %collective-permute-done.6.two, bf16[528,256]{1,0:T(8,128)(2,1)S(1)} %collective-permute-done.5.own_c, ...), custom_call_target="tpu_custom_call" | custom-call | flops 1610612736 | bytes 8388608 | tf_op jit(solution)/shard_map/pallas_call | solution.py:239
  25.6 1.0 %collective-permute-done.4.diag = bf16[528,256]{1,0:T(8,128)(2,1)S(1)} collective-permute-done((bf16[528,256]{1,0:T(8,128)(2,1)S(1)}, bf16[528,256]{1,0:T(8,128)(2,1)S(1)}, u32[]{:S(2)}, u32[]{:S(2)}) %collective-permute-start.4) | collective-permute-done | bytes 270368 | tf_op jit(solution)/shard_map/ppermute | solution.py:333
  26.6 0.0 collective-permute-start.7
  26.6 0.0 collective-permute-done.8.one_c
  26.6 2.0 %shard_map.91 = (f32[2048,256]{1,0:T(8,128)S(1)}, f32[2048,256]{1,0:T(8,128)S(1)}, f32[2048,256]{1,0:T(8,128)S(1)}) custom-call(bf16[528,256]{1,0:T(8,128)(2,1)S(1)} %collective-permute-done.4.diag, bf16[528,256]{1,0:T(8,128)(2,1)S(1)} %collective-permute-done.8.one_c, bf16[528,256]{1,0:T(8,128)(2,1)S(1)} %collective-permute-done.9.two_c, ...), custom_call_target="tpu_custom_call" | custom-call | flops 1610612736 | bytes 12582912 | tf_op jit(solution)/shard_map/pallas_call | solution.py:239
  28.7 3.5 %shard_map.92 = (f32[4096,256]{1,0:T(8,128)}, f32[32,128]{1,0:T(8,128)}) custom-call(s32[1,16]{1,0:T(1,128)S(1)} %copy-done.1, bf16[528,256]{1,0:T(8,128)(2,1)S(1)} %collective-permute-done.7.last, f32[2048,256]{1,0:T(8,128)S(1)} %get-tuple-element.33.mine, f32[2048,256]{1,0:T(8,128)S(1)} %get-tuple-element.34.near, ...), custom_call_target="tpu_custom_call", output_to_operand_aliasing={{0}: (8, {})} | custom-call | tf_op jit(solution)/shard_map/pallas_call | solution.py:297
  (7 shorter events, 0.0 us)
Async XLA Ops:
  1.9 9.0 %collective-permute-start = (bf16[144,256]{1,0:T(8,128)(2,1)S(1)}, bf16[144,256]{1,0:T(8,128)(2,1)S(1)}, u32[]{:S(2)}, u32[]{:S(2)}) collective-permute-start(bf16[144,256]{1,0:T(8,128)(2,1)S(1)} %get-tuple-element.24), channel_id=1, source_target_pairs={{0,16},{1,17},{2,18},{3,19},{4,20},{5,21},{6,22},{7,23},{8,24},{9,... | collective-permute-start | bytes 221192 | tf_op jit(solution)/shard_map/ppermute | solution.py:333
  6.0 6.5 %collective-permute-start.1 = (bf16[144,256]{1,0:T(8,128)(2,1)S(1)}, bf16[144,256]{1,0:T(8,128)(2,1)S(1)}, u32[]{:S(2)}, u32[]{:S(2)}) collective-permute-start(bf16[144,256]{1,0:T(8,128)(2,1)S(1)} %get-tuple-element.25), channel_id=1, source_target_pairs={{0,24},{1,25},{2,26},{3,27},{4,28},{5,29},{6,30},{7,31},{8,16},{9,... | collective-permute-start | bytes 221192 | tf_op jit(solution)/shard_map/ppermute | solution.py:333
  7.4 5.3 %collective-permute-start.2 = (bf16[144,256]{1,0:T(8,128)(2,1)S(1)}, bf16[144,256]{1,0:T(8,128)(2,1)S(1)}, u32[]{:S(2)}, u32[]{:S(2)}) collective-permute-start(bf16[144,256]{1,0:T(8,128)(2,1)S(1)} %get-tuple-element.26), channel_id=1, source_target_pairs={{0,8},{1,9},{2,10},{3,11},{4,12},{5,13},{6,14},{7,15},{8,0},{9,1},... | collective-permute-start | bytes 221192 | tf_op jit(solution)/shard_map/ppermute | solution.py:333
  7.6 6.9 %copy-start = (f32[4096]{0:T(1024)S(1)}, f32[4096]{0:T(1024)}, u32[]{:S(2)}) copy-start(f32[4096]{0:T(1024)} %param.13) | copy-start | bytes 49156
  7.6 6.9 %copy-start.1 = (s32[1,16]{1,0:T(1,128)S(1)}, s32[1,16]{1,0:T(1,128)}, u32[]{:S(2)}) copy-start(s32[1,16]{1,0:T(1,128)} %blocks_ref.3) | copy-start | bytes 196
  12.7 4.5 %collective-permute-start.5 = (bf16[528,256]{1,0:T(8,128)(2,1)S(1)}, bf16[528,256]{1,0:T(8,128)(2,1)S(1)}, u32[]{:S(2)}, u32[]{:S(2)}) collective-permute-start(bf16[528,256]{1,0:T(8,128)(2,1)S(1)} %shard_map.88.own), channel_id=1, source_target_pairs={{0,1},{1,0},{2,3},{3,2},{4,5},{5,4},{6,7},{7,6},{8,9},{9,8},{10,11... | collective-permute-start | bytes 811016 | tf_op jit(solution)/shard_map/ppermute | solution.py:333
  12.8 6.5 %collective-permute-start.3 = (bf16[528,256]{1,0:T(8,128)(2,1)S(1)}, bf16[528,256]{1,0:T(8,128)(2,1)S(1)}, u32[]{:S(2)}, u32[]{:S(2)}) collective-permute-start(bf16[528,256]{1,0:T(8,128)(2,1)S(1)} %shard_map.88.own), channel_id=1, source_target_pairs={{0,2},{1,5},{2,0},{3,7},{4,6},{5,1},{6,4},{7,3},{8,10},{9,13},{10,... | collective-permute-start | bytes 811016 | tf_op jit(solution)/shard_map/ppermute | solution.py:333
  17.2 6.5 %collective-permute-start.6 = (bf16[528,256]{1,0:T(8,128)(2,1)S(1)}, bf16[528,256]{1,0:T(8,128)(2,1)S(1)}, u32[]{:S(2)}, u32[]{:S(2)}) collective-permute-start(bf16[528,256]{1,0:T(8,128)(2,1)S(1)} %shard_map.88.own), channel_id=1, source_target_pairs={{0,4},{1,3},{2,6},{3,1},{4,0},{5,7},{6,2},{7,5},{8,12},{9,11},{10,... | collective-permute-start | bytes 811016 | tf_op jit(solution)/shard_map/ppermute | solution.py:333
  19.3 7.3 %collective-permute-start.4 = (bf16[528,256]{1,0:T(8,128)(2,1)S(1)}, bf16[528,256]{1,0:T(8,128)(2,1)S(1)}, u32[]{:S(2)}, u32[]{:S(2)}) collective-permute-start(bf16[528,256]{1,0:T(8,128)(2,1)S(1)} %collective-permute-done.3.one), channel_id=1, source_target_pairs={{0,4},{1,3},{2,6},{3,1},{4,0},{5,7},{6,2},{7,5},{8,12},{9,11},{10,... | collective-permute-start | bytes 811016 | tf_op jit(solution)/shard_map/ppermute | solution.py:333
  21.6 5.0 %collective-permute-start.8 = (bf16[528,256]{1,0:T(8,128)(2,1)S(1)}, bf16[528,256]{1,0:T(8,128)(2,1)S(1)}, u32[]{:S(2)}, u32[]{:S(2)}) collective-permute-start(bf16[528,256]{1,0:T(8,128)(2,1)S(1)} %collective-permute-done.3.one), channel_id=1, source_target_pairs={{0,1},{1,0},{2,3},{3,2},{4,5},{5,4},{6,7},{7,6},{8,9},{9,8},{10,11... | collective-permute-start | bytes 811016 | tf_op jit(solution)/shard_map/ppermute | solution.py:333
  23.7 2.9 %collective-permute-start.9 = (bf16[528,256]{1,0:T(8,128)(2,1)S(1)}, bf16[528,256]{1,0:T(8,128)(2,1)S(1)}, u32[]{:S(2)}, u32[]{:S(2)}) collective-permute-start(bf16[528,256]{1,0:T(8,128)(2,1)S(1)} %collective-permute-done.6.two), channel_id=1, source_target_pairs={{0,1},{1,0},{2,3},{3,2},{4,5},{5,4},{6,7},{7,6},{8,9},{9,8},{10,11... | collective-permute-start | bytes 811016 | tf_op jit(solution)/shard_map/ppermute | solution.py:333
  26.6 2.0 %collective-permute-start.7 = (bf16[528,256]{1,0:T(8,128)(2,1)S(1)}, bf16[528,256]{1,0:T(8,128)(2,1)S(1)}, u32[]{:S(2)}, u32[]{:S(2)}) collective-permute-start(bf16[528,256]{1,0:T(8,128)(2,1)S(1)} %collective-permute-done.4.diag), channel_id=1, source_target_pairs={{0,1},{1,0},{2,3},{3,2},{4,5},{5,4},{6,7},{7,6},{8,9},{9,8},{10,11... | collective-permute-start | bytes 811016 | tf_op jit(solution)/shard_map/ppermute | solution.py:333

commit v6 on v5

--- a/solution.py
+++ b/solution.py
@@ -147,90 +147,106 @@
     return jnp.dot(pick, ref[0:entries, :], preferred_element_type=F32)
 
 
+def group_sum(ref, place, k, size):
+    slot, within = place
+    entries = slot.shape[1]
+    sub = lax.broadcasted_iota(jnp.int32, (TILE, entries), 0).astype(F32).astype(BF16)
+    picks = []
+    for b in range(k, k + size):
+        here = jnp.where(slot == b, within, -1.0).astype(BF16)
+        picks.append(jnp.where(sub == here, jnp.ones((), BF16), jnp.zeros((), BF16)))
+    pick = jnp.concatenate(picks, axis=0)
+    return jnp.dot(pick, ref[0:entries, :], preferred_element_type=F32)
+
+
 def tile(ref, block):
     return ref.at[pl.ds(pl.multiple_of(block * TILE, TILE), TILE), :]
 
 
-def load_kernel(table_in, table_out, sem):
-    c = pltpu.make_async_copy(table_in, table_out, sem)
-    c.start()
-    c.wait()
-
-
-def load(table):
+CHUNKS = 4
+
+
+def load_kernel(blocks_ref, table_in, table_out, table_ref, loads, kept):
+    n = blocks_ref.shape[1]
+    tiles = table_in.shape[0] // TILE
+    size = tiles // CHUNKS
+    copies = []
+    for i in range(CHUNKS):
+        rows = pl.ds(i * size * TILE, size * TILE)
+        c = pltpu.make_async_copy(table_in.at[rows, :], table_out.at[rows, :], loads.at[i])
+        c.start()
+        copies.append(c)
+    seen = jnp.int32(0)
+    for i in range(CHUNKS):
+        copies[i].wait()
+        for t in range(i * size, (i + 1) * size):
+            touched = blocks_ref[0, jnp.minimum(seen, n - 1)] == t
+
+            @pl.when(jnp.logical_not(touched))
+            def _():
+                pltpu.make_async_copy(tile(table_out, t), tile(table_ref, t), kept).start()
+
+            seen = seen + touched.astype(jnp.int32)
+    for _ in range(tiles - n):
+        pltpu.make_async_copy(tile(table_out, 0), tile(table_ref, 0), kept).wait()
+
+
+def load(blocks, table):
     return pl.pallas_call(
         load_kernel,
-        out_shape=VMEM(table.shape, F32),
-        in_specs=[whole(pltpu.HBM)],
-        out_specs=whole(),
-        scratch_shapes=[pltpu.SemaphoreType.DMA],
+        out_shape=[VMEM(table.shape, F32), jax.ShapeDtypeStruct(table.shape, F32)],
+        in_specs=[whole(SMEM), whole(pltpu.HBM)],
+        out_specs=[whole(), whole(pltpu.HBM)],
+        scratch_shapes=[pltpu.SemaphoreType.DMA((CHUNKS,)), pltpu.SemaphoreType.DMA],
         compiler_params=params(LOAD_MIB),
         cost_estimate=pl.CostEstimate(
             flops=0, bytes_accessed=4 * table.size * 3, transcendentals=0
         ),
-    )(table)
-
-
-def own_kernel(cap, blocks_ref, own, accum_ref, table_in, part, old, table_ref, free_ref, sems):
-    n = part.shape[0] // TILE
-    tiles = accum_ref.shape[0]
-    seen = jnp.int32(0)
-    for t in range(tiles):
-        free_ref[t - seen] = t
-        seen = seen + (blocks_ref[0, jnp.minimum(seen, n - 1)] == t).astype(jnp.int32)
-    copies = [
-        pltpu.make_async_copy(tile(table_in, free_ref[i]), tile(table_ref, free_ref[i]), sems.at[i])
-        for i in range(tiles - n)
-    ]
-    for c in copies:
-        c.start()
+    )(blocks, table)
+
+
+def own_kernel(cap, blocks_ref, own, accum_ref, part, old):
     place = positions(own, cap)
-    for k in range(n):
+    for k in range(part.shape[0] // TILE):
         span = slice(k * TILE, (k + 1) * TILE)
         part[span, :] = block_sum(own, place, k)
         row = accum_ref[pl.ds(blocks_ref[0, k], 1), :]
         old[span, :] = jnp.broadcast_to(row, (TILE, TILE)).T
-    for c in copies:
-        c.wait()
-
-
-def own_sum(blocks, own, accum, table, span, cap):
+
+
+def own_sum(blocks, own, accum, span, cap):
     entries, cols = own.shape[0] - TAIL, own.shape[1]
-    tiles = accum.shape[0]
-    free = tiles - span // TILE
     return pl.pallas_call(
         functools.partial(own_kernel, cap),
         out_shape=[
             jax.ShapeDtypeStruct((span, cols), F32),
             jax.ShapeDtypeStruct((span, TILE), F32),
-            jax.ShapeDtypeStruct(table.shape, F32),
         ],
-        in_specs=[whole(SMEM), whole(), whole(), whole()],
-        out_specs=[whole(), whole(), whole(pltpu.HBM)],
-        scratch_shapes=[SMEM((tiles + 1,), jnp.int32), pltpu.SemaphoreType.DMA((free,))],
+        in_specs=[whole(SMEM), whole(), whole()],
+        out_specs=[whole()] * 2,
         compiler_params=params(),
         cost_estimate=pl.CostEstimate(
             flops=2 * span * entries * cols, bytes_accessed=span * cols * 4, transcendentals=0
         ),
-    )(blocks, own, accum, table)
+    )(blocks, own, accum)
 
 
 def near_kernel(cap, one, two, own_c, part, near, side, part_c):
     places = [positions(ref, cap) for ref in (one, two, own_c)]
-    for k in range(near.shape[0] // TILE):
-        span = slice(k * TILE, (k + 1) * TILE)
-        near[span, :] = part[span, :] + block_sum(one, places[0], k)
-        side[span, :] = block_sum(two, places[1], k)
-        part_c[span, :] = block_sum(own_c, places[2], k)
+    for k in range(0, near.shape[0] // TILE, 4):
+        span = slice(k * TILE, (k + 4) * TILE)
+        near[span, :] = part[span, :] + group_sum(one, places[0], k, 4)
+        side[span, :] = group_sum(two, places[1], k, 4)
+        part_c[span, :] = group_sum(own_c, places[2], k, 4)
 
 
 def rest_kernel(cap, diag, one_c, two_c, near, side, part_c, mine, near_c, side_c):
     places = [positions(ref, cap) for ref in (diag, one_c, two_c)]
-    for k in range(near.shape[0] // TILE):
-        span = slice(k * TILE, (k + 1) * TILE)
-        mine[span, :] = near[span, :] + (side[span, :] + block_sum(diag, places[0], k))
-        near_c[span, :] = part_c[span, :] + block_sum(one_c, places[1], k)
-        side_c[span, :] = block_sum(two_c, places[2], k)
+    for k in range(0, near.shape[0] // TILE, 4):
+        span = slice(k * TILE, (k + 4) * TILE)
+        mine[span, :] = near[span, :] + (side[span, :] + group_sum(diag, places[0], k, 4))
+        near_c[span, :] = part_c[span, :] + group_sum(one_c, places[1], k, 4)
+        side_c[span, :] = group_sum(two_c, places[2], k, 4)
 
 
 def sum_call(kernel, payloads, parts, results, span, cap):
@@ -265,10 +281,9 @@
     ones = jnp.ones((2 * cols, TILE), BF16)
     news = []
     copies = []
-    for k in range(n):
-        span = slice(k * TILE, (k + 1) * TILE)
-        block = pl.multiple_of(blocks_ref[0, k] * TILE, TILE)
-        other = near[span, :] + (side[span, :] + block_sum(last, place, k))
+    for g in range(0, n, 4):
+        span = slice(g * TILE, (g + 4) * TILE)
+        other = near[span, :] + (side[span, :] + group_sum(last, place, g, 4))
         grad = (mine[span, :] + other).astype(BF16).astype(F32)
         square = grad * grad
         high = square.astype(BF16)
@@ -276,14 +291,18 @@
         total = jnp.dot(jnp.concatenate([high, low], axis=1), ones, preferred_element_type=F32)
         new = old[span, :] + total * (1.0 / cols)
         rate = LEARNING_RATE / (jnp.sqrt(new) + EPSILON)
-        for c in range(0, cols, TILE):
-            rows_out[span, c : c + TILE] = (
-                table_in[pl.ds(block, TILE), c : c + TILE] - grad[:, c : c + TILE] * rate
-            )
-        news.append(jnp.sum(jnp.where(diagonal, new, 0.0), axis=0, keepdims=True))
-        c = pltpu.make_async_copy(rows_out.at[span, :], tile(table_ref, blocks_ref[0, k]), sems.at[k])
-        c.start()
-        copies.append(c)
+        for k in range(g, g + 4):
+            block = pl.multiple_of(blocks_ref[0, k] * TILE, TILE)
+            at = slice((k - g) * TILE, (k - g + 1) * TILE)
+            here = slice(k * TILE, (k + 1) * TILE)
+            for c in range(0, cols, TILE):
+                rows_out[here, c : c + TILE] = (
+                    table_in[pl.ds(block, TILE), c : c + TILE] - grad[at, c : c + TILE] * rate[at, :]
+                )
+            news.append(jnp.sum(jnp.where(diagonal, new[at, :], 0.0), axis=0, keepdims=True))
+            c = pltpu.make_async_copy(rows_out.at[here, :], tile(table_ref, blocks_ref[0, k]), sems.at[k])
+            c.start()
+            copies.append(c)
     for k in range(n):
         accum_new[pl.ds(blocks_ref[0, k], 1), :] = news[k]
     c = pltpu.make_async_copy(accum_new, accum_out, sem)
@@ -342,12 +361,13 @@
         return swap(x, lambda r: (0, 1))
 
     mine = pack(send_count, pooled_grad, send_sample, send_row)
-    table = load(after(table, mine[0]))
+    table, target = load(union_blocks, after(table, mine[0]))
     arrived = [swap(mine[j], lambda r: (j, 0)) for j in (2, 3, 1)]
+    early = first(mine[0])
     own = join(after(mine[0], table), *arrived)
-    one = first(own)
-    own_c = core(own)
-    part, old, target = own_sum(union_blocks, own, old_accum, table, span, cap)
+    one = join(early, first(join(*arrived)))
+    own_c = core(after(own, early))
+    part, old = own_sum(union_blocks, own, old_accum, span, cap)
     two = second(after(own, part, own_c))
     diag = second(one)
     near, side, part_c = sum_call(near_kernel, [one, two, own_c], [part], 3, span, cap)

time: 32.4 us -> 31.7 us (0.978)
  waiting for transfers between devices: 6.42 us -> 3.97 us
  starting transfers between devices: 11.4 us -> 13.3 us
    ppermute x10 -> x11, waiting for transfers between devices: 6.42 us -> 3.97 us  [swap(): return lax.ppermute(x, ('shard', 'rep'), pairs)]
    ppermute x10 -> x11, starting transfers between devices: 11.4 us -> 13.3 us  [swap(): return lax.ppermute(x, ('shard', 'rep'), pairs)]
    pallas_call x1, Pallas kernels: 2.22 us -> 3.66 us  [load(): pl.pallas_call(load_kernel, out_shape=[VMEM(table.shape, F32), jax.ShapeD...]
    pallas_call x1, Pallas kernels: 2.64 us -> 1.26 us  [own_sum(): pl.pallas_call(functools.partial(own_kernel, cap), out_shape=[jax.ShapeDt...]
  transfers between devices with their start and end apart: 10 -> 11, of which waited for: 6 -> 3; matrix products, arithmetic and copies ran while one was open for 0% -> 0% of each run, Pallas kernels for 27% -> 28%
where the time goes in v6:
time: 31.7 us; the launch traced here: 31.4 us
  Pallas kernels  13.5 us (43%)
  starting transfers between devices  13.3 us (42%)
  waiting for transfers between devices  3.97 us (13%)
  between operations  0.75 us (2%)
    ppermute x11, starting transfers between devices, swap(): return lax.ppermute(x, ('shard', 'rep'), pairs)  13.3 us
    ppermute x11, waiting for transfers between devices, swap(): return lax.ppermute(x, ('shard', 'rep'), pairs)  3.97 us
    pallas_call x1, Pallas kernels, load(): pl.pallas_call(load_kernel, out_shape=[VMEM(table.shape, F32), jax.ShapeD...  3.66 us
    pallas_call x2, Pallas kernels, sum_call(): pl.pallas_call(functools.partial(kernel, cap), out_shape=[wide] * results...  3.65 us
    pallas_call x1, Pallas kernels, update(): pl.pallas_call(functools.partial(update_kernel, cap), out_shape=[jax.Shap...  3.53 us
    pallas_call x1, Pallas kernels, pack(): pl.pallas_call(pack_kernel, out_shape=[shape] * owners, in_specs=[whole(p...  1.28 us
    pallas_call x1, Pallas kernels, own_sum(): pl.pallas_call(functools.partial(own_kernel, cap), out_shape=[jax.ShapeDt...  1.26 us
  transfers between devices with their start and end apart: 11, of which 3 were waited for; matrix products, arithmetic and copies ran while one was open for 0% of the time, Pallas kernels for 28%

profile of v6, /device:TPU:0, one launch (start us, length us, event | category | flops | bytes accessed | tf_op | source)
XLA Modules:
  0.0 31.4 jit_solution(1030890504975479920)
XLA Ops:
  0.6 1.3 %shard_map.86 = (bf16[144,256]{1,0:T(8,128)(2,1)S(1)}, bf16[144,256]{1,0:T(8,128)(2,1)S(1)}, bf16[144,256]{1,0:T(8,128)(2,1)S(1)}, bf16[144,256]{1,0:T(8,128)(2,1)S(1)}) custom-call(s32[4]{0:T(128)} %count_in.1, bf16[256,256]{1,0:T(8,128)(2,1)} %grad_in.1, s32[4,128]{1,0:T(4,128)} %sample_in.1, s32[4,128]{1,0:T(4,128)} %row_in.1), custom_call_target="tpu_custom_call" | custom-call | tf_op jit(solution)/shard_map/pallas_call | solution.py:83
  1.9 4.1 %collective-permute-start.1 = (bf16[144,256]{1,0:T(8,128)(2,1)S(1)}, bf16[144,256]{1,0:T(8,128)(2,1)S(1)}, u32[]{:S(2)}, u32[]{:S(2)}) collective-permute-start(bf16[144,256]{1,0:T(8,128)(2,1)S(1)} %get-tuple-element.24), channel_id=1, source_target_pairs={{0,16},{1,17},{2,18},{3,19},{4,20},{5,21},{6,22},{7,23},{8,24},{9,... | collective-permute-start | bytes 221192 | tf_op jit(solution)/shard_map/ppermute | solution.py:352
  6.0 1.3 %collective-permute-start.2 = (bf16[144,256]{1,0:T(8,128)(2,1)S(1)}, bf16[144,256]{1,0:T(8,128)(2,1)S(1)}, u32[]{:S(2)}, u32[]{:S(2)}) collective-permute-start(bf16[144,256]{1,0:T(8,128)(2,1)S(1)} %get-tuple-element.25), channel_id=1, source_target_pairs={{0,24},{1,25},{2,26},{3,27},{4,28},{5,29},{6,30},{7,31},{8,16},{9,... | collective-permute-start | bytes 221192 | tf_op jit(solution)/shard_map/ppermute | solution.py:352
  7.4 0.2 collective-permute-start.3
  7.6 1.5 %collective-permute-start = (bf16[144,256]{1,0:T(8,128)(2,1)S(1)}, bf16[144,256]{1,0:T(8,128)(2,1)S(1)}, u32[]{:S(2)}, u32[]{:S(2)}) collective-permute-start(bf16[144,256]{1,0:T(8,128)(2,1)S(1)} %get-tuple-element.29.refs_0_), channel_id=1, source_target_pairs={{0,2},{1,5},{2,0},{3,7},{4,6},{5,1},{6,4},{7,3},{8,10},{9,13},{10,... | collective-permute-start | bytes 221192 | tf_op jit(solution)/shard_map/ppermute | solution.py:352
  9.1 3.7 %shard_map.89 = (f32[4096,256]{1,0:T(8,128)S(1)}, f32[4096,256]{1,0:T(8,128)}) custom-call(s32[1,16]{1,0:T(1,128)} %blocks_ref.5, f32[4096,256]{1,0:T(8,128)} %table_in), custom_call_target="tpu_custom_call" | custom-call | bytes 12582912 | tf_op jit(solution)/shard_map/pallas_call | solution.py:195
  12.8 0.0 collective-permute-done.1.refs_0_.refs_1_
  12.8 0.0 collective-permute-done.2.refs_1_.refs_2_
  12.8 0.1 collective-permute-start.6
  13.0 1.6 %collective-permute-start.4 = (bf16[400,256]{1,0:T(8,128)(2,1)S(1)}, bf16[400,256]{1,0:T(8,128)(2,1)S(1)}, u32[]{:S(2)}, u32[]{:S(2)}) collective-permute-start(bf16[400,256]{1,0:T(8,128)(2,1)S(1)} %shard_map.87), channel_id=1, source_target_pairs={{0,2},{1,5},{2,0},{3,7},{4,6},{5,1},{6,4},{7,3},{8,10},{9,13},{10,... | collective-permute-start | bytes 614408 | tf_op jit(solution)/shard_map/ppermute | solution.py:352
  14.6 1.3 %shard_map.91 = (f32[2048,256]{1,0:T(8,128)S(1)}, f32[2048,128]{1,0:T(8,128)S(1)}) custom-call(s32[1,16]{1,0:T(1,128)S(1)} %copy-done.1, bf16[528,256]{1,0:T(8,128)(2,1)S(1)} %shard_map.90.own, f32[32,128]{1,0:T(8,128)S(1)} %bitcast.2), custom_call_target="tpu_custom_call" | custom-call | flops 536870912 | bytes 2097152 | tf_op jit(solution)/shard_map/pallas_call | solution.py:219
  15.8 0.0 collective-permute-done.6.own_c
  15.8 1.6 %collective-permute-start.7 = (bf16[528,256]{1,0:T(8,128)(2,1)S(1)}, bf16[528,256]{1,0:T(8,128)(2,1)S(1)}, u32[]{:S(2)}, u32[]{:S(2)}) collective-permute-start(bf16[528,256]{1,0:T(8,128)(2,1)S(1)} %shard_map.90.own), channel_id=1, source_target_pairs={{0,4},{1,3},{2,6},{3,1},{4,0},{5,7},{6,2},{7,5},{8,12},{9,11},{10,... | collective-permute-start | bytes 811016 | tf_op jit(solution)/shard_map/ppermute | solution.py:352
  17.4 1.3 %collective-permute-done.4.refs_1_ = bf16[400,256]{1,0:T(8,128)(2,1)S(1)} collective-permute-done((bf16[400,256]{1,0:T(8,128)(2,1)S(1)}, bf16[400,256]{1,0:T(8,128)(2,1)S(1)}, u32[]{:S(2)}, u32[]{:S(2)}) %collective-permute-start.4) | collective-permute-done | bytes 204832 | tf_op jit(solution)/shard_map/ppermute | solution.py:352
  18.8 2.8 %collective-permute-start.5 = (bf16[528,256]{1,0:T(8,128)(2,1)S(1)}, bf16[528,256]{1,0:T(8,128)(2,1)S(1)}, u32[]{:S(2)}, u32[]{:S(2)}) collective-permute-start(bf16[528,256]{1,0:T(8,128)(2,1)S(1)} %shard_map.88.one), channel_id=1, source_target_pairs={{0,4},{1,3},{2,6},{3,1},{4,0},{5,7},{6,2},{7,5},{8,12},{9,11},{10,... | collective-permute-start | bytes 811016 | tf_op jit(solution)/shard_map/ppermute | solution.py:352
  21.6 0.8 %collective-permute-done.7.two = bf16[528,256]{1,0:T(8,128)(2,1)S(1)} collective-permute-done((bf16[528,256]{1,0:T(8,128)(2,1)S(1)}, bf16[528,256]{1,0:T(8,128)(2,1)S(1)}, u32[]{:S(2)}, u32[]{:S(2)}) %collective-permute-start.7) | collective-permute-done | bytes 270368 | tf_op jit(solution)/shard_map/ppermute | solution.py:352
  22.4 0.0 collective-permute-start.10
  22.4 1.8 %shard_map.92 = (f32[2048,256]{1,0:T(8,128)S(1)}, f32[2048,256]{1,0:T(8,128)S(1)}, f32[2048,256]{1,0:T(8,128)S(1)}) custom-call(bf16[528,256]{1,0:T(8,128)(2,1)S(1)} %shard_map.88.one, bf16[528,256]{1,0:T(8,128)(2,1)S(1)} %collective-permute-done.7.two, bf16[528,256]{1,0:T(8,128)(2,1)S(1)} %collective-permute-done.6.own_c, ...), custom_call_target="tpu_custom_call" | custom-call | flops 1610612736 | bytes 8388608 | tf_op jit(solution)/shard_map/pallas_call | solution.py:255
  24.2 1.9 %collective-permute-done.5.diag = bf16[528,256]{1,0:T(8,128)(2,1)S(1)} collective-permute-done((bf16[528,256]{1,0:T(8,128)(2,1)S(1)}, bf16[528,256]{1,0:T(8,128)(2,1)S(1)}, u32[]{:S(2)}, u32[]{:S(2)}) %collective-permute-start.5) | collective-permute-done | bytes 270368 | tf_op jit(solution)/shard_map/ppermute | solution.py:352
  26.1 0.0 collective-permute-done.9.one_c
  26.1 0.0 collective-permute-done.10.two_c
  26.1 1.8 %shard_map.93 = (f32[2048,256]{1,0:T(8,128)S(1)}, f32[2048,256]{1,0:T(8,128)S(1)}, f32[2048,256]{1,0:T(8,128)S(1)}) custom-call(bf16[528,256]{1,0:T(8,128)(2,1)S(1)} %collective-permute-done.5.diag, bf16[528,256]{1,0:T(8,128)(2,1)S(1)} %collective-permute-done.9.one_c, bf16[528,256]{1,0:T(8,128)(2,1)S(1)} %collective-permute-done.10.two_c, ...), custom_call_target="tpu_custom_call" | custom-call | flops 1610612736 | bytes 12582912 | tf_op jit(solution)/shard_map/pallas_call | solution.py:255
  27.9 0.0 collective-permute-done.8.last
  27.9 3.5 %shard_map.94 = (f32[4096,256]{1,0:T(8,128)}, f32[32,128]{1,0:T(8,128)}) custom-call(s32[1,16]{1,0:T(1,128)S(1)} %copy-done.1, bf16[528,256]{1,0:T(8,128)(2,1)S(1)} %collective-permute-done.8.last, f32[2048,256]{1,0:T(8,128)S(1)} %get-tuple-element.37.mine, f32[2048,256]{1,0:T(8,128)S(1)} %get-tuple-element.38.near, ...), custom_call_target="tpu_custom_call", output_to_operand_aliasing={{0}: (8, {})} | custom-call | tf_op jit(solution)/shard_map/pallas_call | solution.py:316
  (11 shorter events, 0.1 us)
Async XLA Ops:
  1.9 10.8 %collective-permute-start.1 = (bf16[144,256]{1,0:T(8,128)(2,1)S(1)}, bf16[144,256]{1,0:T(8,128)(2,1)S(1)}, u32[]{:S(2)}, u32[]{:S(2)}) collective-permute-start(bf16[144,256]{1,0:T(8,128)(2,1)S(1)} %get-tuple-element.24), channel_id=1, source_target_pairs={{0,16},{1,17},{2,18},{3,19},{4,20},{5,21},{6,22},{7,23},{8,24},{9,... | collective-permute-start | bytes 221192 | tf_op jit(solution)/shard_map/ppermute | solution.py:352
  6.0 6.8 %collective-permute-start.2 = (bf16[144,256]{1,0:T(8,128)(2,1)S(1)}, bf16[144,256]{1,0:T(8,128)(2,1)S(1)}, u32[]{:S(2)}, u32[]{:S(2)}) collective-permute-start(bf16[144,256]{1,0:T(8,128)(2,1)S(1)} %get-tuple-element.25), channel_id=1, source_target_pairs={{0,24},{1,25},{2,26},{3,27},{4,28},{5,29},{6,30},{7,31},{8,16},{9,... | collective-permute-start | bytes 221192 | tf_op jit(solution)/shard_map/ppermute | solution.py:352
  7.4 5.4 %collective-permute-start.3 = (bf16[144,256]{1,0:T(8,128)(2,1)S(1)}, bf16[144,256]{1,0:T(8,128)(2,1)S(1)}, u32[]{:S(2)}, u32[]{:S(2)}) collective-permute-start(bf16[144,256]{1,0:T(8,128)(2,1)S(1)} %get-tuple-element.26), channel_id=1, source_target_pairs={{0,8},{1,9},{2,10},{3,11},{4,12},{5,13},{6,14},{7,15},{8,0},{9,1},... | collective-permute-start | bytes 221192 | tf_op jit(solution)/shard_map/ppermute | solution.py:352
  7.6 7.0 %copy-start = (f32[4096]{0:T(1024)S(1)}, f32[4096]{0:T(1024)}, u32[]{:S(2)}) copy-start(f32[4096]{0:T(1024)} %param.13) | copy-start | bytes 49156
  7.6 7.0 %copy-start.1 = (s32[1,16]{1,0:T(1,128)S(1)}, s32[1,16]{1,0:T(1,128)}, u32[]{:S(2)}) copy-start(s32[1,16]{1,0:T(1,128)} %blocks_ref.5) | copy-start | bytes 196
  7.6 5.2 %collective-permute-start = (bf16[144,256]{1,0:T(8,128)(2,1)S(1)}, bf16[144,256]{1,0:T(8,128)(2,1)S(1)}, u32[]{:S(2)}, u32[]{:S(2)}) collective-permute-start(bf16[144,256]{1,0:T(8,128)(2,1)S(1)} %get-tuple-element.29.refs_0_), channel_id=1, source_target_pairs={{0,2},{1,5},{2,0},{3,7},{4,6},{5,1},{6,4},{7,3},{8,10},{9,13},{10,... | collective-permute-start | bytes 221192 | tf_op jit(solution)/shard_map/ppermute | solution.py:352
  12.8 3.0 %collective-permute-start.6 = (bf16[528,256]{1,0:T(8,128)(2,1)S(1)}, bf16[528,256]{1,0:T(8,128)(2,1)S(1)}, u32[]{:S(2)}, u32[]{:S(2)}) collective-permute-start(bf16[528,256]{1,0:T(8,128)(2,1)S(1)} %shard_map.90.own), channel_id=1, source_target_pairs={{0,1},{1,0},{2,3},{3,2},{4,5},{5,4},{6,7},{7,6},{8,9},{9,8},{10,11... | collective-permute-start | bytes 811016 | tf_op jit(solution)/shard_map/ppermute | solution.py:352
  13.0 5.8 %collective-permute-start.4 = (bf16[400,256]{1,0:T(8,128)(2,1)S(1)}, bf16[400,256]{1,0:T(8,128)(2,1)S(1)}, u32[]{:S(2)}, u32[]{:S(2)}) collective-permute-start(bf16[400,256]{1,0:T(8,128)(2,1)S(1)} %shard_map.87), channel_id=1, source_target_pairs={{0,2},{1,5},{2,0},{3,7},{4,6},{5,1},{6,4},{7,3},{8,10},{9,13},{10,... | collective-permute-start | bytes 614408 | tf_op jit(solution)/shard_map/ppermute | solution.py:352
  15.8 6.5 %collective-permute-start.7 = (bf16[528,256]{1,0:T(8,128)(2,1)S(1)}, bf16[528,256]{1,0:T(8,128)(2,1)S(1)}, u32[]{:S(2)}, u32[]{:S(2)}) collective-permute-start(bf16[528,256]{1,0:T(8,128)(2,1)S(1)} %shard_map.90.own), channel_id=1, source_target_pairs={{0,4},{1,3},{2,6},{3,1},{4,0},{5,7},{6,2},{7,5},{8,12},{9,11},{10,... | collective-permute-start | bytes 811016 | tf_op jit(solution)/shard_map/ppermute | solution.py:352
  18.8 7.2 %collective-permute-start.5 = (bf16[528,256]{1,0:T(8,128)(2,1)S(1)}, bf16[528,256]{1,0:T(8,128)(2,1)S(1)}, u32[]{:S(2)}, u32[]{:S(2)}) collective-permute-start(bf16[528,256]{1,0:T(8,128)(2,1)S(1)} %shard_map.88.one), channel_id=1, source_target_pairs={{0,4},{1,3},{2,6},{3,1},{4,0},{5,7},{6,2},{7,5},{8,12},{9,11},{10,... | collective-permute-start | bytes 811016 | tf_op jit(solution)/shard_map/ppermute | solution.py:352
  21.6 4.4 %collective-permute-start.9 = (bf16[528,256]{1,0:T(8,128)(2,1)S(1)}, bf16[528,256]{1,0:T(8,128)(2,1)S(1)}, u32[]{:S(2)}, u32[]{:S(2)}) collective-permute-start(bf16[528,256]{1,0:T(8,128)(2,1)S(1)} %shard_map.88.one), channel_id=1, source_target_pairs={{0,1},{1,0},{2,3},{3,2},{4,5},{5,4},{6,7},{7,6},{8,9},{9,8},{10,11... | collective-permute-start | bytes 811016 | tf_op jit(solution)/shard_map/ppermute | solution.py:352
  22.4 3.7 %collective-permute-start.10 = (bf16[528,256]{1,0:T(8,128)(2,1)S(1)}, bf16[528,256]{1,0:T(8,128)(2,1)S(1)}, u32[]{:S(2)}, u32[]{:S(2)}) collective-permute-start(bf16[528,256]{1,0:T(8,128)(2,1)S(1)} %collective-permute-done.7.two), channel_id=1, source_target_pairs={{0,1},{1,0},{2,3},{3,2},{4,5},{5,4},{6,7},{7,6},{8,9},{9,8},{10,11... | collective-permute-start | bytes 811016 | tf_op jit(solution)/shard_map/ppermute | solution.py:352
  26.1 1.9 %collective-permute-start.8 = (bf16[528,256]{1,0:T(8,128)(2,1)S(1)}, bf16[528,256]{1,0:T(8,128)(2,1)S(1)}, u32[]{:S(2)}, u32[]{:S(2)}) collective-permute-start(bf16[528,256]{1,0:T(8,128)(2,1)S(1)} %collective-permute-done.5.diag), channel_id=1, source_target_pairs={{0,1},{1,0},{2,3},{3,2},{4,5},{5,4},{6,7},{7,6},{8,9},{9,8},{10,11... | collective-permute-start | bytes 811016 | tf_op jit(solution)/shard_map/ppermute | solution.py:352

commit v7 on v6

--- a/solution.py
+++ b/solution.py
@@ -205,48 +205,49 @@
     )(blocks, table)
 
 
-def own_kernel(cap, blocks_ref, own, accum_ref, part, old):
-    place = positions(own, cap)
+def own_kernel(cap, blocks_ref, own, own_c, accum_ref, part, part_c, old):
+    places = [positions(ref, cap) for ref in (own, own_c)]
     for k in range(part.shape[0] // TILE):
         span = slice(k * TILE, (k + 1) * TILE)
-        part[span, :] = block_sum(own, place, k)
+        part[span, :] = block_sum(own, places[0], k)
+        part_c[span, :] = block_sum(own_c, places[1], k)
         row = accum_ref[pl.ds(blocks_ref[0, k], 1), :]
         old[span, :] = jnp.broadcast_to(row, (TILE, TILE)).T
 
 
-def own_sum(blocks, own, accum, span, cap):
+def own_sum(blocks, own, own_c, accum, span, cap):
     entries, cols = own.shape[0] - TAIL, own.shape[1]
     return pl.pallas_call(
         functools.partial(own_kernel, cap),
         out_shape=[
             jax.ShapeDtypeStruct((span, cols), F32),
+            jax.ShapeDtypeStruct((span, cols), F32),
             jax.ShapeDtypeStruct((span, TILE), F32),
         ],
-        in_specs=[whole(SMEM), whole(), whole()],
-        out_specs=[whole()] * 2,
+        in_specs=[whole(SMEM)] + [whole()] * 3,
+        out_specs=[whole()] * 3,
         compiler_params=params(),
         cost_estimate=pl.CostEstimate(
             flops=2 * span * entries * cols, bytes_accessed=span * cols * 4, transcendentals=0
         ),
-    )(blocks, own, accum)
-
-
-def near_kernel(cap, one, two, own_c, part, near, side, part_c):
-    places = [positions(ref, cap) for ref in (one, two, own_c)]
+    )(blocks, own, own_c, accum)
+
+
+def near_kernel(cap, one, two, one_c, part, part_c, near, side, near_c):
+    places = [positions(ref, cap) for ref in (one, two, one_c)]
     for k in range(0, near.shape[0] // TILE, 4):
         span = slice(k * TILE, (k + 4) * TILE)
         near[span, :] = part[span, :] + group_sum(one, places[0], k, 4)
         side[span, :] = group_sum(two, places[1], k, 4)
-        part_c[span, :] = group_sum(own_c, places[2], k, 4)
-
-
-def rest_kernel(cap, diag, one_c, two_c, near, side, part_c, mine, near_c, side_c):
-    places = [positions(ref, cap) for ref in (diag, one_c, two_c)]
+        near_c[span, :] = part_c[span, :] + group_sum(one_c, places[2], k, 4)
+
+
+def rest_kernel(cap, diag, two_c, near, side, mine, side_c):
+    places = [positions(ref, cap) for ref in (diag, two_c)]
     for k in range(0, near.shape[0] // TILE, 4):
         span = slice(k * TILE, (k + 4) * TILE)
         mine[span, :] = near[span, :] + (side[span, :] + group_sum(diag, places[0], k, 4))
-        near_c[span, :] = part_c[span, :] + group_sum(one_c, places[1], k, 4)
-        side_c[span, :] = group_sum(two_c, places[2], k, 4)
+        side_c[span, :] = group_sum(two_c, places[1], k, 4)
 
 
 def sum_call(kernel, payloads, parts, results, span, cap):
@@ -367,15 +368,13 @@
     own = join(after(mine[0], table), *arrived)
     one = join(early, first(join(*arrived)))
     own_c = core(after(own, early))
-    part, old = own_sum(union_blocks, own, old_accum, span, cap)
-    two = second(after(own, part, own_c))
+    part, part_c, old = own_sum(union_blocks, own, own_c, old_accum, span, cap)
+    two = second(after(own, part))
     diag = second(one)
-    near, side, part_c = sum_call(near_kernel, [one, two, own_c], [part], 3, span, cap)
     one_c, two_c = core(one), core(two)
+    near, side, near_c = sum_call(near_kernel, [one, two, one_c], [part, part_c], 3, span, cap)
     last = core(after(diag, near))
-    mine, near_c, side_c = sum_call(
-        rest_kernel, [diag, one_c, two_c], [near, side, part_c], 3, span, cap
-    )
+    mine, side_c = sum_call(rest_kernel, [diag, two_c], [near, side], 2, span, cap)
     table_out, accum_out = update(
         union_blocks, last, (mine, near_c, side_c), old, table, old_accum, target, cap
     )

time: 31.7 us -> 31 us (0.978)
  starting transfers between devices: 13.3 us -> 12.2 us
  waiting for transfers between devices: 3.97 us -> 4.49 us
    ppermute x11, starting transfers between devices: 13.3 us -> 12.2 us  [swap(): return lax.ppermute(x, ('shard', 'rep'), pairs)]
    pallas_call x1, Pallas kernels: 1.26 us -> 1.8 us  [own_sum(): pl.pallas_call(functools.partial(own_kernel, cap), out_shape=[jax.ShapeDt...]
    pallas_call x2, Pallas kernels: 3.65 us -> 3.13 us  [sum_call(): pl.pallas_call(functools.partial(kernel, cap), out_shape=[wide] * results...]
    ppermute x11, waiting for transfers between devices: 3.97 us -> 4.49 us  [swap(): return lax.ppermute(x, ('shard', 'rep'), pairs)]
  transfers between devices with their start and end apart: 11 -> 11, of which waited for: 3 -> 4; matrix products, arithmetic and copies ran while one was open for 0% -> 0% of each run, Pallas kernels for 28% -> 28%
where the time goes in v7:
time: 31 us; the launch traced here: 30.9 us
  Pallas kernels  13.4 us (43%)
  starting transfers between devices  12.2 us (39%)
  waiting for transfers between devices  4.49 us (14%)
  between operations  0.75 us (2%)
    ppermute x11, starting transfers between devices, swap(): return lax.ppermute(x, ('shard', 'rep'), pairs)  12.2 us
    ppermute x11, waiting for transfers between devices, swap(): return lax.ppermute(x, ('shard', 'rep'), pairs)  4.49 us
    pallas_call x1, Pallas kernels, load(): pl.pallas_call(load_kernel, out_shape=[VMEM(table.shape, F32), jax.ShapeD...  3.66 us
    pallas_call x1, Pallas kernels, update(): pl.pallas_call(functools.partial(update_kernel, cap), out_shape=[jax.Shap...  3.5 us
    pallas_call x2, Pallas kernels, sum_call(): pl.pallas_call(functools.partial(kernel, cap), out_shape=[wide] * results...  3.13 us
    pallas_call x1, Pallas kernels, own_sum(): pl.pallas_call(functools.partial(own_kernel, cap), out_shape=[jax.ShapeDt...  1.8 us
    pallas_call x1, Pallas kernels, pack(): pl.pallas_call(pack_kernel, out_shape=[shape] * owners, in_specs=[whole(p...  1.28 us
  transfers between devices with their start and end apart: 11, of which 4 were waited for; matrix products, arithmetic and copies ran while one was open for 0% of the time, Pallas kernels for 28%

profile of v7, /device:TPU:0, one launch (start us, length us, event | category | flops | bytes accessed | tf_op | source)
XLA Modules:
  0.0 30.9 jit_solution(18370563897864048724)
XLA Ops:
  0.6 1.3 %shard_map.86 = (bf16[144,256]{1,0:T(8,128)(2,1)S(1)}, bf16[144,256]{1,0:T(8,128)(2,1)S(1)}, bf16[144,256]{1,0:T(8,128)(2,1)S(1)}, bf16[144,256]{1,0:T(8,128)(2,1)S(1)}) custom-call(s32[4]{0:T(128)} %count_in.1, bf16[256,256]{1,0:T(8,128)(2,1)} %grad_in.1, s32[4,128]{1,0:T(4,128)} %sample_in.1, s32[4,128]{1,0:T(4,128)} %row_in.1), custom_call_target="tpu_custom_call" | custom-call | tf_op jit(solution)/shard_map/pallas_call | solution.py:83
  1.9 4.1 %collective-permute-start.1 = (bf16[144,256]{1,0:T(8,128)(2,1)S(1)}, bf16[144,256]{1,0:T(8,128)(2,1)S(1)}, u32[]{:S(2)}, u32[]{:S(2)}) collective-permute-start(bf16[144,256]{1,0:T(8,128)(2,1)S(1)} %get-tuple-element.24), channel_id=1, source_target_pairs={{0,16},{1,17},{2,18},{3,19},{4,20},{5,21},{6,22},{7,23},{8,24},{9,... | collective-permute-start | bytes 221192 | tf_op jit(solution)/shard_map/ppermute | solution.py:353
  6.0 1.3 %collective-permute-start.2 = (bf16[144,256]{1,0:T(8,128)(2,1)S(1)}, bf16[144,256]{1,0:T(8,128)(2,1)S(1)}, u32[]{:S(2)}, u32[]{:S(2)}) collective-permute-start(bf16[144,256]{1,0:T(8,128)(2,1)S(1)} %get-tuple-element.25), channel_id=1, source_target_pairs={{0,24},{1,25},{2,26},{3,27},{4,28},{5,29},{6,30},{7,31},{8,16},{9,... | collective-permute-start | bytes 221192 | tf_op jit(solution)/shard_map/ppermute | solution.py:353
  7.4 0.2 collective-permute-start.3
  7.6 1.5 %collective-permute-start = (bf16[144,256]{1,0:T(8,128)(2,1)S(1)}, bf16[144,256]{1,0:T(8,128)(2,1)S(1)}, u32[]{:S(2)}, u32[]{:S(2)}) collective-permute-start(bf16[144,256]{1,0:T(8,128)(2,1)S(1)} %get-tuple-element.29.refs_0_), channel_id=1, source_target_pairs={{0,2},{1,5},{2,0},{3,7},{4,6},{5,1},{6,4},{7,3},{8,10},{9,13},{10,... | collective-permute-start | bytes 221192 | tf_op jit(solution)/shard_map/ppermute | solution.py:353
  9.1 3.7 %shard_map.89 = (f32[4096,256]{1,0:T(8,128)S(1)}, f32[4096,256]{1,0:T(8,128)}) custom-call(s32[1,16]{1,0:T(1,128)} %blocks_ref.5, f32[4096,256]{1,0:T(8,128)} %table_in), custom_call_target="tpu_custom_call" | custom-call | bytes 12582912 | tf_op jit(solution)/shard_map/pallas_call | solution.py:195
  12.8 0.0 collective-permute-done.1.refs_0_.refs_1_
  12.8 0.0 collective-permute-done.2.refs_1_.refs_2_
  12.8 0.0 collective-permute-done.3.refs_2_.refs_3_
  12.8 0.0 collective-permute-done.refs_0_
  12.8 0.1 collective-permute-start.6
  13.0 1.6 %collective-permute-start.4 = (bf16[400,256]{1,0:T(8,128)(2,1)S(1)}, bf16[400,256]{1,0:T(8,128)(2,1)S(1)}, u32[]{:S(2)}, u32[]{:S(2)}) collective-permute-start(bf16[400,256]{1,0:T(8,128)(2,1)S(1)} %shard_map.87), channel_id=1, source_target_pairs={{0,2},{1,5},{2,0},{3,7},{4,6},{5,1},{6,4},{7,3},{8,10},{9,13},{10,... | collective-permute-start | bytes 614408 | tf_op jit(solution)/shard_map/ppermute | solution.py:353
  14.6 0.0 collective-permute-done.6.own_c
  14.6 1.8 %shard_map.91 = (f32[2048,256]{1,0:T(8,128)S(1)}, f32[2048,256]{1,0:T(8,128)S(1)}, f32[2048,128]{1,0:T(8,128)S(1)}) custom-call(s32[1,16]{1,0:T(1,128)S(1)} %copy-done.1, bf16[528,256]{1,0:T(8,128)(2,1)S(1)} %shard_map.90.own, bf16[528,256]{1,0:T(8,128)(2,1)S(1)} %collective-permute-done.6.own_c, f32[32,128]{1,0:T(8,128)S(1)} %bitcast.2), custom_call_target="tpu_custom_call" | custom-call | flops 536870912 | bytes 2097152 | tf_op jit(solution)/shard_map/pallas_call | solution.py:220
  16.4 1.6 %collective-permute-start.7 = (bf16[528,256]{1,0:T(8,128)(2,1)S(1)}, bf16[528,256]{1,0:T(8,128)(2,1)S(1)}, u32[]{:S(2)}, u32[]{:S(2)}) collective-permute-start(bf16[528,256]{1,0:T(8,128)(2,1)S(1)} %shard_map.90.own), channel_id=1, source_target_pairs={{0,4},{1,3},{2,6},{3,1},{4,0},{5,7},{6,2},{7,5},{8,12},{9,11},{10,... | collective-permute-start | bytes 811016 | tf_op jit(solution)/shard_map/ppermute | solution.py:353
  18.0 0.8 %collective-permute-done.4.refs_1_ = bf16[400,256]{1,0:T(8,128)(2,1)S(1)} collective-permute-done((bf16[400,256]{1,0:T(8,128)(2,1)S(1)}, bf16[400,256]{1,0:T(8,128)(2,1)S(1)}, u32[]{:S(2)}, u32[]{:S(2)}) %collective-permute-start.4) | collective-permute-done | bytes 204832 | tf_op jit(solution)/shard_map/ppermute | solution.py:353
  18.8 0.1 collective-permute-start.8
  18.9 1.6 %collective-permute-start.5 = (bf16[528,256]{1,0:T(8,128)(2,1)S(1)}, bf16[528,256]{1,0:T(8,128)(2,1)S(1)}, u32[]{:S(2)}, u32[]{:S(2)}) collective-permute-start(bf16[528,256]{1,0:T(8,128)(2,1)S(1)} %shard_map.88.one), channel_id=1, source_target_pairs={{0,4},{1,3},{2,6},{3,1},{4,0},{5,7},{6,2},{7,5},{8,12},{9,11},{10,... | collective-permute-start | bytes 811016 | tf_op jit(solution)/shard_map/ppermute | solution.py:353
  20.5 2.4 %collective-permute-done.7.two = bf16[528,256]{1,0:T(8,128)(2,1)S(1)} collective-permute-done((bf16[528,256]{1,0:T(8,128)(2,1)S(1)}, bf16[528,256]{1,0:T(8,128)(2,1)S(1)}, u32[]{:S(2)}, u32[]{:S(2)}) %collective-permute-start.7) | collective-permute-done | bytes 270368 | tf_op jit(solution)/shard_map/ppermute | solution.py:353
  22.9 1.8 %shard_map.92 = (f32[2048,256]{1,0:T(8,128)S(1)}, f32[2048,256]{1,0:T(8,128)S(1)}, f32[2048,256]{1,0:T(8,128)S(1)}) custom-call(bf16[528,256]{1,0:T(8,128)(2,1)S(1)} %shard_map.88.one, bf16[528,256]{1,0:T(8,128)(2,1)S(1)} %collective-permute-done.7.two, bf16[528,256]{1,0:T(8,128)(2,1)S(1)} %collective-permute-done.8.one_c, ...), custom_call_target="tpu_custom_call" | custom-call | flops 1610612736 | bytes 10485760 | tf_op jit(solution)/shard_map/pallas_call | solution.py:256
  24.8 1.1 %collective-permute-done.5.diag = bf16[528,256]{1,0:T(8,128)(2,1)S(1)} collective-permute-done((bf16[528,256]{1,0:T(8,128)(2,1)S(1)}, bf16[528,256]{1,0:T(8,128)(2,1)S(1)}, u32[]{:S(2)}, u32[]{:S(2)}) %collective-permute-start.5) | collective-permute-done | bytes 270368 | tf_op jit(solution)/shard_map/ppermute | solution.py:353
  25.8 1.3 %shard_map.93 = (f32[2048,256]{1,0:T(8,128)S(1)}, f32[2048,256]{1,0:T(8,128)S(1)}) custom-call(bf16[528,256]{1,0:T(8,128)(2,1)S(1)} %collective-permute-done.5.diag, bf16[528,256]{1,0:T(8,128)(2,1)S(1)} %collective-permute-done.10.two_c, f32[2048,256]{1,0:T(8,128)S(1)} %get-tuple-element.34.near, f32[2048,256]{1,0:T(8,128)S(1)} %get-tuple-element.36.side), custom_call_target="tpu_custom_call" | custom-call | flops 1073741824 | bytes 8388608 | tf_op jit(solution)/shard_map/pallas_call | solution.py:256
  27.1 0.2 collective-permute-done.9.last
  27.4 3.5 %shard_map.94 = (f32[4096,256]{1,0:T(8,128)}, f32[32,128]{1,0:T(8,128)}) custom-call(s32[1,16]{1,0:T(1,128)S(1)} %copy-done.1, bf16[528,256]{1,0:T(8,128)(2,1)S(1)} %collective-permute-done.9.last, f32[2048,256]{1,0:T(8,128)S(1)} %get-tuple-element.37.mine, f32[2048,256]{1,0:T(8,128)S(1)} %get-tuple-element.38.near, ...), custom_call_target="tpu_custom_call", output_to_operand_aliasing={{0}: (8, {})} | custom-call | tf_op jit(solution)/shard_map/pallas_call | solution.py:317
  (11 shorter events, 0.1 us)
Async XLA Ops:
  1.9 10.8 %collective-permute-start.1 = (bf16[144,256]{1,0:T(8,128)(2,1)S(1)}, bf16[144,256]{1,0:T(8,128)(2,1)S(1)}, u32[]{:S(2)}, u32[]{:S(2)}) collective-permute-start(bf16[144,256]{1,0:T(8,128)(2,1)S(1)} %get-tuple-element.24), channel_id=1, source_target_pairs={{0,16},{1,17},{2,18},{3,19},{4,20},{5,21},{6,22},{7,23},{8,24},{9,... | collective-permute-start | bytes 221192 | tf_op jit(solution)/shard_map/ppermute | solution.py:353
  6.0 6.8 %collective-permute-start.2 = (bf16[144,256]{1,0:T(8,128)(2,1)S(1)}, bf16[144,256]{1,0:T(8,128)(2,1)S(1)}, u32[]{:S(2)}, u32[]{:S(2)}) collective-permute-start(bf16[144,256]{1,0:T(8,128)(2,1)S(1)} %get-tuple-element.25), channel_id=1, source_target_pairs={{0,24},{1,25},{2,26},{3,27},{4,28},{5,29},{6,30},{7,31},{8,16},{9,... | collective-permute-start | bytes 221192 | tf_op jit(solution)/shard_map/ppermute | solution.py:353
  7.4 5.4 %collective-permute-start.3 = (bf16[144,256]{1,0:T(8,128)(2,1)S(1)}, bf16[144,256]{1,0:T(8,128)(2,1)S(1)}, u32[]{:S(2)}, u32[]{:S(2)}) collective-permute-start(bf16[144,256]{1,0:T(8,128)(2,1)S(1)} %get-tuple-element.26), channel_id=1, source_target_pairs={{0,8},{1,9},{2,10},{3,11},{4,12},{5,13},{6,14},{7,15},{8,0},{9,1},... | collective-permute-start | bytes 221192 | tf_op jit(solution)/shard_map/ppermute | solution.py:353
  7.6 7.0 %copy-start = (f32[4096]{0:T(1024)S(1)}, f32[4096]{0:T(1024)}, u32[]{:S(2)}) copy-start(f32[4096]{0:T(1024)} %param.13) | copy-start | bytes 49156
  7.6 7.0 %copy-start.1 = (s32[1,16]{1,0:T(1,128)S(1)}, s32[1,16]{1,0:T(1,128)}, u32[]{:S(2)}) copy-start(s32[1,16]{1,0:T(1,128)} %blocks_ref.5) | copy-start | bytes 196
  7.6 5.2 %collective-permute-start = (bf16[144,256]{1,0:T(8,128)(2,1)S(1)}, bf16[144,256]{1,0:T(8,128)(2,1)S(1)}, u32[]{:S(2)}, u32[]{:S(2)}) collective-permute-start(bf16[144,256]{1,0:T(8,128)(2,1)S(1)} %get-tuple-element.29.refs_0_), channel_id=1, source_target_pairs={{0,2},{1,5},{2,0},{3,7},{4,6},{5,1},{6,4},{7,3},{8,10},{9,13},{10,... | collective-permute-start | bytes 221192 | tf_op jit(solution)/shard_map/ppermute | solution.py:353
  12.8 1.7 %collective-permute-start.6 = (bf16[528,256]{1,0:T(8,128)(2,1)S(1)}, bf16[528,256]{1,0:T(8,128)(2,1)S(1)}, u32[]{:S(2)}, u32[]{:S(2)}) collective-permute-start(bf16[528,256]{1,0:T(8,128)(2,1)S(1)} %shard_map.90.own), channel_id=1, source_target_pairs={{0,1},{1,0},{2,3},{3,2},{4,5},{5,4},{6,7},{7,6},{8,9},{9,8},{10,11... | collective-permute-start | bytes 811016 | tf_op jit(solution)/shard_map/ppermute | solution.py:353
  13.0 5.8 %collective-permute-start.4 = (bf16[400,256]{1,0:T(8,128)(2,1)S(1)}, bf16[400,256]{1,0:T(8,128)(2,1)S(1)}, u32[]{:S(2)}, u32[]{:S(2)}) collective-permute-start(bf16[400,256]{1,0:T(8,128)(2,1)S(1)} %shard_map.87), channel_id=1, source_target_pairs={{0,2},{1,5},{2,0},{3,7},{4,6},{5,1},{6,4},{7,3},{8,10},{9,13},{10,... | collective-permute-start | bytes 614408 | tf_op jit(solution)/shard_map/ppermute | solution.py:353
  16.4 6.5 %collective-permute-start.7 = (bf16[528,256]{1,0:T(8,128)(2,1)S(1)}, bf16[528,256]{1,0:T(8,128)(2,1)S(1)}, u32[]{:S(2)}, u32[]{:S(2)}) collective-permute-start(bf16[528,256]{1,0:T(8,128)(2,1)S(1)} %shard_map.90.own), channel_id=1, source_target_pairs={{0,4},{1,3},{2,6},{3,1},{4,0},{5,7},{6,2},{7,5},{8,12},{9,11},{10,... | collective-permute-start | bytes 811016 | tf_op jit(solution)/shard_map/ppermute | solution.py:353
  18.8 4.1 %collective-permute-start.8 = (bf16[528,256]{1,0:T(8,128)(2,1)S(1)}, bf16[528,256]{1,0:T(8,128)(2,1)S(1)}, u32[]{:S(2)}, u32[]{:S(2)}) collective-permute-start(bf16[528,256]{1,0:T(8,128)(2,1)S(1)} %shard_map.88.one), channel_id=1, source_target_pairs={{0,1},{1,0},{2,3},{3,2},{4,5},{5,4},{6,7},{7,6},{8,9},{9,8},{10,11... | collective-permute-start | bytes 811016 | tf_op jit(solution)/shard_map/ppermute | solution.py:353
  18.9 6.9 %collective-permute-start.5 = (bf16[528,256]{1,0:T(8,128)(2,1)S(1)}, bf16[528,256]{1,0:T(8,128)(2,1)S(1)}, u32[]{:S(2)}, u32[]{:S(2)}) collective-permute-start(bf16[528,256]{1,0:T(8,128)(2,1)S(1)} %shard_map.88.one), channel_id=1, source_target_pairs={{0,4},{1,3},{2,6},{3,1},{4,0},{5,7},{6,2},{7,5},{8,12},{9,11},{10,... | collective-permute-start | bytes 811016 | tf_op jit(solution)/shard_map/ppermute | solution.py:353
  22.9 2.9 %collective-permute-start.10 = (bf16[528,256]{1,0:T(8,128)(2,1)S(1)}, bf16[528,256]{1,0:T(8,128)(2,1)S(1)}, u32[]{:S(2)}, u32[]{:S(2)}) collective-permute-start(bf16[528,256]{1,0:T(8,128)(2,1)S(1)} %collective-permute-done.7.two), channel_id=1, source_target_pairs={{0,1},{1,0},{2,3},{3,2},{4,5},{5,4},{6,7},{7,6},{8,9},{9,8},{10,11... | collective-permute-start | bytes 811016 | tf_op jit(solution)/shard_map/ppermute | solution.py:353
  25.8 1.5 %collective-permute-start.9 = (bf16[528,256]{1,0:T(8,128)(2,1)S(1)}, bf16[528,256]{1,0:T(8,128)(2,1)S(1)}, u32[]{:S(2)}, u32[]{:S(2)}) collective-permute-start(bf16[528,256]{1,0:T(8,128)(2,1)S(1)} %collective-permute-done.5.diag), channel_id=1, source_target_pairs={{0,1},{1,0},{2,3},{3,2},{4,5},{5,4},{6,7},{7,6},{8,9},{9,8},{10,11... | collective-permute-start | bytes 811016 | tf_op jit(solution)/shard_map/ppermute | solution.py:353

commit v8 on v7

--- a/solution.py
+++ b/solution.py
@@ -207,12 +207,13 @@
 
 def own_kernel(cap, blocks_ref, own, own_c, accum_ref, part, part_c, old):
     places = [positions(ref, cap) for ref in (own, own_c)]
+    for k in range(0, part.shape[0] // TILE, 4):
+        span = slice(k * TILE, (k + 4) * TILE)
+        part[span, :] = group_sum(own, places[0], k, 4)
+        part_c[span, :] = group_sum(own_c, places[1], k, 4)
     for k in range(part.shape[0] // TILE):
-        span = slice(k * TILE, (k + 1) * TILE)
-        part[span, :] = block_sum(own, places[0], k)
-        part_c[span, :] = block_sum(own_c, places[1], k)
         row = accum_ref[pl.ds(blocks_ref[0, k], 1), :]
-        old[span, :] = jnp.broadcast_to(row, (TILE, TILE)).T
+        old[k * TILE : (k + 1) * TILE, :] = jnp.broadcast_to(row, (TILE, TILE)).T
 
 
 def own_sum(blocks, own, own_c, accum, span, cap):
@@ -279,20 +280,22 @@
     diagonal = lax.broadcasted_iota(jnp.int32, (TILE, TILE), 0) == lax.broadcasted_iota(
         jnp.int32, (TILE, TILE), 1
     )
-    ones = jnp.ones((2 * cols, TILE), BF16)
+    ones = jnp.ones((2 * TILE, TILE), BF16)
     news = []
     copies = []
-    for g in range(0, n, 4):
-        span = slice(g * TILE, (g + 4) * TILE)
-        other = near[span, :] + (side[span, :] + group_sum(last, place, g, 4))
+    bounds = sorted({0, n // 2, 3 * n // 4, n})
+    for g, end in zip(bounds, bounds[1:]):
+        span = slice(g * TILE, end * TILE)
+        other = near[span, :] + (side[span, :] + group_sum(last, place, g, end - g))
         grad = (mine[span, :] + other).astype(BF16).astype(F32)
         square = grad * grad
+        square = sum(square[:, c : c + TILE] for c in range(0, cols, TILE))
         high = square.astype(BF16)
         low = (square - high.astype(F32)).astype(BF16)
         total = jnp.dot(jnp.concatenate([high, low], axis=1), ones, preferred_element_type=F32)
         new = old[span, :] + total * (1.0 / cols)
-        rate = LEARNING_RATE / (jnp.sqrt(new) + EPSILON)
-        for k in range(g, g + 4):
+        rate = LEARNING_RATE / (new * lax.rsqrt(new) + EPSILON)
+        for k in range(g, end):
             block = pl.multiple_of(blocks_ref[0, k] * TILE, TILE)
             at = slice((k - g) * TILE, (k - g + 1) * TILE)
             here = slice(k * TILE, (k + 1) * TILE)

time: 31 us -> 30.7 us (level)
    pallas_call x1, Pallas kernels: 3.5 us -> 3.17 us  [update(): pl.pallas_call(functools.partial(update_kernel, cap), out_shape=[jax.Shap...]
  transfers between devices with their start and end apart: 11 -> 11, of which waited for: 4 -> 4; matrix products, arithmetic and copies ran while one was open for 0% -> 0% of each run, Pallas kernels for 28% -> 29%
where the time goes in v8:
time: 30.7 us; the launch traced here: 30.5 us
  Pallas kernels  13.2 us (43%)
  starting transfers between devices  12.1 us (39%)
  waiting for transfers between devices  4.53 us (15%)
  between operations  0.75 us (2%)
    ppermute x11, starting transfers between devices, swap(): return lax.ppermute(x, ('shard', 'rep'), pairs)  12.1 us
    ppermute x11, waiting for transfers between devices, swap(): return lax.ppermute(x, ('shard', 'rep'), pairs)  4.53 us
    pallas_call x1, Pallas kernels, load(): pl.pallas_call(load_kernel, out_shape=[VMEM(table.shape, F32), jax.ShapeD...  3.71 us
    pallas_call x1, Pallas kernels, update(): pl.pallas_call(functools.partial(update_kernel, cap), out_shape=[jax.Shap...  3.17 us
    pallas_call x2, Pallas kernels, sum_call(): pl.pallas_call(functools.partial(kernel, cap), out_shape=[wide] * results...  3.13 us
    pallas_call x1, Pallas kernels, own_sum(): pl.pallas_call(functools.partial(own_kernel, cap), out_shape=[jax.ShapeDt...  1.8 us
    pallas_call x1, Pallas kernels, pack(): pl.pallas_call(pack_kernel, out_shape=[shape] * owners, in_specs=[whole(p...  1.28 us
  transfers between devices with their start and end apart: 11, of which 4 were waited for; matrix products, arithmetic and copies ran while one was open for 0% of the time, Pallas kernels for 29%

profile of v8, /device:TPU:0, one launch (start us, length us, event | category | flops | bytes accessed | tf_op | source)
XLA Modules:
  0.0 30.5 jit_solution(707904153932608389)
XLA Ops:
  0.6 1.3 %shard_map.86 = (bf16[144,256]{1,0:T(8,128)(2,1)S(1)}, bf16[144,256]{1,0:T(8,128)(2,1)S(1)}, bf16[144,256]{1,0:T(8,128)(2,1)S(1)}, bf16[144,256]{1,0:T(8,128)(2,1)S(1)}) custom-call(s32[4]{0:T(128)} %count_in.1, bf16[256,256]{1,0:T(8,128)(2,1)} %grad_in.1, s32[4,128]{1,0:T(4,128)} %sample_in.1, s32[4,128]{1,0:T(4,128)} %row_in.1), custom_call_target="tpu_custom_call" | custom-call | tf_op jit(solution)/shard_map/pallas_call | solution.py:83
  1.9 4.1 %collective-permute-start.1 = (bf16[144,256]{1,0:T(8,128)(2,1)S(1)}, bf16[144,256]{1,0:T(8,128)(2,1)S(1)}, u32[]{:S(2)}, u32[]{:S(2)}) collective-permute-start(bf16[144,256]{1,0:T(8,128)(2,1)S(1)} %get-tuple-element.24), channel_id=1, source_target_pairs={{0,16},{1,17},{2,18},{3,19},{4,20},{5,21},{6,22},{7,23},{8,24},{9,... | collective-permute-start | bytes 221192 | tf_op jit(solution)/shard_map/ppermute | solution.py:356
  6.0 1.3 %collective-permute-start.2 = (bf16[144,256]{1,0:T(8,128)(2,1)S(1)}, bf16[144,256]{1,0:T(8,128)(2,1)S(1)}, u32[]{:S(2)}, u32[]{:S(2)}) collective-permute-start(bf16[144,256]{1,0:T(8,128)(2,1)S(1)} %get-tuple-element.25), channel_id=1, source_target_pairs={{0,24},{1,25},{2,26},{3,27},{4,28},{5,29},{6,30},{7,31},{8,16},{9,... | collective-permute-start | bytes 221192 | tf_op jit(solution)/shard_map/ppermute | solution.py:356
  7.4 0.2 collective-permute-start.3
  7.6 1.5 %collective-permute-start = (bf16[144,256]{1,0:T(8,128)(2,1)S(1)}, bf16[144,256]{1,0:T(8,128)(2,1)S(1)}, u32[]{:S(2)}, u32[]{:S(2)}) collective-permute-start(bf16[144,256]{1,0:T(8,128)(2,1)S(1)} %get-tuple-element.29.refs_0_), channel_id=1, source_target_pairs={{0,2},{1,5},{2,0},{3,7},{4,6},{5,1},{6,4},{7,3},{8,10},{9,13},{10,... | collective-permute-start | bytes 221192 | tf_op jit(solution)/shard_map/ppermute | solution.py:356
  9.1 3.7 %shard_map.89 = (f32[4096,256]{1,0:T(8,128)S(1)}, f32[4096,256]{1,0:T(8,128)}) custom-call(s32[1,16]{1,0:T(1,128)} %blocks_ref.5, f32[4096,256]{1,0:T(8,128)} %table_in), custom_call_target="tpu_custom_call" | custom-call | bytes 12582912 | tf_op jit(solution)/shard_map/pallas_call | solution.py:195
  12.8 0.0 collective-permute-done.1.refs_0_.refs_1_
  12.8 0.0 collective-permute-done.2.refs_1_.refs_2_
  12.9 0.0 collective-permute-done.refs_0_
  12.9 0.1 collective-permute-start.6
  13.0 1.6 %collective-permute-start.4 = (bf16[400,256]{1,0:T(8,128)(2,1)S(1)}, bf16[400,256]{1,0:T(8,128)(2,1)S(1)}, u32[]{:S(2)}, u32[]{:S(2)}) collective-permute-start(bf16[400,256]{1,0:T(8,128)(2,1)S(1)} %shard_map.87), channel_id=1, source_target_pairs={{0,2},{1,5},{2,0},{3,7},{4,6},{5,1},{6,4},{7,3},{8,10},{9,13},{10,... | collective-permute-start | bytes 614408 | tf_op jit(solution)/shard_map/ppermute | solution.py:356
  14.6 0.0 collective-permute-done.6.own_c
  14.6 1.8 %shard_map.91 = (f32[2048,256]{1,0:T(8,128)S(1)}, f32[2048,256]{1,0:T(8,128)S(1)}, f32[2048,128]{1,0:T(8,128)S(1)}) custom-call(s32[1,16]{1,0:T(1,128)S(1)} %copy-done.1, bf16[528,256]{1,0:T(8,128)(2,1)S(1)} %shard_map.90.own, bf16[528,256]{1,0:T(8,128)(2,1)S(1)} %collective-permute-done.6.own_c, f32[32,128]{1,0:T(8,128)S(1)} %bitcast.2), custom_call_target="tpu_custom_call" | custom-call | flops 536870912 | bytes 2097152 | tf_op jit(solution)/shard_map/pallas_call | solution.py:221
  16.4 1.6 %collective-permute-start.7 = (bf16[528,256]{1,0:T(8,128)(2,1)S(1)}, bf16[528,256]{1,0:T(8,128)(2,1)S(1)}, u32[]{:S(2)}, u32[]{:S(2)}) collective-permute-start(bf16[528,256]{1,0:T(8,128)(2,1)S(1)} %shard_map.90.own), channel_id=1, source_target_pairs={{0,4},{1,3},{2,6},{3,1},{4,0},{5,7},{6,2},{7,5},{8,12},{9,11},{10,... | collective-permute-start | bytes 811016 | tf_op jit(solution)/shard_map/ppermute | solution.py:356
  18.0 0.8 %collective-permute-done.4.refs_1_ = bf16[400,256]{1,0:T(8,128)(2,1)S(1)} collective-permute-done((bf16[400,256]{1,0:T(8,128)(2,1)S(1)}, bf16[400,256]{1,0:T(8,128)(2,1)S(1)}, u32[]{:S(2)}, u32[]{:S(2)}) %collective-permute-start.4) | collective-permute-done | bytes 204832 | tf_op jit(solution)/shard_map/ppermute | solution.py:356
  18.8 0.1 collective-permute-start.8
  18.9 1.6 %collective-permute-start.5 = (bf16[528,256]{1,0:T(8,128)(2,1)S(1)}, bf16[528,256]{1,0:T(8,128)(2,1)S(1)}, u32[]{:S(2)}, u32[]{:S(2)}) collective-permute-start(bf16[528,256]{1,0:T(8,128)(2,1)S(1)} %shard_map.88.one), channel_id=1, source_target_pairs={{0,4},{1,3},{2,6},{3,1},{4,0},{5,7},{6,2},{7,5},{8,12},{9,11},{10,... | collective-permute-start | bytes 811016 | tf_op jit(solution)/shard_map/ppermute | solution.py:356
  20.5 2.4 %collective-permute-done.7.two = bf16[528,256]{1,0:T(8,128)(2,1)S(1)} collective-permute-done((bf16[528,256]{1,0:T(8,128)(2,1)S(1)}, bf16[528,256]{1,0:T(8,128)(2,1)S(1)}, u32[]{:S(2)}, u32[]{:S(2)}) %collective-permute-start.7) | collective-permute-done | bytes 270368 | tf_op jit(solution)/shard_map/ppermute | solution.py:356
  22.9 0.0 collective-permute-start.10
  22.9 1.8 %shard_map.92 = (f32[2048,256]{1,0:T(8,128)S(1)}, f32[2048,256]{1,0:T(8,128)S(1)}, f32[2048,256]{1,0:T(8,128)S(1)}) custom-call(bf16[528,256]{1,0:T(8,128)(2,1)S(1)} %shard_map.88.one, bf16[528,256]{1,0:T(8,128)(2,1)S(1)} %collective-permute-done.7.two, bf16[528,256]{1,0:T(8,128)(2,1)S(1)} %collective-permute-done.8.one_c, ...), custom_call_target="tpu_custom_call" | custom-call | flops 1610612736 | bytes 10485760 | tf_op jit(solution)/shard_map/pallas_call | solution.py:257
  24.8 1.1 %collective-permute-done.5.diag = bf16[528,256]{1,0:T(8,128)(2,1)S(1)} collective-permute-done((bf16[528,256]{1,0:T(8,128)(2,1)S(1)}, bf16[528,256]{1,0:T(8,128)(2,1)S(1)}, u32[]{:S(2)}, u32[]{:S(2)}) %collective-permute-start.5) | collective-permute-done | bytes 270368 | tf_op jit(solution)/shard_map/ppermute | solution.py:356
  25.8 1.3 %shard_map.93 = (f32[2048,256]{1,0:T(8,128)S(1)}, f32[2048,256]{1,0:T(8,128)S(1)}) custom-call(bf16[528,256]{1,0:T(8,128)(2,1)S(1)} %collective-permute-done.5.diag, bf16[528,256]{1,0:T(8,128)(2,1)S(1)} %collective-permute-done.10.two_c, f32[2048,256]{1,0:T(8,128)S(1)} %get-tuple-element.34.near, f32[2048,256]{1,0:T(8,128)S(1)} %get-tuple-element.36.side), custom_call_target="tpu_custom_call" | custom-call | flops 1073741824 | bytes 8388608 | tf_op jit(solution)/shard_map/pallas_call | solution.py:257
  27.1 0.2 collective-permute-done.9.last
  27.4 3.2 %shard_map.94 = (f32[4096,256]{1,0:T(8,128)}, f32[32,128]{1,0:T(8,128)}) custom-call(s32[1,16]{1,0:T(1,128)S(1)} %copy-done.1, bf16[528,256]{1,0:T(8,128)(2,1)S(1)} %collective-permute-done.9.last, f32[2048,256]{1,0:T(8,128)S(1)} %get-tuple-element.37.mine, f32[2048,256]{1,0:T(8,128)S(1)} %get-tuple-element.38.near, ...), custom_call_target="tpu_custom_call", output_to_operand_aliasing={{0}: (8, {})} | custom-call | tf_op jit(solution)/shard_map/pallas_call | solution.py:320
  (11 shorter events, 0.1 us)
Async XLA Ops:
  1.9 10.9 %collective-permute-start.1 = (bf16[144,256]{1,0:T(8,128)(2,1)S(1)}, bf16[144,256]{1,0:T(8,128)(2,1)S(1)}, u32[]{:S(2)}, u32[]{:S(2)}) collective-permute-start(bf16[144,256]{1,0:T(8,128)(2,1)S(1)} %get-tuple-element.24), channel_id=1, source_target_pairs={{0,16},{1,17},{2,18},{3,19},{4,20},{5,21},{6,22},{7,23},{8,24},{9,... | collective-permute-start | bytes 221192 | tf_op jit(solution)/shard_map/ppermute | solution.py:356
  6.0 6.8 %collective-permute-start.2 = (bf16[144,256]{1,0:T(8,128)(2,1)S(1)}, bf16[144,256]{1,0:T(8,128)(2,1)S(1)}, u32[]{:S(2)}, u32[]{:S(2)}) collective-permute-start(bf16[144,256]{1,0:T(8,128)(2,1)S(1)} %get-tuple-element.25), channel_id=1, source_target_pairs={{0,24},{1,25},{2,26},{3,27},{4,28},{5,29},{6,30},{7,31},{8,16},{9,... | collective-permute-start | bytes 221192 | tf_op jit(solution)/shard_map/ppermute | solution.py:356
  7.4 5.5 %collective-permute-start.3 = (bf16[144,256]{1,0:T(8,128)(2,1)S(1)}, bf16[144,256]{1,0:T(8,128)(2,1)S(1)}, u32[]{:S(2)}, u32[]{:S(2)}) collective-permute-start(bf16[144,256]{1,0:T(8,128)(2,1)S(1)} %get-tuple-element.26), channel_id=1, source_target_pairs={{0,8},{1,9},{2,10},{3,11},{4,12},{5,13},{6,14},{7,15},{8,0},{9,1},... | collective-permute-start | bytes 221192 | tf_op jit(solution)/shard_map/ppermute | solution.py:356
  7.6 7.0 %copy-start = (f32[4096]{0:T(1024)S(1)}, f32[4096]{0:T(1024)}, u32[]{:S(2)}) copy-start(f32[4096]{0:T(1024)} %param.13) | copy-start | bytes 49156
  7.6 7.0 %copy-start.1 = (s32[1,16]{1,0:T(1,128)S(1)}, s32[1,16]{1,0:T(1,128)}, u32[]{:S(2)}) copy-start(s32[1,16]{1,0:T(1,128)} %blocks_ref.5) | copy-start | bytes 196
  7.6 5.3 %collective-permute-start = (bf16[144,256]{1,0:T(8,128)(2,1)S(1)}, bf16[144,256]{1,0:T(8,128)(2,1)S(1)}, u32[]{:S(2)}, u32[]{:S(2)}) collective-permute-start(bf16[144,256]{1,0:T(8,128)(2,1)S(1)} %get-tuple-element.29.refs_0_), channel_id=1, source_target_pairs={{0,2},{1,5},{2,0},{3,7},{4,6},{5,1},{6,4},{7,3},{8,10},{9,13},{10,... | collective-permute-start | bytes 221192 | tf_op jit(solution)/shard_map/ppermute | solution.py:356
  12.9 1.7 %collective-permute-start.6 = (bf16[528,256]{1,0:T(8,128)(2,1)S(1)}, bf16[528,256]{1,0:T(8,128)(2,1)S(1)}, u32[]{:S(2)}, u32[]{:S(2)}) collective-permute-start(bf16[528,256]{1,0:T(8,128)(2,1)S(1)} %shard_map.90.own), channel_id=1, source_target_pairs={{0,1},{1,0},{2,3},{3,2},{4,5},{5,4},{6,7},{7,6},{8,9},{9,8},{10,11... | collective-permute-start | bytes 811016 | tf_op jit(solution)/shard_map/ppermute | solution.py:356
  13.0 5.8 %collective-permute-start.4 = (bf16[400,256]{1,0:T(8,128)(2,1)S(1)}, bf16[400,256]{1,0:T(8,128)(2,1)S(1)}, u32[]{:S(2)}, u32[]{:S(2)}) collective-permute-start(bf16[400,256]{1,0:T(8,128)(2,1)S(1)} %shard_map.87), channel_id=1, source_target_pairs={{0,2},{1,5},{2,0},{3,7},{4,6},{5,1},{6,4},{7,3},{8,10},{9,13},{10,... | collective-permute-start | bytes 614408 | tf_op jit(solution)/shard_map/ppermute | solution.py:356
  16.4 6.5 %collective-permute-start.7 = (bf16[528,256]{1,0:T(8,128)(2,1)S(1)}, bf16[528,256]{1,0:T(8,128)(2,1)S(1)}, u32[]{:S(2)}, u32[]{:S(2)}) collective-permute-start(bf16[528,256]{1,0:T(8,128)(2,1)S(1)} %shard_map.90.own), channel_id=1, source_target_pairs={{0,4},{1,3},{2,6},{3,1},{4,0},{5,7},{6,2},{7,5},{8,12},{9,11},{10,... | collective-permute-start | bytes 811016 | tf_op jit(solution)/shard_map/ppermute | solution.py:356
  18.8 4.1 %collective-permute-start.8 = (bf16[528,256]{1,0:T(8,128)(2,1)S(1)}, bf16[528,256]{1,0:T(8,128)(2,1)S(1)}, u32[]{:S(2)}, u32[]{:S(2)}) collective-permute-start(bf16[528,256]{1,0:T(8,128)(2,1)S(1)} %shard_map.88.one), channel_id=1, source_target_pairs={{0,1},{1,0},{2,3},{3,2},{4,5},{5,4},{6,7},{7,6},{8,9},{9,8},{10,11... | collective-permute-start | bytes 811016 | tf_op jit(solution)/shard_map/ppermute | solution.py:356
  18.9 6.9 %collective-permute-start.5 = (bf16[528,256]{1,0:T(8,128)(2,1)S(1)}, bf16[528,256]{1,0:T(8,128)(2,1)S(1)}, u32[]{:S(2)}, u32[]{:S(2)}) collective-permute-start(bf16[528,256]{1,0:T(8,128)(2,1)S(1)} %shard_map.88.one), channel_id=1, source_target_pairs={{0,4},{1,3},{2,6},{3,1},{4,0},{5,7},{6,2},{7,5},{8,12},{9,11},{10,... | collective-permute-start | bytes 811016 | tf_op jit(solution)/shard_map/ppermute | solution.py:356
  22.9 2.9 %collective-permute-start.10 = (bf16[528,256]{1,0:T(8,128)(2,1)S(1)}, bf16[528,256]{1,0:T(8,128)(2,1)S(1)}, u32[]{:S(2)}, u32[]{:S(2)}) collective-permute-start(bf16[528,256]{1,0:T(8,128)(2,1)S(1)} %collective-permute-done.7.two), channel_id=1, source_target_pairs={{0,1},{1,0},{2,3},{3,2},{4,5},{5,4},{6,7},{7,6},{8,9},{9,8},{10,11... | collective-permute-start | bytes 811016 | tf_op jit(solution)/shard_map/ppermute | solution.py:356
  25.8 1.5 %collective-permute-start.9 = (bf16[528,256]{1,0:T(8,128)(2,1)S(1)}, bf16[528,256]{1,0:T(8,128)(2,1)S(1)}, u32[]{:S(2)}, u32[]{:S(2)}) collective-permute-start(bf16[528,256]{1,0:T(8,128)(2,1)S(1)} %collective-permute-done.5.diag), channel_id=1, source_target_pairs={{0,1},{1,0},{2,3},{3,2},{4,5},{5,4},{6,7},{7,6},{8,9},{9,8},{10,11... | collective-permute-start | bytes 811016 | tf_op jit(solution)/shard_map/ppermute | solution.py:356

commit v9 on v8

--- a/solution.py
+++ b/solution.py
@@ -55,26 +55,26 @@
 
     copies[0].wait()
     copies[1].wait()
-    total = picks(0)
-    for o in range(1, owners):
-        total = total + picks(o)
-    lengths = jnp.sum(total, axis=1, keepdims=True)
-    copies[2].wait()
-    scaled = (grad_ref[...].astype(F32) * (1.0 / jnp.maximum(lengths, 1.0))).astype(BF16)
+    chosen = [picks(me ^ j) for j in range(owners)]
+    lengths = jnp.sum(sum(chosen), axis=1, keepdims=True)
+    share = 1.0 / jnp.maximum(lengths, 1.0)
+    chosen = [c.astype(BF16) for c in chosen]
     copies[3].wait()
     tail_row = lax.broadcasted_iota(jnp.int32, (TAIL, cap), 0)
     for j in range(owners):
-        o = me ^ j
-        values = lax.dot_general(
-            picks(o).astype(BF16), scaled, (((0,), (0,)), ((), ())), preferred_element_type=F32
-        )
-        out_refs[j][0:cap, :] = values.astype(BF16)
-        row = row_ref[pl.ds(o, 1), :]
+        row = row_ref[pl.ds(me ^ j, 1), :]
         slot = row // TILE
         within = row - slot * TILE
         tail = jnp.where(tail_row == 0, slot, jnp.where(tail_row == 1, within, 0))
         out_refs[j][cap : cap + TAIL, :] = jnp.zeros((TAIL, cols), BF16)
         out_refs[j][cap : cap + TAIL, 0:cap] = tail.astype(F32).astype(BF16)
+    copies[2].wait()
+    scaled = (grad_ref[...].astype(F32) * share).astype(BF16)
+    for j in range(owners):
+        values = lax.dot_general(
+            chosen[j], scaled, (((0,), (0,)), ((), ())), preferred_element_type=F32
+        )
+        out_refs[j][0:cap, :] = values.astype(BF16)
 
 
 def pack(count, grad, sample, row):

time: 30.7 us -> 30.7 us (level)
  no operation moved by 1% of the time
where the time goes in v9:
time: 30.7 us; the launch traced here: 30.5 us
  Pallas kernels  13.2 us (43%)
  starting transfers between devices  12.1 us (39%)
  waiting for transfers between devices  4.53 us (15%)
  between operations  0.75 us (2%)
    ppermute x11, starting transfers between devices, swap(): return lax.ppermute(x, ('shard', 'rep'), pairs)  12.1 us
    ppermute x11, waiting for transfers between devices, swap(): return lax.ppermute(x, ('shard', 'rep'), pairs)  4.53 us
    pallas_call x1, Pallas kernels, load(): pl.pallas_call(load_kernel, out_shape=[VMEM(table.shape, F32), jax.ShapeD...  3.71 us
    pallas_call x1, Pallas kernels, update(): pl.pallas_call(functools.partial(update_kernel, cap), out_shape=[jax.Shap...  3.18 us
    pallas_call x2, Pallas kernels, sum_call(): pl.pallas_call(functools.partial(kernel, cap), out_shape=[wide] * results...  3.12 us
    pallas_call x1, Pallas kernels, own_sum(): pl.pallas_call(functools.partial(own_kernel, cap), out_shape=[jax.ShapeDt...  1.8 us
    pallas_call x1, Pallas kernels, pack(): pl.pallas_call(pack_kernel, out_shape=[shape] * owners, in_specs=[whole(p...  1.28 us
  transfers between devices with their start and end apart: 11, of which 4 were waited for; matrix products, arithmetic and copies ran while one was open for 0% of the time, Pallas kernels for 29%

profile of v9, /device:TPU:0, one launch (start us, length us, event | category | flops | bytes accessed | tf_op | source)
XLA Modules:
  0.0 30.5 jit_solution(13581810293165496565)
XLA Ops:
  0.6 1.3 %shard_map.86 = (bf16[144,256]{1,0:T(8,128)(2,1)S(1)}, bf16[144,256]{1,0:T(8,128)(2,1)S(1)}, bf16[144,256]{1,0:T(8,128)(2,1)S(1)}, bf16[144,256]{1,0:T(8,128)(2,1)S(1)}) custom-call(s32[4]{0:T(128)} %count_in.1, bf16[256,256]{1,0:T(8,128)(2,1)} %grad_in.1, s32[4,128]{1,0:T(4,128)} %sample_in.1, s32[4,128]{1,0:T(4,128)} %row_in.1), custom_call_target="tpu_custom_call" | custom-call | tf_op jit(solution)/shard_map/pallas_call | solution.py:83
  1.9 4.1 %collective-permute-start.1 = (bf16[144,256]{1,0:T(8,128)(2,1)S(1)}, bf16[144,256]{1,0:T(8,128)(2,1)S(1)}, u32[]{:S(2)}, u32[]{:S(2)}) collective-permute-start(bf16[144,256]{1,0:T(8,128)(2,1)S(1)} %get-tuple-element.24), channel_id=1, source_target_pairs={{0,16},{1,17},{2,18},{3,19},{4,20},{5,21},{6,22},{7,23},{8,24},{9,... | collective-permute-start | bytes 221192 | tf_op jit(solution)/shard_map/ppermute | solution.py:356
  6.0 1.3 %collective-permute-start.2 = (bf16[144,256]{1,0:T(8,128)(2,1)S(1)}, bf16[144,256]{1,0:T(8,128)(2,1)S(1)}, u32[]{:S(2)}, u32[]{:S(2)}) collective-permute-start(bf16[144,256]{1,0:T(8,128)(2,1)S(1)} %get-tuple-element.25), channel_id=1, source_target_pairs={{0,24},{1,25},{2,26},{3,27},{4,28},{5,29},{6,30},{7,31},{8,16},{9,... | collective-permute-start | bytes 221192 | tf_op jit(solution)/shard_map/ppermute | solution.py:356
  7.4 0.2 collective-permute-start.3
  7.6 1.5 %collective-permute-start = (bf16[144,256]{1,0:T(8,128)(2,1)S(1)}, bf16[144,256]{1,0:T(8,128)(2,1)S(1)}, u32[]{:S(2)}, u32[]{:S(2)}) collective-permute-start(bf16[144,256]{1,0:T(8,128)(2,1)S(1)} %get-tuple-element.29.refs_0_), channel_id=1, source_target_pairs={{0,2},{1,5},{2,0},{3,7},{4,6},{5,1},{6,4},{7,3},{8,10},{9,13},{10,... | collective-permute-start | bytes 221192 | tf_op jit(solution)/shard_map/ppermute | solution.py:356
  9.1 3.7 %shard_map.89 = (f32[4096,256]{1,0:T(8,128)S(1)}, f32[4096,256]{1,0:T(8,128)}) custom-call(s32[1,16]{1,0:T(1,128)} %blocks_ref.5, f32[4096,256]{1,0:T(8,128)} %table_in), custom_call_target="tpu_custom_call" | custom-call | bytes 12582912 | tf_op jit(solution)/shard_map/pallas_call | solution.py:195
  12.8 0.0 collective-permute-done.1.refs_0_.refs_1_
  12.8 0.0 collective-permute-done.2.refs_1_.refs_2_
  12.9 0.0 collective-permute-done.refs_0_
  12.9 0.1 collective-permute-start.6
  13.0 1.6 %collective-permute-start.4 = (bf16[400,256]{1,0:T(8,128)(2,1)S(1)}, bf16[400,256]{1,0:T(8,128)(2,1)S(1)}, u32[]{:S(2)}, u32[]{:S(2)}) collective-permute-start(bf16[400,256]{1,0:T(8,128)(2,1)S(1)} %shard_map.87), channel_id=1, source_target_pairs={{0,2},{1,5},{2,0},{3,7},{4,6},{5,1},{6,4},{7,3},{8,10},{9,13},{10,... | collective-permute-start | bytes 614408 | tf_op jit(solution)/shard_map/ppermute | solution.py:356
  14.6 1.8 %shard_map.91 = (f32[2048,256]{1,0:T(8,128)S(1)}, f32[2048,256]{1,0:T(8,128)S(1)}, f32[2048,128]{1,0:T(8,128)S(1)}) custom-call(s32[1,16]{1,0:T(1,128)S(1)} %copy-done.1, bf16[528,256]{1,0:T(8,128)(2,1)S(1)} %shard_map.90.own, bf16[528,256]{1,0:T(8,128)(2,1)S(1)} %collective-permute-done.6.own_c, f32[32,128]{1,0:T(8,128)S(1)} %bitcast.2), custom_call_target="tpu_custom_call" | custom-call | flops 536870912 | bytes 2097152 | tf_op jit(solution)/shard_map/pallas_call | solution.py:221
  16.4 1.6 %collective-permute-start.7 = (bf16[528,256]{1,0:T(8,128)(2,1)S(1)}, bf16[528,256]{1,0:T(8,128)(2,1)S(1)}, u32[]{:S(2)}, u32[]{:S(2)}) collective-permute-start(bf16[528,256]{1,0:T(8,128)(2,1)S(1)} %shard_map.90.own), channel_id=1, source_target_pairs={{0,4},{1,3},{2,6},{3,1},{4,0},{5,7},{6,2},{7,5},{8,12},{9,11},{10,... | collective-permute-start | bytes 811016 | tf_op jit(solution)/shard_map/ppermute | solution.py:356
  18.0 0.8 %collective-permute-done.4.refs_1_ = bf16[400,256]{1,0:T(8,128)(2,1)S(1)} collective-permute-done((bf16[400,256]{1,0:T(8,128)(2,1)S(1)}, bf16[400,256]{1,0:T(8,128)(2,1)S(1)}, u32[]{:S(2)}, u32[]{:S(2)}) %collective-permute-start.4) | collective-permute-done | bytes 204832 | tf_op jit(solution)/shard_map/ppermute | solution.py:356
  18.8 0.1 collective-permute-start.8
  18.9 1.6 %collective-permute-start.5 = (bf16[528,256]{1,0:T(8,128)(2,1)S(1)}, bf16[528,256]{1,0:T(8,128)(2,1)S(1)}, u32[]{:S(2)}, u32[]{:S(2)}) collective-permute-start(bf16[528,256]{1,0:T(8,128)(2,1)S(1)} %shard_map.88.one), channel_id=1, source_target_pairs={{0,4},{1,3},{2,6},{3,1},{4,0},{5,7},{6,2},{7,5},{8,12},{9,11},{10,... | collective-permute-start | bytes 811016 | tf_op jit(solution)/shard_map/ppermute | solution.py:356
  20.5 2.4 %collective-permute-done.7.two = bf16[528,256]{1,0:T(8,128)(2,1)S(1)} collective-permute-done((bf16[528,256]{1,0:T(8,128)(2,1)S(1)}, bf16[528,256]{1,0:T(8,128)(2,1)S(1)}, u32[]{:S(2)}, u32[]{:S(2)}) %collective-permute-start.7) | collective-permute-done | bytes 270368 | tf_op jit(solution)/shard_map/ppermute | solution.py:356
  22.9 0.0 collective-permute-start.10
  22.9 0.0 collective-permute-done.8.one_c
  22.9 1.8 %shard_map.92 = (f32[2048,256]{1,0:T(8,128)S(1)}, f32[2048,256]{1,0:T(8,128)S(1)}, f32[2048,256]{1,0:T(8,128)S(1)}) custom-call(bf16[528,256]{1,0:T(8,128)(2,1)S(1)} %shard_map.88.one, bf16[528,256]{1,0:T(8,128)(2,1)S(1)} %collective-permute-done.7.two, bf16[528,256]{1,0:T(8,128)(2,1)S(1)} %collective-permute-done.8.one_c, ...), custom_call_target="tpu_custom_call" | custom-call | flops 1610612736 | bytes 10485760 | tf_op jit(solution)/shard_map/pallas_call | solution.py:257
  24.7 1.1 %collective-permute-done.5.diag = bf16[528,256]{1,0:T(8,128)(2,1)S(1)} collective-permute-done((bf16[528,256]{1,0:T(8,128)(2,1)S(1)}, bf16[528,256]{1,0:T(8,128)(2,1)S(1)}, u32[]{:S(2)}, u32[]{:S(2)}) %collective-permute-start.5) | collective-permute-done | bytes 270368 | tf_op jit(solution)/shard_map/ppermute | solution.py:356
  25.8 1.3 %shard_map.93 = (f32[2048,256]{1,0:T(8,128)S(1)}, f32[2048,256]{1,0:T(8,128)S(1)}) custom-call(bf16[528,256]{1,0:T(8,128)(2,1)S(1)} %collective-permute-done.5.diag, bf16[528,256]{1,0:T(8,128)(2,1)S(1)} %collective-permute-done.10.two_c, f32[2048,256]{1,0:T(8,128)S(1)} %get-tuple-element.34.near, f32[2048,256]{1,0:T(8,128)S(1)} %get-tuple-element.36.side), custom_call_target="tpu_custom_call" | custom-call | flops 1073741824 | bytes 8388608 | tf_op jit(solution)/shard_map/pallas_call | solution.py:257
  27.1 0.2 collective-permute-done.9.last
  27.3 3.2 %shard_map.94 = (f32[4096,256]{1,0:T(8,128)}, f32[32,128]{1,0:T(8,128)}) custom-call(s32[1,16]{1,0:T(1,128)S(1)} %copy-done.1, bf16[528,256]{1,0:T(8,128)(2,1)S(1)} %collective-permute-done.9.last, f32[2048,256]{1,0:T(8,128)S(1)} %get-tuple-element.37.mine, f32[2048,256]{1,0:T(8,128)S(1)} %get-tuple-element.38.near, ...), custom_call_target="tpu_custom_call", output_to_operand_aliasing={{0}: (8, {})} | custom-call | tf_op jit(solution)/shard_map/pallas_call | solution.py:320
  (11 shorter events, 0.1 us)
Async XLA Ops:
  1.9 10.9 %collective-permute-start.1 = (bf16[144,256]{1,0:T(8,128)(2,1)S(1)}, bf16[144,256]{1,0:T(8,128)(2,1)S(1)}, u32[]{:S(2)}, u32[]{:S(2)}) collective-permute-start(bf16[144,256]{1,0:T(8,128)(2,1)S(1)} %get-tuple-element.24), channel_id=1, source_target_pairs={{0,16},{1,17},{2,18},{3,19},{4,20},{5,21},{6,22},{7,23},{8,24},{9,... | collective-permute-start | bytes 221192 | tf_op jit(solution)/shard_map/ppermute | solution.py:356
  6.0 6.8 %collective-permute-start.2 = (bf16[144,256]{1,0:T(8,128)(2,1)S(1)}, bf16[144,256]{1,0:T(8,128)(2,1)S(1)}, u32[]{:S(2)}, u32[]{:S(2)}) collective-permute-start(bf16[144,256]{1,0:T(8,128)(2,1)S(1)} %get-tuple-element.25), channel_id=1, source_target_pairs={{0,24},{1,25},{2,26},{3,27},{4,28},{5,29},{6,30},{7,31},{8,16},{9,... | collective-permute-start | bytes 221192 | tf_op jit(solution)/shard_map/ppermute | solution.py:356
  7.4 5.5 %collective-permute-start.3 = (bf16[144,256]{1,0:T(8,128)(2,1)S(1)}, bf16[144,256]{1,0:T(8,128)(2,1)S(1)}, u32[]{:S(2)}, u32[]{:S(2)}) collective-permute-start(bf16[144,256]{1,0:T(8,128)(2,1)S(1)} %get-tuple-element.26), channel_id=1, source_target_pairs={{0,8},{1,9},{2,10},{3,11},{4,12},{5,13},{6,14},{7,15},{8,0},{9,1},... | collective-permute-start | bytes 221192 | tf_op jit(solution)/shard_map/ppermute | solution.py:356
  7.6 7.0 %copy-start = (f32[4096]{0:T(1024)S(1)}, f32[4096]{0:T(1024)}, u32[]{:S(2)}) copy-start(f32[4096]{0:T(1024)} %param.13) | copy-start | bytes 49156
  7.6 7.0 %copy-start.1 = (s32[1,16]{1,0:T(1,128)S(1)}, s32[1,16]{1,0:T(1,128)}, u32[]{:S(2)}) copy-start(s32[1,16]{1,0:T(1,128)} %blocks_ref.5) | copy-start | bytes 196
  7.6 5.3 %collective-permute-start = (bf16[144,256]{1,0:T(8,128)(2,1)S(1)}, bf16[144,256]{1,0:T(8,128)(2,1)S(1)}, u32[]{:S(2)}, u32[]{:S(2)}) collective-permute-start(bf16[144,256]{1,0:T(8,128)(2,1)S(1)} %get-tuple-element.29.refs_0_), channel_id=1, source_target_pairs={{0,2},{1,5},{2,0},{3,7},{4,6},{5,1},{6,4},{7,3},{8,10},{9,13},{10,... | collective-permute-start | bytes 221192 | tf_op jit(solution)/shard_map/ppermute | solution.py:356
  12.9 1.7 %collective-permute-start.6 = (bf16[528,256]{1,0:T(8,128)(2,1)S(1)}, bf16[528,256]{1,0:T(8,128)(2,1)S(1)}, u32[]{:S(2)}, u32[]{:S(2)}) collective-permute-start(bf16[528,256]{1,0:T(8,128)(2,1)S(1)} %shard_map.90.own), channel_id=1, source_target_pairs={{0,1},{1,0},{2,3},{3,2},{4,5},{5,4},{6,7},{7,6},{8,9},{9,8},{10,11... | collective-permute-start | bytes 811016 | tf_op jit(solution)/shard_map/ppermute | solution.py:356
  13.0 5.8 %collective-permute-start.4 = (bf16[400,256]{1,0:T(8,128)(2,1)S(1)}, bf16[400,256]{1,0:T(8,128)(2,1)S(1)}, u32[]{:S(2)}, u32[]{:S(2)}) collective-permute-start(bf16[400,256]{1,0:T(8,128)(2,1)S(1)} %shard_map.87), channel_id=1, source_target_pairs={{0,2},{1,5},{2,0},{3,7},{4,6},{5,1},{6,4},{7,3},{8,10},{9,13},{10,... | collective-permute-start | bytes 614408 | tf_op jit(solution)/shard_map/ppermute | solution.py:356
  16.4 6.5 %collective-permute-start.7 = (bf16[528,256]{1,0:T(8,128)(2,1)S(1)}, bf16[528,256]{1,0:T(8,128)(2,1)S(1)}, u32[]{:S(2)}, u32[]{:S(2)}) collective-permute-start(bf16[528,256]{1,0:T(8,128)(2,1)S(1)} %shard_map.90.own), channel_id=1, source_target_pairs={{0,4},{1,3},{2,6},{3,1},{4,0},{5,7},{6,2},{7,5},{8,12},{9,11},{10,... | collective-permute-start | bytes 811016 | tf_op jit(solution)/shard_map/ppermute | solution.py:356
  18.8 4.1 %collective-permute-start.8 = (bf16[528,256]{1,0:T(8,128)(2,1)S(1)}, bf16[528,256]{1,0:T(8,128)(2,1)S(1)}, u32[]{:S(2)}, u32[]{:S(2)}) collective-permute-start(bf16[528,256]{1,0:T(8,128)(2,1)S(1)} %shard_map.88.one), channel_id=1, source_target_pairs={{0,1},{1,0},{2,3},{3,2},{4,5},{5,4},{6,7},{7,6},{8,9},{9,8},{10,11... | collective-permute-start | bytes 811016 | tf_op jit(solution)/shard_map/ppermute | solution.py:356
  18.9 6.9 %collective-permute-start.5 = (bf16[528,256]{1,0:T(8,128)(2,1)S(1)}, bf16[528,256]{1,0:T(8,128)(2,1)S(1)}, u32[]{:S(2)}, u32[]{:S(2)}) collective-permute-start(bf16[528,256]{1,0:T(8,128)(2,1)S(1)} %shard_map.88.one), channel_id=1, source_target_pairs={{0,4},{1,3},{2,6},{3,1},{4,0},{5,7},{6,2},{7,5},{8,12},{9,11},{10,... | collective-permute-start | bytes 811016 | tf_op jit(solution)/shard_map/ppermute | solution.py:356
  22.9 2.9 %collective-permute-start.10 = (bf16[528,256]{1,0:T(8,128)(2,1)S(1)}, bf16[528,256]{1,0:T(8,128)(2,1)S(1)}, u32[]{:S(2)}, u32[]{:S(2)}) collective-permute-start(bf16[528,256]{1,0:T(8,128)(2,1)S(1)} %collective-permute-done.7.two), channel_id=1, source_target_pairs={{0,1},{1,0},{2,3},{3,2},{4,5},{5,4},{6,7},{7,6},{8,9},{9,8},{10,11... | collective-permute-start | bytes 811016 | tf_op jit(solution)/shard_map/ppermute | solution.py:356
  25.8 1.5 %collective-permute-start.9 = (bf16[528,256]{1,0:T(8,128)(2,1)S(1)}, bf16[528,256]{1,0:T(8,128)(2,1)S(1)}, u32[]{:S(2)}, u32[]{:S(2)}) collective-permute-start(bf16[528,256]{1,0:T(8,128)(2,1)S(1)} %collective-permute-done.5.diag), channel_id=1, source_target_pairs={{0,1},{1,0},{2,3},{3,2},{4,5},{5,4},{6,7},{7,6},{8,9},{9,8},{10,11... | collective-permute-start | bytes 811016 | tf_op jit(solution)/shard_map/ppermute | solution.py:356

commit v10 on v9

--- a/solution.py
+++ b/solution.py
@@ -356,10 +356,10 @@
         return lax.ppermute(x, ("shard", "rep"), pairs)
 
     def first(x):
+        return swap(x, lambda r: (0, 4 if r % 2 == 0 else 2))
+
+    def second(x):
         return swap(x, lambda r: (0, 2 if r % 2 == 0 else 4))
-
-    def second(x):
-        return swap(x, lambda r: (0, 4 if r % 2 == 0 else 2))
 
     def core(x):
         return swap(x, lambda r: (0, 1))

time: 30.7 us -> 30.7 us (level)
  transfers between devices with their start and end apart: 11 -> 11, of which waited for: 4 -> 4; matrix products, arithmetic and copies ran while one was open for 0% -> 0% of each run, Pallas kernels for 29% -> 28%
where the time goes in v10:
time: 30.7 us; the launch traced here: 30.6 us
  Pallas kernels  13.1 us (43%)
  starting transfers between devices  12.1 us (39%)
  waiting for transfers between devices  4.59 us (15%)
  between operations  0.75 us (2%)
    ppermute x11, starting transfers between devices, swap(): return lax.ppermute(x, ('shard', 'rep'), pairs)  12.1 us
    ppermute x11, waiting for transfers between devices, swap(): return lax.ppermute(x, ('shard', 'rep'), pairs)  4.59 us
    pallas_call x1, Pallas kernels, load(): pl.pallas_call(load_kernel, out_shape=[VMEM(table.shape, F32), jax.ShapeD...  3.66 us
    pallas_call x1, Pallas kernels, update(): pl.pallas_call(functools.partial(update_kernel, cap), out_shape=[jax.Shap...  3.18 us
    pallas_call x2, Pallas kernels, sum_call(): pl.pallas_call(functools.partial(kernel, cap), out_shape=[wide] * results...  3.12 us
    pallas_call x1, Pallas kernels, own_sum(): pl.pallas_call(functools.partial(own_kernel, cap), out_shape=[jax.ShapeDt...  1.8 us
    pallas_call x1, Pallas kernels, pack(): pl.pallas_call(pack_kernel, out_shape=[shape] * owners, in_specs=[whole(p...  1.28 us
  transfers between devices with their start and end apart: 11, of which 4 were waited for; matrix products, arithmetic and copies ran while one was open for 0% of the time, Pallas kernels for 28%

profile of v10, /device:TPU:0, one launch (start us, length us, event | category | flops | bytes accessed | tf_op | source)
XLA Modules:
  0.0 30.6 jit_solution(4767192492642037458)
XLA Ops:
  0.6 1.3 %shard_map.86 = (bf16[144,256]{1,0:T(8,128)(2,1)S(1)}, bf16[144,256]{1,0:T(8,128)(2,1)S(1)}, bf16[144,256]{1,0:T(8,128)(2,1)S(1)}, bf16[144,256]{1,0:T(8,128)(2,1)S(1)}) custom-call(s32[4]{0:T(128)} %count_in.1, bf16[256,256]{1,0:T(8,128)(2,1)} %grad_in.1, s32[4,128]{1,0:T(4,128)} %sample_in.1, s32[4,128]{1,0:T(4,128)} %row_in.1), custom_call_target="tpu_custom_call" | custom-call | tf_op jit(solution)/shard_map/pallas_call | solution.py:83
  1.9 4.1 %collective-permute-start.1 = (bf16[144,256]{1,0:T(8,128)(2,1)S(1)}, bf16[144,256]{1,0:T(8,128)(2,1)S(1)}, u32[]{:S(2)}, u32[]{:S(2)}) collective-permute-start(bf16[144,256]{1,0:T(8,128)(2,1)S(1)} %get-tuple-element.24), channel_id=1, source_target_pairs={{0,16},{1,17},{2,18},{3,19},{4,20},{5,21},{6,22},{7,23},{8,24},{9,... | collective-permute-start | bytes 221192 | tf_op jit(solution)/shard_map/ppermute | solution.py:356
  6.0 1.3 %collective-permute-start.2 = (bf16[144,256]{1,0:T(8,128)(2,1)S(1)}, bf16[144,256]{1,0:T(8,128)(2,1)S(1)}, u32[]{:S(2)}, u32[]{:S(2)}) collective-permute-start(bf16[144,256]{1,0:T(8,128)(2,1)S(1)} %get-tuple-element.25), channel_id=1, source_target_pairs={{0,24},{1,25},{2,26},{3,27},{4,28},{5,29},{6,30},{7,31},{8,16},{9,... | collective-permute-start | bytes 221192 | tf_op jit(solution)/shard_map/ppermute | solution.py:356
  7.4 0.2 collective-permute-start.3
  7.6 1.5 %collective-permute-start = (bf16[144,256]{1,0:T(8,128)(2,1)S(1)}, bf16[144,256]{1,0:T(8,128)(2,1)S(1)}, u32[]{:S(2)}, u32[]{:S(2)}) collective-permute-start(bf16[144,256]{1,0:T(8,128)(2,1)S(1)} %get-tuple-element.29.refs_0_), channel_id=1, source_target_pairs={{0,4},{1,3},{2,6},{3,1},{4,0},{5,7},{6,2},{7,5},{8,12},{9,11},{10,... | collective-permute-start | bytes 221192 | tf_op jit(solution)/shard_map/ppermute | solution.py:356
  9.1 3.7 %shard_map.89 = (f32[4096,256]{1,0:T(8,128)S(1)}, f32[4096,256]{1,0:T(8,128)}) custom-call(s32[1,16]{1,0:T(1,128)} %blocks_ref.5, f32[4096,256]{1,0:T(8,128)} %table_in), custom_call_target="tpu_custom_call" | custom-call | bytes 12582912 | tf_op jit(solution)/shard_map/pallas_call | solution.py:195
  12.8 0.0 collective-permute-done.1.refs_0_.refs_1_
  12.8 0.0 collective-permute-done.3.refs_2_.refs_3_
  12.9 0.0 collective-permute-done.refs_0_
  12.9 0.1 collective-permute-start.6
  13.0 1.6 %collective-permute-start.4 = (bf16[400,256]{1,0:T(8,128)(2,1)S(1)}, bf16[400,256]{1,0:T(8,128)(2,1)S(1)}, u32[]{:S(2)}, u32[]{:S(2)}) collective-permute-start(bf16[400,256]{1,0:T(8,128)(2,1)S(1)} %shard_map.87), channel_id=1, source_target_pairs={{0,4},{1,3},{2,6},{3,1},{4,0},{5,7},{6,2},{7,5},{8,12},{9,11},{10,... | collective-permute-start | bytes 614408 | tf_op jit(solution)/shard_map/ppermute | solution.py:356
  14.6 0.0 collective-permute-done.6.own_c
  14.6 1.8 %shard_map.91 = (f32[2048,256]{1,0:T(8,128)S(1)}, f32[2048,256]{1,0:T(8,128)S(1)}, f32[2048,128]{1,0:T(8,128)S(1)}) custom-call(s32[1,16]{1,0:T(1,128)S(1)} %copy-done.1, bf16[528,256]{1,0:T(8,128)(2,1)S(1)} %shard_map.90.own, bf16[528,256]{1,0:T(8,128)(2,1)S(1)} %collective-permute-done.6.own_c, f32[32,128]{1,0:T(8,128)S(1)} %bitcast.2), custom_call_target="tpu_custom_call" | custom-call | flops 536870912 | bytes 2097152 | tf_op jit(solution)/shard_map/pallas_call | solution.py:221
  16.4 1.6 %collective-permute-start.7 = (bf16[528,256]{1,0:T(8,128)(2,1)S(1)}, bf16[528,256]{1,0:T(8,128)(2,1)S(1)}, u32[]{:S(2)}, u32[]{:S(2)}) collective-permute-start(bf16[528,256]{1,0:T(8,128)(2,1)S(1)} %shard_map.90.own), channel_id=1, source_target_pairs={{0,2},{1,5},{2,0},{3,7},{4,6},{5,1},{6,4},{7,3},{8,10},{9,13},{10,... | collective-permute-start | bytes 811016 | tf_op jit(solution)/shard_map/ppermute | solution.py:356
  18.0 0.8 %collective-permute-done.4.refs_1_ = bf16[400,256]{1,0:T(8,128)(2,1)S(1)} collective-permute-done((bf16[400,256]{1,0:T(8,128)(2,1)S(1)}, bf16[400,256]{1,0:T(8,128)(2,1)S(1)}, u32[]{:S(2)}, u32[]{:S(2)}) %collective-permute-start.4) | collective-permute-done | bytes 204832 | tf_op jit(solution)/shard_map/ppermute | solution.py:356
  18.8 0.1 collective-permute-start.8
  18.9 1.6 %collective-permute-start.5 = (bf16[528,256]{1,0:T(8,128)(2,1)S(1)}, bf16[528,256]{1,0:T(8,128)(2,1)S(1)}, u32[]{:S(2)}, u32[]{:S(2)}) collective-permute-start(bf16[528,256]{1,0:T(8,128)(2,1)S(1)} %shard_map.88.one), channel_id=1, source_target_pairs={{0,2},{1,5},{2,0},{3,7},{4,6},{5,1},{6,4},{7,3},{8,10},{9,13},{10,... | collective-permute-start | bytes 811016 | tf_op jit(solution)/shard_map/ppermute | solution.py:356
  20.5 2.4 %collective-permute-done.7.two = bf16[528,256]{1,0:T(8,128)(2,1)S(1)} collective-permute-done((bf16[528,256]{1,0:T(8,128)(2,1)S(1)}, bf16[528,256]{1,0:T(8,128)(2,1)S(1)}, u32[]{:S(2)}, u32[]{:S(2)}) %collective-permute-start.7) | collective-permute-done | bytes 270368 | tf_op jit(solution)/shard_map/ppermute | solution.py:356
  22.9 0.0 collective-permute-done.8.one_c
  22.9 1.8 %shard_map.92 = (f32[2048,256]{1,0:T(8,128)S(1)}, f32[2048,256]{1,0:T(8,128)S(1)}, f32[2048,256]{1,0:T(8,128)S(1)}) custom-call(bf16[528,256]{1,0:T(8,128)(2,1)S(1)} %shard_map.88.one, bf16[528,256]{1,0:T(8,128)(2,1)S(1)} %collective-permute-done.7.two, bf16[528,256]{1,0:T(8,128)(2,1)S(1)} %collective-permute-done.8.one_c, ...), custom_call_target="tpu_custom_call" | custom-call | flops 1610612736 | bytes 10485760 | tf_op jit(solution)/shard_map/pallas_call | solution.py:257
  24.8 1.1 %collective-permute-done.5.diag = bf16[528,256]{1,0:T(8,128)(2,1)S(1)} collective-permute-done((bf16[528,256]{1,0:T(8,128)(2,1)S(1)}, bf16[528,256]{1,0:T(8,128)(2,1)S(1)}, u32[]{:S(2)}, u32[]{:S(2)}) %collective-permute-start.5) | collective-permute-done | bytes 270368 | tf_op jit(solution)/shard_map/ppermute | solution.py:356
  25.8 1.3 %shard_map.93 = (f32[2048,256]{1,0:T(8,128)S(1)}, f32[2048,256]{1,0:T(8,128)S(1)}) custom-call(bf16[528,256]{1,0:T(8,128)(2,1)S(1)} %collective-permute-done.5.diag, bf16[528,256]{1,0:T(8,128)(2,1)S(1)} %collective-permute-done.10.two_c, f32[2048,256]{1,0:T(8,128)S(1)} %get-tuple-element.34.near, f32[2048,256]{1,0:T(8,128)S(1)} %get-tuple-element.36.side), custom_call_target="tpu_custom_call" | custom-call | flops 1073741824 | bytes 8388608 | tf_op jit(solution)/shard_map/pallas_call | solution.py:257
  27.1 0.2 collective-permute-done.9.last
  27.4 3.2 %shard_map.94 = (f32[4096,256]{1,0:T(8,128)}, f32[32,128]{1,0:T(8,128)}) custom-call(s32[1,16]{1,0:T(1,128)S(1)} %copy-done.1, bf16[528,256]{1,0:T(8,128)(2,1)S(1)} %collective-permute-done.9.last, f32[2048,256]{1,0:T(8,128)S(1)} %get-tuple-element.37.mine, f32[2048,256]{1,0:T(8,128)S(1)} %get-tuple-element.38.near, ...), custom_call_target="tpu_custom_call", output_to_operand_aliasing={{0}: (8, {})} | custom-call | tf_op jit(solution)/shard_map/pallas_call | solution.py:320
  (11 shorter events, 0.1 us)
Async XLA Ops:
  1.9 10.9 %collective-permute-start.1 = (bf16[144,256]{1,0:T(8,128)(2,1)S(1)}, bf16[144,256]{1,0:T(8,128)(2,1)S(1)}, u32[]{:S(2)}, u32[]{:S(2)}) collective-permute-start(bf16[144,256]{1,0:T(8,128)(2,1)S(1)} %get-tuple-element.24), channel_id=1, source_target_pairs={{0,16},{1,17},{2,18},{3,19},{4,20},{5,21},{6,22},{7,23},{8,24},{9,... | collective-permute-start | bytes 221192 | tf_op jit(solution)/shard_map/ppermute | solution.py:356
  6.0 6.8 %collective-permute-start.2 = (bf16[144,256]{1,0:T(8,128)(2,1)S(1)}, bf16[144,256]{1,0:T(8,128)(2,1)S(1)}, u32[]{:S(2)}, u32[]{:S(2)}) collective-permute-start(bf16[144,256]{1,0:T(8,128)(2,1)S(1)} %get-tuple-element.25), channel_id=1, source_target_pairs={{0,24},{1,25},{2,26},{3,27},{4,28},{5,29},{6,30},{7,31},{8,16},{9,... | collective-permute-start | bytes 221192 | tf_op jit(solution)/shard_map/ppermute | solution.py:356
  7.4 5.4 %collective-permute-start.3 = (bf16[144,256]{1,0:T(8,128)(2,1)S(1)}, bf16[144,256]{1,0:T(8,128)(2,1)S(1)}, u32[]{:S(2)}, u32[]{:S(2)}) collective-permute-start(bf16[144,256]{1,0:T(8,128)(2,1)S(1)} %get-tuple-element.26), channel_id=1, source_target_pairs={{0,8},{1,9},{2,10},{3,11},{4,12},{5,13},{6,14},{7,15},{8,0},{9,1},... | collective-permute-start | bytes 221192 | tf_op jit(solution)/shard_map/ppermute | solution.py:356
  7.6 7.0 %copy-start = (f32[4096]{0:T(1024)S(1)}, f32[4096]{0:T(1024)}, u32[]{:S(2)}) copy-start(f32[4096]{0:T(1024)} %param.13) | copy-start | bytes 49156
  7.6 7.0 %copy-start.1 = (s32[1,16]{1,0:T(1,128)S(1)}, s32[1,16]{1,0:T(1,128)}, u32[]{:S(2)}) copy-start(s32[1,16]{1,0:T(1,128)} %blocks_ref.5) | copy-start | bytes 196
  7.6 5.3 %collective-permute-start = (bf16[144,256]{1,0:T(8,128)(2,1)S(1)}, bf16[144,256]{1,0:T(8,128)(2,1)S(1)}, u32[]{:S(2)}, u32[]{:S(2)}) collective-permute-start(bf16[144,256]{1,0:T(8,128)(2,1)S(1)} %get-tuple-element.29.refs_0_), channel_id=1, source_target_pairs={{0,4},{1,3},{2,6},{3,1},{4,0},{5,7},{6,2},{7,5},{8,12},{9,11},{10,... | collective-permute-start | bytes 221192 | tf_op jit(solution)/shard_map/ppermute | solution.py:356
  12.9 1.7 %collective-permute-start.6 = (bf16[528,256]{1,0:T(8,128)(2,1)S(1)}, bf16[528,256]{1,0:T(8,128)(2,1)S(1)}, u32[]{:S(2)}, u32[]{:S(2)}) collective-permute-start(bf16[528,256]{1,0:T(8,128)(2,1)S(1)} %shard_map.90.own), channel_id=1, source_target_pairs={{0,1},{1,0},{2,3},{3,2},{4,5},{5,4},{6,7},{7,6},{8,9},{9,8},{10,11... | collective-permute-start | bytes 811016 | tf_op jit(solution)/shard_map/ppermute | solution.py:356
  13.0 5.8 %collective-permute-start.4 = (bf16[400,256]{1,0:T(8,128)(2,1)S(1)}, bf16[400,256]{1,0:T(8,128)(2,1)S(1)}, u32[]{:S(2)}, u32[]{:S(2)}) collective-permute-start(bf16[400,256]{1,0:T(8,128)(2,1)S(1)} %shard_map.87), channel_id=1, source_target_pairs={{0,4},{1,3},{2,6},{3,1},{4,0},{5,7},{6,2},{7,5},{8,12},{9,11},{10,... | collective-permute-start | bytes 614408 | tf_op jit(solution)/shard_map/ppermute | solution.py:356
  16.4 6.5 %collective-permute-start.7 = (bf16[528,256]{1,0:T(8,128)(2,1)S(1)}, bf16[528,256]{1,0:T(8,128)(2,1)S(1)}, u32[]{:S(2)}, u32[]{:S(2)}) collective-permute-start(bf16[528,256]{1,0:T(8,128)(2,1)S(1)} %shard_map.90.own), channel_id=1, source_target_pairs={{0,2},{1,5},{2,0},{3,7},{4,6},{5,1},{6,4},{7,3},{8,10},{9,13},{10,... | collective-permute-start | bytes 811016 | tf_op jit(solution)/shard_map/ppermute | solution.py:356
  18.8 4.1 %collective-permute-start.8 = (bf16[528,256]{1,0:T(8,128)(2,1)S(1)}, bf16[528,256]{1,0:T(8,128)(2,1)S(1)}, u32[]{:S(2)}, u32[]{:S(2)}) collective-permute-start(bf16[528,256]{1,0:T(8,128)(2,1)S(1)} %shard_map.88.one), channel_id=1, source_target_pairs={{0,1},{1,0},{2,3},{3,2},{4,5},{5,4},{6,7},{7,6},{8,9},{9,8},{10,11... | collective-permute-start | bytes 811016 | tf_op jit(solution)/shard_map/ppermute | solution.py:356
  18.9 6.9 %collective-permute-start.5 = (bf16[528,256]{1,0:T(8,128)(2,1)S(1)}, bf16[528,256]{1,0:T(8,128)(2,1)S(1)}, u32[]{:S(2)}, u32[]{:S(2)}) collective-permute-start(bf16[528,256]{1,0:T(8,128)(2,1)S(1)} %shard_map.88.one), channel_id=1, source_target_pairs={{0,2},{1,5},{2,0},{3,7},{4,6},{5,1},{6,4},{7,3},{8,10},{9,13},{10,... | collective-permute-start | bytes 811016 | tf_op jit(solution)/shard_map/ppermute | solution.py:356
  22.9 2.9 %collective-permute-start.10 = (bf16[528,256]{1,0:T(8,128)(2,1)S(1)}, bf16[528,256]{1,0:T(8,128)(2,1)S(1)}, u32[]{:S(2)}, u32[]{:S(2)}) collective-permute-start(bf16[528,256]{1,0:T(8,128)(2,1)S(1)} %collective-permute-done.7.two), channel_id=1, source_target_pairs={{0,1},{1,0},{2,3},{3,2},{4,5},{5,4},{6,7},{7,6},{8,9},{9,8},{10,11... | collective-permute-start | bytes 811016 | tf_op jit(solution)/shard_map/ppermute | solution.py:356
  25.8 1.5 %collective-permute-start.9 = (bf16[528,256]{1,0:T(8,128)(2,1)S(1)}, bf16[528,256]{1,0:T(8,128)(2,1)S(1)}, u32[]{:S(2)}, u32[]{:S(2)}) collective-permute-start(bf16[528,256]{1,0:T(8,128)(2,1)S(1)} %collective-permute-done.5.diag), channel_id=1, source_target_pairs={{0,1},{1,0},{2,3},{3,2},{4,5},{5,4},{6,7},{7,6},{8,9},{9,8},{10,11... | collective-permute-start | bytes 811016 | tf_op jit(solution)/shard_map/ppermute | solution.py:356
